TPU v7x, 128 devices: a whole 4x4x4 slice. The times are simulated.
128 devices in a mesh: index: 32 (over z, y, core), rep: 4 (over x).
Axes of the slice: x: 4, y: 4, z: 4, core: 2. Of those that a mesh axis runs over, the one named last changes fastest.
Arguments:
- queries: bfloat16 [1536, 32, 128], P('index'), may hold values from -32 to 32
- listed: int32 [1536, 8], P('index'), may hold values from 0 to 2047, as said below
- page_slot: int32 [2048], replicated, may hold values from 0 to 2047, as said below
- counts: int32 [2048], P('index'), may hold values from 768 to 1024
- page_store: bfloat16 [2048, 1024, 128], P('index', 'rep'), may hold values from -18 to 18
Outputs:
- losses: float32 [1536], P('index')
- query_grads: bfloat16 [1536, 32, 128], P('index')
Inputs may be any that keep to these rules, and one draw needn't show every extreme that they name: Page ids; the 8 pages of a query are different. Storage row r lies on index r // 64. Over the 48 queries of one index, at most 24 listed pages lie on any one index, and in every draw one index is named exactly 24 times by the queries of every index. The k-th page of a query lies at row (o + k) mod 64 of its index, for one offset o per query. `page_slot`: A permutation of the page ids.
All inputs are finite; a program needn't handle non-finite values.
Results may differ from a plain program's by a relative error of at most 0.01785.
Values may be sent and summed in bfloat16 or wider, within the bound.
No kernel may reach another device: no remote copies, remote signals or barrier semaphores. Data moves between devices by JAX's collectives and lax.ppermute only.
A program may use at most 128 MiB of HBM per device.

v0:
```python
import math

import jax
import jax.numpy as jnp
from jax import lax
from jax.sharding import PartitionSpec as P

TAU = 0.1
LOSS_SCALE = 32.0
NEG = -1e30


def combined_all(value, axis, combine):
    everything = jax.tree.map(lambda part: lax.all_gather(part, axis), value)
    initial = jax.tree.map(lambda part: part[0], everything)

    def hop(k, so_far):
        return combine(so_far, jax.tree.map(lambda part: part[k], everything))

    return lax.fori_loop(1, lax.axis_size(axis), hop, initial)


def part_stats(block_tokens, block_pages, page_store, counts, rep_pos, sim_scale):
    picked = page_store[block_pages]
    limits = counts[block_pages]
    part_len = page_store.shape[1]
    position = rep_pos * part_len + jnp.arange(part_len, dtype=jnp.int32)
    usable = (position[None, :] < limits[:, None])[:, None, :]
    logits = (
        jnp.einsum("btw,bpw->btp", block_tokens, picked, preferred_element_type=jnp.float32)
        * sim_scale
    )
    logits = jnp.where(usable, logits, NEG)
    peaks = jnp.max(logits, axis=2)
    weights = jnp.where(usable, jnp.exp(logits - peaks[:, :, None]), 0.0)
    totals = jnp.sum(weights, axis=2)
    vectors = jnp.einsum(
        "btp,bpw->btw", weights.astype(jnp.bfloat16), picked, preferred_element_type=jnp.float32
    )
    return (peaks, totals, vectors)


def combine(first, second):
    peak_a, total_a = first
    peak_b, total_b = second
    larger = jnp.maximum(peak_a, peak_b)
    return (larger, total_a * jnp.exp(peak_a - larger) + total_b * jnp.exp(peak_b - larger))


def per_device(queries, listed, page_slot, counts, page_store):
    groups = lax.axis_size("index")
    rep_pos = lax.axis_index("rep")
    query_count, query_len, feature = queries.shape
    list_len = listed.shape[1]
    page_count = page_store.shape[0]
    pair_count = query_count * list_len
    capacity = 2 * pair_count // groups
    stored = page_slot[listed.reshape(pair_count)]
    owners = stored // page_count
    local_page = stored % page_count
    onehot = (owners[:, None] == jnp.arange(groups, dtype=jnp.int32)[None, :]).astype(jnp.int32)
    before = jnp.cumsum(onehot, axis=0) - onehot
    slot_rank = jnp.sum(before * onehot, axis=1)
    slot_place = owners * capacity + slot_rank
    slot_query = (
        jnp.full((groups * capacity,), query_count, jnp.int32)
        .at[slot_place]
        .set(jnp.arange(pair_count, dtype=jnp.int32) // list_len)
    )
    slot_page = jnp.zeros((groups * capacity,), jnp.int32).at[slot_place].set(local_page)
    padded = jnp.concatenate([queries, jnp.zeros((1, query_len, feature), queries.dtype)], axis=0)
    outgoing = padded[slot_query].reshape(groups, capacity, query_len, feature)
    out_pages = slot_page.reshape(groups, capacity)
    arrived = lax.all_to_all(outgoing, "index", split_axis=0, concat_axis=0, tiled=True)
    arrived_pages = lax.all_to_all(out_pages, "index", split_axis=0, concat_axis=0, tiled=True)
    block_slots = 16
    step_count = groups * capacity // block_slots
    sim_scale = 1.0 / (math.sqrt(feature) * TAU)

    def slot_block(inputs):
        return part_stats(inputs[0], inputs[1], page_store, counts, rep_pos, sim_scale)

    peaks, totals, vectors = lax.map(
        slot_block,
        (
            arrived.reshape(step_count, block_slots, query_len, feature),
            arrived_pages.reshape(step_count, block_slots),
        ),
    )
    peaks = peaks.reshape(groups, capacity, query_len)
    totals = totals.reshape(groups, capacity, query_len)
    vectors = vectors.reshape(groups, capacity, query_len, feature)
    largest, denominator = combined_all((peaks, totals), "rep", combine)
    shares = jnp.exp(peaks - largest)
    terms = vectors * shares[..., None]
    scores = jnp.sum(TAU * (largest + jnp.log(denominator)), axis=2)
    back_scores = lax.all_to_all(scores, "index", split_axis=0, concat_axis=0, tiled=True)
    summed = lax.psum(terms.astype(jnp.bfloat16), "rep").astype(jnp.float32)
    directions = (summed / (denominator[..., None] * math.sqrt(feature))).astype(jnp.bfloat16)
    back_dirs = lax.all_to_all(directions, "index", split_axis=0, concat_axis=0, tiled=True)
    pair_scores = back_scores.reshape(groups * capacity)[slot_place].reshape(query_count, list_len)
    pair_dirs = back_dirs.reshape(groups * capacity, query_len, feature)[slot_place].reshape(
        query_count, list_len, query_len, feature
    )
    highest = jnp.max(pair_scores, axis=1, keepdims=True)
    log_total = highest[:, 0] + jnp.log(jnp.sum(jnp.exp(pair_scores - highest), axis=1))
    losses = log_total - pair_scores[:, 0]
    probability = jnp.exp(pair_scores - log_total[:, None])
    target = (jnp.arange(list_len) == 0).astype(jnp.float32)
    coefficient = LOSS_SCALE * (probability - target[None, :])
    gradients = jnp.sum(
        coefficient[:, :, None, None] * pair_dirs.astype(jnp.float32), axis=1
    ).astype(jnp.bfloat16)
    return (losses, gradients)


def solution(mesh):
    return jax.shard_map(
        per_device,
        mesh=mesh,
        in_specs=(
            P("index", None, None),
            P("index", None),
            P(),
            P("index"),
            P("index", "rep", None),
        ),
        out_specs=(P("index"), P("index", None, None)),
        check_vma=False,
    )
```

profile of v0, /device:TPU:0, one launch (start us, length us, event | category | flops | bytes accessed | tf_op | source)
XLA Modules:
  0.0 712.1 jit_solution(13746176413089887323)
XLA Ops:
  12.0 2.9 scatter_custom_fusion
  15.6 8.4 %all-to-all-start = ((s32[32,1,24]{2,1,0:T(1,128)}), s32[32,1,24]{2,1,0:T(1,128)S(1)}, u32[]{:S(2)}, u32[]{:S(2)}) async-start(s32[32,1,24]{2,1,0:T(1,128)} %bitcast.10), calls=%async_computation | async-start | bytes 32768 | tf_op jit(solution)/shard_map/all_to_all | solution.py:75
  28.0 4.4 gather_fusion.3
  32.4 7.6 %all-to-all-start.1 = ((bf16[32,24,32,128]{3,2,1,0:T(8,128)(2,1)}), bf16[32,24,32,128]{3,2,1,0:T(8,128)(2,1)}, u32[]{:S(2)}, u32[]{:S(2)}) async-start(bf16[32,24,32,128]{3,2,1,0:T(8,128)(2,1)} %bitcast.102), calls=%async_computation.1 | async-start | bytes 12582912 | tf_op jit(solution)/shard_map/all_to_all | solution.py:74
  41.3 76.6 %all-to-all-done.1 = bf16[32,24,32,128]{3,2,1,0:T(8,128)(2,1)} async-done(((bf16[32,24,32,128]{3,2,1,0:T(8,128)(2,1)}), bf16[32,24,32,128]{3,2,1,0:T(8,128)(2,1)}, u32[]{:S(2)}, u32[]{:S(2)}) %all-to-all-start.1) | async-done | bytes 6291488 | tf_op jit(solution)/shard_map/all_to_all | solution.py:74
  117.9 314.1 %while.33 = (s32[]{:T(128)}, f32[48,16,32]{2,1,0:T(8,128)S(1)}, f32[48,16,32]{2,1,0:T(8,128)S(1)}, f32[48,16,32,128]{3,2,1,0:T(8,128)}, s32[]{:T(128)}, /*index=...) while((s32[]{:T(128)}, f32[48,16,32]{2,1,0:T(8,128)S(1)}, ...), condition=%wide.region_8.9_spmd, body=%wide.region_5.8_spmd.sunk | while | flops 68292912 | bytes 6225521 | solution.py:83
  118.7 2.9 gather_fusion
  125.2 2.9 gather_fusion
  131.8 2.9 gather_fusion
  138.3 2.9 gather_fusion
  144.8 2.9 gather_fusion
  151.4 2.9 gather_fusion
  158.0 2.9 gather_fusion
  164.5 2.9 gather_fusion
  171.0 2.9 gather_fusion
  177.6 2.9 gather_fusion
  184.1 2.9 gather_fusion
  190.7 2.9 gather_fusion
  197.2 2.9 gather_fusion
  203.8 2.9 gather_fusion
  210.3 2.9 gather_fusion
  216.9 2.9 gather_fusion
  223.4 2.9 gather_fusion
  229.9 2.9 gather_fusion
  236.5 2.9 gather_fusion
  243.0 2.9 gather_fusion
  249.6 2.9 gather_fusion
  256.1 2.9 gather_fusion
  262.7 2.9 gather_fusion
  269.2 2.9 gather_fusion
  275.8 2.9 gather_fusion
  282.3 2.9 gather_fusion
  288.9 2.9 gather_fusion
  295.4 2.9 gather_fusion
  302.0 2.9 gather_fusion
  308.5 2.9 gather_fusion
  315.0 2.9 gather_fusion
  321.6 2.9 gather_fusion
  328.1 2.9 gather_fusion
  334.6 2.9 gather_fusion
  341.2 2.9 gather_fusion
  347.8 2.9 gather_fusion
  354.3 2.9 gather_fusion
  360.9 2.9 gather_fusion
  367.4 2.9 gather_fusion
  374.0 2.9 gather_fusion
  380.5 2.9 gather_fusion
  387.1 2.9 gather_fusion
  393.6 2.9 gather_fusion
  400.2 2.9 gather_fusion
  406.7 2.9 gather_fusion
  413.2 2.9 gather_fusion
  419.8 2.9 gather_fusion
  426.3 2.9 gather_fusion
  432.1 18.4 %all_gather.6 = f32[4,32,24,32]{3,2,1,0:T(8,128)S(1)} all-gather(f32[1,32,24,32]{3,2,1,0:T(8,128)S(1)} %bitcast.105), channel_id=1, replica_groups=mesh['index'=32,'rep'=4] {'rep'}, dimensions={0}, use_global_device_ids=true | all-gather | bytes 491520 | tf_op jit(solution)/shard_map/all_gather | solution.py:14
  450.5 15.4 %all_gather.7 = f32[4,32,24,32]{3,2,1,0:T(8,128)S(1)} all-gather(f32[1,32,24,32]{3,2,1,0:T(8,128)S(1)} %bitcast.107), channel_id=1, replica_groups=mesh['index'=32,'rep'=4] {'rep'}, dimensions={0}, use_global_device_ids=true | all-gather | bytes 491520 | tf_op jit(solution)/shard_map/all_gather | solution.py:14
  467.1 4.1 while.34
  472.0 9.0 %multiply_convert_fusion = bf16[32,24,32,128]{3,2,1,0:T(8,128)(2,1)} fusion(f32[32,24,32,128]{3,2,1,0:T(8,128)} %bitcast.103, f32[32,24,32]{2,1,0:T(8,128)S(1)} %get-tuple-element.285), kind=kLoop, calls=%fused_computation.37 | loop fusion | flops 6291456 | bytes 18972672 | tf_op jit(solution)/shard_map/convert_element_type | solution.py:98
  481.0 5.2 all-to-all-start.2
  486.2 119.5 %all-reduce.3.cloned.1.call-done = bf16[32,24,32,128]{3,2,1,0:T(8,128)(2,1)} async-done(((bf16[32,24,32,128]{3,2,1,0:T(8,128)(2,1)}), bf16[32,24,32,128]{3,2,1,0:T(8,128)(2,1)}) %all-reduce.3.cloned.1.call-update) | async-done | bytes 6291472 | tf_op jit(solution)/shard_map/psum | solution.py:98
  605.7 8.2 %divide_convert_fusion = bf16[32,24,32,128]{3,2,1,0:T(8,128)(2,1)} fusion(bf16[32,24,32,128]{3,2,1,0:T(8,128)(2,1)} %all-reduce.3.cloned.1.call-done, f32[32,24,32]{2,1,0:T(8,128)S(1)} %get-tuple-element.283), kind=kLoop, calls=%fused_computation.36 | loop fusion | flops 9437184 | bytes 12681216 | tf_op jit(solution)/shard_map/convert_element_type | solution.py:99
  613.9 7.4 %all-to-all-start.3 = ((bf16[32,24,32,128]{3,2,1,0:T(8,128)(2,1)}), bf16[32,24,32,128]{3,2,1,0:T(8,128)(2,1)}, u32[]{:S(2)}, u32[]{:S(2)}) async-start(bf16[32,24,32,128]{3,2,1,0:T(8,128)(2,1)} %divide_convert_fusion), calls=%async_computation.3 | async-start | bytes 12582912 | tf_op jit(solution)/shard_map/all_to_all | solution.py:100
  625.6 73.5 %all-to-all-done.3 = bf16[32,24,32,128]{3,2,1,0:T(8,128)(2,1)} async-done(((bf16[32,24,32,128]{3,2,1,0:T(8,128)(2,1)}), bf16[32,24,32,128]{3,2,1,0:T(8,128)(2,1)}, u32[]{:S(2)}, u32[]{:S(2)}) %all-to-all-start.3) | async-done | bytes 6291488 | tf_op jit(solution)/shard_map/all_to_all | solution.py:100
  699.2 4.0 gather_fusion.5
  (486 shorter events, 193.3 us)
Async XLA Ops:
  7.2 0.9 copy-start
  15.6 16.8 %all-to-all-start = ((s32[32,1,24]{2,1,0:T(1,128)}), s32[32,1,24]{2,1,0:T(1,128)S(1)}, u32[]{:S(2)}, u32[]{:S(2)}) async-start(s32[32,1,24]{2,1,0:T(1,128)} %bitcast.10), calls=%async_computation | async-start | bytes 32768 | tf_op jit(solution)/shard_map/all_to_all | solution.py:75
  32.4 85.5 %copy-start.1 = (s32[64]{0:T(128)S(1)}, s32[64]{0:T(128)}, u32[]{:S(2)}) copy-start(s32[64]{0:T(128)} %param.12) | copy-start | bytes 772
  32.4 85.5 %all-to-all-start.1 = ((bf16[32,24,32,128]{3,2,1,0:T(8,128)(2,1)}), bf16[32,24,32,128]{3,2,1,0:T(8,128)(2,1)}, u32[]{:S(2)}, u32[]{:S(2)}) async-start(bf16[32,24,32,128]{3,2,1,0:T(8,128)(2,1)} %bitcast.102), calls=%async_computation.1 | async-start | bytes 12582912 | tf_op jit(solution)/shard_map/all_to_all | solution.py:74
  40.0 565.7 %all-reduce.3.cloned.1.call-start = ((), (), s32[]{:S(2)}) async-start(), calls=%async_computation.4 | async-start | bytes 12582912 | tf_op jit(solution)/shard_map/psum | solution.py:98
  465.9 1.2 copy-start.2
  481.0 132.9 %all-to-all-start.2 = ((f32[32,1,24]{2,1,0:T(1,128)}), f32[32,1,24]{2,1,0:T(1,128)S(1)}, u32[]{:S(2)}, u32[]{:S(2)}) async-start(f32[32,1,24]{2,1,0:T(1,128)} %bitcast.17), calls=%async_computation.2 | async-start | bytes 32768 | tf_op jit(solution)/shard_map/all_to_all | solution.py:97
  613.9 85.3 %all-to-all-start.3 = ((bf16[32,24,32,128]{3,2,1,0:T(8,128)(2,1)}), bf16[32,24,32,128]{3,2,1,0:T(8,128)(2,1)}, u32[]{:S(2)}, u32[]{:S(2)}) async-start(bf16[32,24,32,128]{3,2,1,0:T(8,128)(2,1)} %divide_convert_fusion), calls=%async_computation.3 | async-start | bytes 12582912 | tf_op jit(solution)/shard_map/all_to_all | solution.py:100
Sparse Core Ops, SparseCore 0:
  481.2 124.5 all-reduce.2
where the time goes:
time: 716 us; the launch traced here: 712 us
  waiting for transfers between devices  270 us (38%)
  local copies, waits for them, and re-layouts  197 us (28%)
  matrix products  121 us (17%)
  other arithmetic  45.1 us (6%)
  blocking collectives  33.8 us (5%)
  starting transfers between devices  28.6 us (4%)
  between operations  14.3 us (2%)
    gather x48, local copies, waits for them, and re-layouts, part_stats(): picked = page_store[block_pages]  141 us
    psum x1, waiting for transfers between devices, per_device(): summed = lax.psum(terms.astype(jnp.bfloat16), 'rep').astype(jnp.float32)  120 us
    all_to_all x1, waiting for transfers between devices, per_device(): lax.all_to_all(outgoing, 'index', split_axis=0, concat_axis=0, tiled=True)  76.6 us
    all_to_all x1, waiting for transfers between devices, per_device(): lax.all_to_all(directions, 'index', split_axis=0, concat_axis=0, tiled=True)  73.5 us
    dot_general x48, matrix products, part_stats(): jnp.einsum('btw,bpw->btp', block_tokens, picked, preferred_element_type=j...  69.7 us
    dot_general x48, matrix products, part_stats(): jnp.einsum('btp,bpw->btw', weights.astype(jnp.bfloat16), picked, preferre...  51 us
    all_gather x2, blocking collectives, combined_all(): everything = jax.tree.map(lambda part: lax.all_gather(part, axis), value)  33.8 us
    gather x48, local copies, waits for them, and re-layouts, part_stats(): limits = counts[block_pages]  31.6 us
  transfers between devices with their start and end apart: 5, of which 3 were waited for; matrix products, arithmetic and copies ran while one was open for 3% of the time, Pallas kernels for 0%

commit v1 on v0

v1 whole, which is shorter than its diff:
```python
import functools
import math

import jax
import jax.numpy as jnp
from jax import lax
from jax.experimental import pallas as pl
from jax.experimental.pallas import tpu as pltpu
from jax.sharding import PartitionSpec as P

TAU = 0.1
LOSS_SCALE = 32.0
NEG = -1e30
BLOCK = 4
UNROLL = 4
RING = 4
F32 = jnp.float32
BF16 = jnp.bfloat16

SMEM = pl.BlockSpec(memory_space=pltpu.SMEM)
VMEM = pl.BlockSpec(memory_space=pltpu.VMEM)
ANY = pl.BlockSpec(memory_space=pl.ANY)


def params(mib):
    return pltpu.CompilerParams(vmem_limit_bytes=mib * 1024 * 1024)


def place_of(z, y, core):
    return ((z % RING) * RING + (y % RING)) * 2 + core


def ring_pairs(second, step):
    pairs = []
    for z in range(RING):
        for y in range(RING):
            for core in range(2):
                if (core == 0) != second:
                    there = place_of(z, y + step, core)
                else:
                    there = place_of(z + step, y, core)
                pairs.append((place_of(z, y, core), there))
    return pairs


CORE_PAIRS = [(i, i ^ 1) for i in range(2 * RING * RING)]


def across(x):
    return lax.ppermute(x, "index", CORE_PAIRS)


def gather_queries(queries, core):
    half = queries.shape[0] // 2
    keep = lax.dynamic_slice_in_dim(queries, core * half, half, 0)
    give = lax.dynamic_slice_in_dim(queries, (1 - core) * half, half, 0)
    got = across(give)
    own = jnp.where(core == 0, jnp.stack([keep, got]), jnp.stack([got, keep]))

    def spread(x, second):
        n = x.shape[0] // 2
        right = lax.ppermute(x, "index", ring_pairs(second, 1))
        left = lax.ppermute(x, "index", ring_pairs(second, -1))
        far_a = lax.ppermute(right[:n], "index", ring_pairs(second, 1))
        far_b = lax.ppermute(left[n:], "index", ring_pairs(second, -1))
        return right, left, far_a, far_b

    right, left, far_a, far_b = spread(own, False)
    own_spread = spread(own, True)
    rest = jnp.concatenate([right, left, far_a, far_b], axis=0)
    rest_spread = spread(rest, True)
    pieces = []
    for p, x in enumerate((own, own_spread[0], own_spread[1])):
        pieces.append((x, 8 * p))
    pieces.append((own_spread[2], 24))
    pieces.append((own_spread[3], 25))
    for p, x in enumerate((rest, rest_spread[0], rest_spread[1])):
        pieces.append((x, 8 * p + 2))
    pieces.append((rest_spread[2], 26))
    pieces.append((rest_spread[3], 29))
    swapped = [(across(x), 32 + at) for x, at in pieces]
    return pieces + swapped


def route_kernel(capacity, pages, list_len, listed, page_slot, table, place, used):
    slots = table.shape[0]
    pairs = listed.shape[0]

    def clear(i, _):
        for k in range(8):
            table[i * 8 + k] = -1
        return 0

    lax.fori_loop(0, slots // 8, clear, 0)

    def clear_used(i, _):
        used[i] = 0
        return 0

    lax.fori_loop(0, used.shape[0], clear_used, 0)

    def step(q, _):
        for k in range(list_len):
            i = q * list_len + k
            row = page_slot[listed[i]]
            owner = row // pages
            n = used[owner]
            used[owner] = n + 1
            j = owner * capacity + jnp.minimum(n, capacity - 1)
            table[j] = q * pages + (row - owner * pages)
            place[i] = j
        return 0

    lax.fori_loop(0, pairs // list_len, step, 0)


def sort_kernel(
    capacity, pages, half, blocks, arrived, me, order, slot_pad, slot_at, block_page, block_at, block_count, count, start, first
):
    slots = arrived.shape[0]
    groups = slots // capacity
    z = me[0] // (2 * RING)
    y = (me[0] // 2) % RING
    core = me[0] % 2

    def clear(i, _):
        for k in range(8):
            order[i * 8 + k] = 0
            slot_pad[i * 8 + k] = -1
        return 0

    lax.fori_loop(0, blocks * BLOCK // 8, clear, 0)

    def clear_blocks(i, _):
        block_page[i] = 0
        block_at[i] = slots
        return 0

    lax.fori_loop(0, blocks, clear_blocks, 0)

    def clear_count(i, _):
        count[i] = 0
        return 0

    lax.fori_loop(0, pages + 1, clear_count, 0)

    def bucket(code):
        return jnp.where(code < 0, pages, code % pages)

    def tally(i, _):
        for k in range(8):
            p = bucket(arrived[i * 8 + k])
            count[p] = count[p] + 1
        return 0

    lax.fori_loop(0, slots // 8, tally, 0)

    def lay(p, carry):
        at, b = carry
        n = count[p]
        start[p] = at
        first[p] = b * BLOCK
        count[p] = 0
        steps = (n + BLOCK - 1) // BLOCK

        def one(k, _):
            block_page[b + k] = p
            block_at[b + k] = at + k * BLOCK
            return 0

        lax.fori_loop(0, steps, one, 0)
        return at + n, b + steps

    at, total = lax.fori_loop(0, pages, lay, (jnp.int32(0), jnp.int32(0)))
    block_count[0] = total
    start[pages] = at
    first[pages] = blocks * BLOCK
    count[pages] = 0

    def rank(there, mine):
        apart = (there - mine + RING) % RING
        return jnp.where(apart == 0, 0, jnp.where(apart == RING - 1, 1, jnp.where(apart == 1, 2, 3)))

    def source(s, _):
        dz = rank(s // (2 * RING), z)
        dy = rank((s // 2) % RING, y)
        sc = s % 2
        low = ((jnp.where(core == 0, 0, RING) + dz) * RING + dy) * 2 + sc
        high = ((jnp.where(core == 1, 0, RING) + dy) * RING + dz) * 2 + sc
        low_base = low * half
        high_base = high * half - half

        def inner(j, _):
            i = s * capacity + j
            code = arrived[i]
            p = bucket(code)
            q = jnp.maximum(code, 0) // pages
            r = count[p]
            count[p] = r + 1
            e = first[p] + r
            order[e] = q + jnp.where(q < half, low_base, high_base)
            slot_pad[e] = i
            slot_at[start[p] + r] = i
            return 0

        lax.fori_loop(0, capacity, inner, 0)
        return 0

    lax.fori_loop(0, groups, source, 0)


def pair_kernel(places, scale, order, block_page, block_at, block_count, limits, *refs):
    n_pieces = len(places)
    store = refs[0]
    pieces = refs[1 : 1 + n_pieces]
    vectors, peaks, totals, held, pages, sems = refs[1 + n_pieces :]
    copies = [pltpu.make_async_copy(store, pages, sems.at[n_pieces])]
    for k, (ref, at) in enumerate(zip(pieces, places, strict=True)):
        copies.append(pltpu.make_async_copy(ref, held.at[pl.ds(at, ref.shape[0])], sems.at[k]))
    for c in copies:
        c.start()
    for c in copies:
        c.wait()
    part = pages.shape[1]
    rows = BLOCK * held.shape[1]
    feature = held.shape[2]
    power = scale * math.log2(math.e)
    lane = lax.broadcasted_iota(jnp.int32, (1, part), 1)
    eye = lax.broadcasted_iota(jnp.int32, (rows, rows), 0) == lax.broadcasted_iota(jnp.int32, (rows, rows), 1)

    def as_row(column):
        return jnp.sum(jnp.where(eye, column, 0.0), axis=0, keepdims=True)

    def step(it, _):
        for u in range(UNROLL):
            b = it * UNROLL + u
            p = block_page[b]
            tokens = jnp.concatenate([held[order[b * BLOCK + i]] for i in range(BLOCK)], axis=0)
            page = pages[p]
            raw = lax.dot_general(tokens, page, (((1,), (1,)), ((), ())), preferred_element_type=F32)
            raw = jnp.where(lane < limits[p], raw, NEG)
            top = jnp.max(raw, axis=1, keepdims=True)
            weights = jnp.exp2((raw - top) * power)
            total = jnp.sum(weights, axis=1, keepdims=True)
            out = jnp.dot(weights.astype(BF16), page, preferred_element_type=F32)
            vectors[pl.ds(block_at[b], BLOCK)] = out.astype(BF16).reshape(BLOCK, rows // BLOCK, feature)
            peaks[pl.ds(b, 1), :] = as_row(jnp.maximum(top * scale, NEG))
            totals[pl.ds(b, 1), :] = as_row(total)
        return 0

    lax.fori_loop(0, (block_count[0] + UNROLL - 1) // UNROLL, step, 0)


def scale_kernel(root, block_at, block_count, me, slot_cols, *refs):
    stats = refs[:8]
    vectors = refs[8]
    outs = refs[9:17]
    scores = refs[17]
    factors, logs, wide = refs[18:]
    peaks, totals = stats[:4], stats[4:]
    blocks, rows = factors.shape
    tokens = rows // BLOCK
    feature = vectors.shape[2]
    largest = functools.reduce(jnp.maximum, [p[...] for p in peaks])
    shares = [jnp.exp(p[...] - largest) for p in peaks]
    denominator = sum(t[...] * s for t, s in zip(totals, shares, strict=True))
    factors[...] = shares[0] / (denominator * root)
    logs[...] = TAU * (largest + jnp.log(denominator))

    lanes = lax.broadcasted_iota(jnp.int32, (8, 128), 1)
    n_rows = scores.shape[0]

    def score(v, acc):
        at = pl.multiple_of(v * 8, 8)
        block = logs[pl.ds(at, 8), :]
        cols = slot_cols[pl.ds(at, 8), :]
        acc = list(acc)
        for i in range(BLOCK):
            value = jnp.sum(jnp.where(lanes // tokens == i, block, 0.0), axis=1, keepdims=True)
            slot = cols[:, i : i + 1]
            for k in range(n_rows):
                acc[k] = jnp.where(lanes + 128 * k == slot, value, acc[k])
        return tuple(acc)

    acc = lax.fori_loop(0, blocks // 8, score, tuple(jnp.zeros((8, 128), F32) for _ in range(n_rows)))
    scores[...] = jnp.concatenate([jnp.sum(a, axis=0, keepdims=True) for a in acc], axis=0)

    eye = lax.broadcasted_iota(jnp.int32, (rows, rows), 0) == lax.broadcasted_iota(jnp.int32, (rows, rows), 1)
    share = tokens // 4

    def step(it, _):
        for u in range(UNROLL):
            b = it * UNROLL + u
            row = factors[pl.ds(b, 1), :]
            column = jnp.sum(jnp.where(eye, row, 0.0), axis=1, keepdims=True)
            at = block_at[b]
            block = vectors[pl.ds(at, BLOCK)].astype(F32).reshape(rows, feature) * column
            for i in range(BLOCK):
                for t in range(4):
                    first = i * tokens + t * share
                    wide[t, pl.ds(pl.multiple_of((at + i) * share, share), share), :] = block[first : first + share]
        return 0

    lax.fori_loop(0, (block_count[0] + UNROLL - 1) // UNROLL, step, 0)

    rep = me[1]
    length = outs[0].shape[0]
    chunk = 128
    for p in range(4):
        t = (rep + p) % 4
        for h in range(2):

            def narrow(i, _):
                at = pl.multiple_of(i * chunk, chunk)
                outs[p * 2 + h][pl.ds(at, chunk), :] = wide[t, pl.ds(at + h * length, chunk), :].astype(BF16)
                return 0

            lax.fori_loop(0, length // chunk, narrow, 0)


def slot_kernel(share, slot_at, in_a, own_a, in_b, own_b, out, wide):
    chunk = 16
    for h, (x, own) in enumerate(((in_a, own_a), (in_b, own_b))):
        length = x.shape[0]
        per = chunk // share

        def move(i, _):
            for k in range(4):
                at = pl.multiple_of((i * 4 + k) * chunk, chunk)
                both = x[pl.ds(at, chunk), :].astype(F32) + own[pl.ds(at, chunk), :].astype(F32)
                for s in range(per):
                    slot = slot_at[h * (length // share) + (i * 4 + k) * per + s]
                    wide[pl.ds(pl.multiple_of(slot * share, share), share), :] = both[s * share : (s + 1) * share]
            return 0

        lax.fori_loop(0, length // chunk // 4, move, 0)

    def narrow(i, _):
        at = pl.multiple_of(i * 128, 128)
        out[pl.ds(at, 128), :] = wide[pl.ds(at, 128), :].astype(BF16)
        return 0

    lax.fori_loop(0, out.shape[0] // 128, narrow, 0)


def gradient_kernel(share, list_len, place, weight, directions, out, wide):
    def widen(i, _):
        at = pl.multiple_of(i * 128, 128)
        wide[pl.ds(at, 128), :] = directions[pl.ds(at, 128), :].astype(F32)
        return 0

    lax.fori_loop(0, directions.shape[0] // 128, widen, 0)

    def step(i, _):
        parts = []
        for s in range(2):
            total = jnp.zeros((share, out.shape[1]), F32)
            for k in range(list_len):
                e = (i * 2 + s) * list_len + k
                at = pl.multiple_of(place[e] * share, share)
                total = total + weight[e] * wide[pl.ds(at, share), :]
            parts.append(total)
        out[pl.ds(pl.multiple_of(i * 2 * share, 2 * share), 2 * share), :] = jnp.concatenate(parts, axis=0).astype(BF16)
        return 0

    lax.fori_loop(0, out.shape[0] // share // 2, step, 0)


def ints(*shape):
    return jax.ShapeDtypeStruct(shape, jnp.int32)


def per_device(queries, listed, page_slot, counts, page_store):
    groups = lax.axis_size("index")
    index = lax.axis_index("index").astype(jnp.int32)
    rep = lax.axis_index("rep").astype(jnp.int32)
    reps = lax.axis_size("rep")
    query_count, query_len, feature = queries.shape
    list_len = listed.shape[1]
    pages, part, _ = page_store.shape
    pairs = query_count * list_len
    capacity = 2 * pairs // groups
    slots = groups * capacity
    half = query_count // 2
    share = query_len // reps
    blocks = (slots + (BLOCK - 1) * pages) // BLOCK
    blocks = (blocks + 7) // 8 * 8
    rows = BLOCK * query_len
    me = jnp.stack([index, rep])

    table, place = pl.pallas_call(
        functools.partial(route_kernel, capacity, pages, list_len),
        out_shape=(ints(slots), ints(pairs)),
        in_specs=[SMEM, SMEM],
        out_specs=(SMEM, SMEM),
        scratch_shapes=[pltpu.SMEM((groups,), jnp.int32)],
        name="route",
    )(listed.reshape(pairs), page_slot)
    arrived = lax.all_to_all(table.reshape(groups, capacity), "index", split_axis=0, concat_axis=0, tiled=True)

    pieces = gather_queries(queries, index % 2)

    order, slot_pad, slot_at, block_page, block_at, block_count = pl.pallas_call(
        functools.partial(sort_kernel, capacity, pages, half, blocks),
        out_shape=(ints(blocks * BLOCK + slots), ints(blocks * BLOCK + slots), ints(slots), ints(blocks), ints(blocks), ints(1)),
        in_specs=[SMEM, SMEM],
        out_specs=(SMEM,) * 6,
        scratch_shapes=[pltpu.SMEM((pages + 1,), jnp.int32)] * 3,
        name="sort_pairs",
    )(arrived.reshape(slots), me)

    limits = counts - rep * part
    flat = [x.reshape((-1,) + x.shape[-2:]) for x, _ in pieces]
    places = [at * half for _, at in pieces]
    scale = 1.0 / (math.sqrt(feature) * TAU)
    vectors, peaks, totals = pl.pallas_call(
        functools.partial(pair_kernel, places, scale),
        out_shape=(
            jax.ShapeDtypeStruct((slots + 2 * BLOCK, query_len, feature), BF16),
            jax.ShapeDtypeStruct((blocks, rows), F32),
            jax.ShapeDtypeStruct((blocks, rows), F32),
        ),
        in_specs=[SMEM] * 5 + [ANY] * (1 + len(flat)),
        out_specs=(VMEM, VMEM, VMEM),
        scratch_shapes=[
            pltpu.VMEM((groups * query_count, query_len, feature), BF16),
            pltpu.VMEM((pages, part, feature), BF16),
            pltpu.SemaphoreType.DMA((len(flat) + 1,)),
        ],
        compiler_params=params(48),
        name="pairs",
    )(order, block_page, block_at, block_count, limits, page_store, *flat)

    def rep_pairs(step):
        return [(i, (i + step) % reps) for i in range(reps)]

    stats = jnp.stack([peaks, totals])
    everyone = [stats] + [lax.ppermute(stats, "rep", rep_pairs(s)) for s in (1, -1, 2)]
    length = slots // 2 * share
    results = pl.pallas_call(
        functools.partial(scale_kernel, math.sqrt(feature)),
        out_shape=(jax.ShapeDtypeStruct((length, feature), BF16),) * 8 + (jax.ShapeDtypeStruct((slots // 128, 128), F32),),
        in_specs=[SMEM] * 3 + [VMEM] * 10,
        out_specs=(VMEM,) * 9,
        scratch_shapes=[
            pltpu.VMEM((blocks, rows), F32),
            pltpu.VMEM((blocks, rows), F32),
            pltpu.VMEM((4, (slots + 2 * BLOCK) * share, feature), F32),
        ],
        compiler_params=params(48),
        name="scale",
    )(
        block_at,
        block_count,
        me,
        slot_pad[: blocks * BLOCK].reshape(blocks, BLOCK),
        *[s[0] for s in everyone],
        *[s[1] for s in everyone],
        vectors,
    )
    scores = results[8]
    back = lax.all_to_all(scores.reshape(groups, capacity), "index", split_axis=0, concat_axis=0, tiled=True)
    pair_scores = back.reshape(slots)[place].reshape(query_count, list_len)
    highest = jnp.max(pair_scores, axis=1, keepdims=True)
    log_total = highest[:, 0] + jnp.log(jnp.sum(jnp.exp(pair_scores - highest), axis=1))
    losses = log_total - pair_scores[:, 0]
    probability = jnp.exp(pair_scores - log_total[:, None])
    target = (jnp.arange(list_len) == 0).astype(F32)
    coefficient = LOSS_SCALE * (probability - target[None, :])

    def travel(h, step, turn):
        held = results[turn[0] * 2 + h]
        for p in turn[1:3]:
            held = lax.ppermute(held, "rep", rep_pairs(step))
            held = (held.astype(F32) + results[p * 2 + h].astype(F32)).astype(BF16)
        return lax.ppermute(held, "rep", rep_pairs(step))

    in_a = travel(0, 1, (3, 2, 1))
    in_b = travel(1, -1, (1, 2, 3))
    outgoing = pl.pallas_call(
        functools.partial(slot_kernel, share),
        out_shape=jax.ShapeDtypeStruct((slots * share, feature), BF16),
        in_specs=[SMEM] + [VMEM] * 4,
        out_specs=VMEM,
        scratch_shapes=[pltpu.VMEM((slots * share, feature), F32)],
        compiler_params=params(32),
        name="slots",
    )(slot_at, in_a, results[0], in_b, results[1])
    returned = lax.all_to_all(
        outgoing.reshape(groups, capacity * share, feature), "index", split_axis=0, concat_axis=0, tiled=True
    )
    quarter = pl.pallas_call(
        functools.partial(gradient_kernel, share, list_len),
        out_shape=jax.ShapeDtypeStruct((query_count * share, feature), BF16),
        in_specs=[SMEM, SMEM, VMEM],
        out_specs=VMEM,
        scratch_shapes=[pltpu.VMEM((slots * share, feature), F32)],
        compiler_params=params(32),
        name="gradients",
    )(place, coefficient.reshape(pairs), returned.reshape(slots * share, feature))
    gathered = lax.all_gather(quarter.reshape(query_count, share, feature), "rep")
    gradients = jnp.transpose(gathered, (1, 0, 2, 3)).reshape(query_count, query_len, feature)
    return (losses, gradients)


def solution(mesh):
    return jax.shard_map(
        per_device,
        mesh=mesh,
        in_specs=(
            P("index", None, None),
            P("index", None),
            P(),
            P("index"),
            P("index", "rep", None),
        ),
        out_specs=(P("index"), P("index", None, None)),
        check_vma=False,
    )
```

time: 716 us -> 305 us (0.43)
  local copies, waits for them, and re-layouts: 197 us -> 28.6 us
  waiting for transfers between devices: 270 us -> 114 us
  matrix products: 121 us -> 0 us
  Pallas kernels: 0 us -> 80.6 us
  other arithmetic: 45.1 us -> 6.88 us
  starting transfers between devices: 28.6 us -> 58.2 us
  blocking collectives: 33.8 us -> 12.5 us
  between operations: 14.3 us -> 1.17 us
    gather x100 -> x1, local copies, waits for them, and re-layouts: 186 us -> 1.89 us  [per_device(): pair_scores = back.reshape(slots)[place].reshape(query_count, list_len)]
    all_to_all x4 -> x3, waiting for transfers between devices: 150 us -> 26 us  [the longest x1 19.4 us: per_device(): lax.all_to_all(outgoing.reshape(groups, capacity * share, feature), 'inde...]
    dot_general x96 -> x0, matrix products: 121 us -> none  [the longest x48 69.7 us: part_stats(): jnp.einsum('btw,bpw->btp', block_tokens, picked, preferred_element_type=j...]
    psum x1 -> x0, waiting for transfers between devices: 120 us -> none  [per_device(): summed = lax.psum(terms.astype(jnp.bfloat16), 'rep').astype(jnp.float32)]
    ppermute x0 -> x32, waiting for transfers between devices: none -> 87.8 us  [the longest x4 33.7 us: travel(): held = lax.ppermute(held, 'rep', rep_pairs(step))]
    pallas_call x0 -> x6, Pallas kernels: none -> 80.6 us  [the longest x1 29.2 us: per_device(): pl.pallas_call(functools.partial(pair_kernel, places, scale), out_shape=(...]
    ppermute x0 -> x32, starting transfers between devices: none -> 38.2 us  [the longest x3 8.76 us: spread(): far_b = lax.ppermute(left[n:], 'index', ring_pairs(second, -1))]
    all_gather x2 -> x1, blocking collectives: 33.8 us -> 12.5 us  [per_device(): lax.all_gather(quarter.reshape(query_count, share, feature), 'rep')]
  transfers between devices with their start and end apart: 5 -> 35, of which waited for: 3 -> 16; matrix products, arithmetic and copies ran while one was open for 3% -> 6% of each run, Pallas kernels for 0% -> 12%
where the time goes in v1:
time: 305 us; the launch traced here: 302 us
  waiting for transfers between devices  114 us (37%)
  Pallas kernels  80.6 us (26%)
  starting transfers between devices  58.2 us (19%)
  local copies, waits for them, and re-layouts  28.6 us (9%)
  blocking collectives  12.5 us (4%)
  other arithmetic  6.88 us (2%)
    ppermute x4, waiting for transfers between devices, travel(): held = lax.ppermute(held, 'rep', rep_pairs(step))  33.7 us
    pallas_call x1, Pallas kernels, per_device(): pl.pallas_call(functools.partial(pair_kernel, places, scale), out_shape=(...  29.2 us
    pallas_call x1, Pallas kernels, per_device(): pl.pallas_call(functools.partial(sort_kernel, capacity, pages, half, bloc...  25.2 us
    ppermute x3, waiting for transfers between devices, spread(): right = lax.ppermute(x, 'index', ring_pairs(second, 1))  21.1 us
    all_to_all x1, waiting for transfers between devices, per_device(): lax.all_to_all(outgoing.reshape(groups, capacity * share, feature), 'inde...  19.4 us
    unnamed x62, local copies, waits for them, and re-layouts  15.3 us
    pallas_call x1, Pallas kernels, per_device(): pl.pallas_call(functools.partial(scale_kernel, math.sqrt(feature)), out_s...  14.3 us
    all_gather x1, blocking collectives, per_device(): lax.all_gather(quarter.reshape(query_count, share, feature), 'rep')  12.5 us
  transfers between devices with their start and end apart: 35, of which 16 were waited for; matrix products, arithmetic and copies ran while one was open for 6% of the time, Pallas kernels for 12%

profile of v1, /device:TPU:0, one launch (start us, length us, event | category | flops | bytes accessed | tf_op | source)
XLA Modules:
  0.0 301.7 jit_solution(7485695540647264963)
XLA Ops:
  0.7 1.1 dynamic-slice_bitcast_fusion
  1.8 1.4 collective-permute-done
  3.3 1.7 collective-permute-start.5
  5.0 1.6 collective-permute-start.6
  6.6 5.8 %collective-permute-done.5 = bf16[2,24,32,128]{3,2,1,0:T(8,128)(2,1)S(1)} collective-permute-done((bf16[2,24,32,128]{3,2,1,0:T(8,128)(2,1)S(1)}, bf16[2,24,32,128]{3,2,1,0:T(8,128)(2,1)S(1)}, u32[]{:S(2)}, u32[]{:S(2)}) %collective-permute-start.5) | collective-permute-done | bytes 393248 | tf_op jit(solution)/shard_map/ppermute | solution.py:62
  12.9 2.9 collective-permute-start.8
  15.8 0.8 constant_dynamic-update-slice_fusion.3
  16.5 0.8 constant_dynamic-update-slice_fusion.2
  17.3 2.0 collective-permute-done.7
  20.7 2.0 collective-permute-start.9
  22.7 2.1 collective-permute-start.10
  24.8 3.2 %collective-permute-start.2 = (bf16[2,24,32,128]{3,2,1,0:T(8,128)(2,1)S(1)}, bf16[2,24,32,128]{3,2,1,0:T(8,128)(2,1)S(1)}, u32[]{:S(2)}, u32[]{:S(2)}) collective-permute-start(bf16[2,24,32,128]{3,2,1,0:T(8,128)(2,1)S(1)} %maximum_select_fusion), channel_id=1, source_target_pairs={{0,96},{4,28},{8,104},{12,4},{16,112},{20,12},{24,120},{28,20},{32... | collective-permute-start | bytes 1179656 | tf_op jit(solution)/shard_map/ppermute | solution.py:63
  28.0 15.4 %collective-permute-done.1 = bf16[2,24,32,128]{3,2,1,0:T(8,128)(2,1)S(1)} collective-permute-done((bf16[2,24,32,128]{3,2,1,0:T(8,128)(2,1)S(1)}, bf16[2,24,32,128]{3,2,1,0:T(8,128)(2,1)S(1)}, u32[]{:S(2)}, u32[]{:S(2)}) %collective-permute-start.1) | collective-permute-done | bytes 393248 | tf_op jit(solution)/shard_map/ppermute | solution.py:62
  43.6 3.3 %collective-permute-start.4 = (bf16[1,24,32,128]{3,2,1,0:T(8,128)(2,1)S(1)}, bf16[1,24,32,128]{3,2,1,0:T(8,128)(2,1)S(1)}, u32[]{:S(2)}, u32[]{:S(2)}) collective-permute-start(bf16[1,24,32,128]{3,2,1,0:T(8,128)(2,1)S(1)} %slice.67), channel_id=1, source_target_pairs={{0,96},{4,28},{8,104},{12,4},{16,112},{20,12},{24,120},{28,20},{32... | collective-permute-start | bytes 589832 | tf_op jit(solution)/shard_map/ppermute | solution.py:65
  46.8 3.5 %collective-permute-done.3 = bf16[1,24,32,128]{3,2,1,0:T(8,128)(2,1)S(1)} collective-permute-done((bf16[1,24,32,128]{3,2,1,0:T(8,128)(2,1)S(1)}, bf16[1,24,32,128]{3,2,1,0:T(8,128)(2,1)S(1)}, u32[]{:S(2)}, u32[]{:S(2)}) %collective-permute-start.3) | collective-permute-done | bytes 196640 | tf_op jit(solution)/shard_map/ppermute | solution.py:64
  51.4 1.1 slice.70
  52.5 1.1 slice.71
  53.7 0.7 copy-done.4
  54.5 0.7 copy-done.14
  56.5 2.6 collective-permute-start.12
  59.1 0.7 copy-done.6
  59.9 0.8 copy-done.8
  61.2 5.1 %collective-permute-done.11 = bf16[3,24,32,128]{3,2,1,0:T(8,128)(2,1)S(1)} collective-permute-done((bf16[3,24,32,128]{3,2,1,0:T(8,128)(2,1)S(1)}, bf16[3,24,32,128]{3,2,1,0:T(8,128)(2,1)S(1)}, u32[]{:S(2)}, u32[]{:S(2)}) %collective-permute-start.11) | collective-permute-done | bytes 589856 | tf_op jit(solution)/shard_map/ppermute | solution.py:64
  67.5 1.4 reshape.123.listed
  68.9 6.4 %route.1 = (s32[768]{0:T(1024)}, s32[384]{0:T(512)}) custom-call(s32[384]{0:T(512)} %reshape.123.listed, s32[2048]{0:T(1024)} %page_slot.1), custom_call_target="tpu_custom_call" | custom-call | tf_op jit(solution)/shard_map/route/pallas_call | solution.py:391
  75.3 1.3 all_to_all.15
  76.6 7.6 %all-to-all-start = ((s32[32,1,24]{2,1,0:T(1,128)}), s32[32,1,24]{2,1,0:T(1,128)}, u32[]{:S(2)}, u32[]{:S(2)}) async-start(s32[32,1,24]{2,1,0:T(1,128)} %bitcast), calls=%async_computation | async-start | bytes 32768 | tf_op jit(solution)/shard_map/all_to_all | solution.py:399
  84.9 6.6 %all-to-all-done = s32[32,1,24]{2,1,0:T(1,128)} async-done(((s32[32,1,24]{2,1,0:T(1,128)}), s32[32,1,24]{2,1,0:T(1,128)}, u32[]{:S(2)}, u32[]{:S(2)}) %all-to-all-start) | async-done | bytes 3104 | tf_op jit(solution)/shard_map/all_to_all | solution.py:399
  92.1 2.0 reduce.8
  94.1 1.4 reshape.124.arrived
  95.5 25.2 %sort_pairs.1 = (s32[1728]{0:T(1024)}, s32[1728]{0:T(1024)}, s32[768]{0:T(1024)}, s32[240]{0:T(256)}, s32[240]{0:T(256)}, /*index=5*/s32[1]{0:T(128)}) custom-call(s32[768]{0:T(1024)} %reshape.124.arrived, s32[2]{0:T(128)} %pad_add_fusion.me), custom_call_target="tpu_custom_call" | custom-call | tf_op jit(solution)/shard_map/sort_pairs/pallas_call | solution.py:403
  120.8 1.0 copy-done.5
  121.8 1.0 copy-done.7
  122.7 1.0 copy-done.9
  123.7 0.9 copy-done.11
  124.7 0.9 copy-done.13
  125.6 0.9 copy-done.15
  126.5 0.9 copy-done.17
  127.5 0.7 copy-done.18
  129.5 29.2 %pairs.1 = (bf16[776,32,128]{2,1,0:T(8,128)(2,1)}, f32[240,128]{1,0:T(8,128)S(1)}, f32[240,128]{1,0:T(8,128)S(1)}) custom-call(s32[1728]{0:T(1024)S(1)} %copy-done.18, s32[240]{0:T(256)S(1)} %copy-done.24, s32[240]{0:T(256)S(1)} %copy-done.20, s32[1]{0:T(128)} %get-tuple-element.24.block_count, s32[64]{0:T(128)S(1)} %broadcast_subtract_fusion.limits, ...), custom_call_target="tpu_custom_call" | custom-call | tf_op jit(solution)/shard_map/pairs/pallas_call | solution.py:416
  158.7 3.1 %collective-permute-start.25 = (f32[2,240,128]{2,1,0:T(8,128)S(1)}, f32[2,240,128]{2,1,0:T(8,128)S(1)}, u32[]{:S(2)}, u32[]{:S(2)}) collective-permute-start(f32[2,240,128]{2,1,0:T(8,128)S(1)} %pad_maximum_fusion), channel_id=1, source_target_pairs={{0,2},{1,3},{2,0},{3,1},{4,6},{5,7},{6,4},{7,5},{8,10},{9,11},{10,... | collective-permute-start | bytes 737288 | tf_op jit(solution)/shard_map/ppermute | solution.py:438
  161.8 1.1 collective-permute-start.24
  163.2 1.0 collective-permute-start.23
  164.1 4.9 %collective-permute-done.25 = f32[2,240,128]{2,1,0:T(8,128)S(1)} collective-permute-done((f32[2,240,128]{2,1,0:T(8,128)S(1)}, f32[2,240,128]{2,1,0:T(8,128)S(1)}, u32[]{:S(2)}, u32[]{:S(2)}) %collective-permute-start.25) | collective-permute-done | bytes 245792 | tf_op jit(solution)/shard_map/ppermute | solution.py:438
  169.0 5.3 %collective-permute-done.24 = f32[2,240,128]{2,1,0:T(8,128)S(1)} collective-permute-done((f32[2,240,128]{2,1,0:T(8,128)S(1)}, f32[2,240,128]{2,1,0:T(8,128)S(1)}, u32[]{:S(2)}, u32[]{:S(2)}) %collective-permute-start.24) | collective-permute-done | bytes 245792 | tf_op jit(solution)/shard_map/ppermute | solution.py:438
  174.5 14.3 %scale.1 = (bf16[3072,128]{1,0:T(8,128)(2,1)S(1)}, bf16[3072,128]{1,0:T(8,128)(2,1)S(1)}, bf16[3072,128]{1,0:T(8,128)(2,1)S(1)}, bf16[3072,128]{1,0:T(8,128)(2,1...) custom-call(s32[240]{0:T(256)S(1)} %copy-done.21, ...), custom_call_target="tpu_custom_call" | custom-call | tf_op jit(solution)/shard_map/scale/pallas_call | solution.py:440
  188.8 2.8 collective-permute-start.29
  191.6 17.4 %collective-permute-done.29 = bf16[3072,128]{1,0:T(8,128)(2,1)S(1)} collective-permute-done((bf16[3072,128]{1,0:T(8,128)(2,1)S(1)}, bf16[3072,128]{1,0:T(8,128)(2,1)S(1)}, u32[]{:S(2)}, u32[]{:S(2)}) %collective-permute-start.29) | collective-permute-done | bytes 786464 | tf_op jit(solution)/shard_map/ppermute | solution.py:474
  209.2 3.8 %collective-permute-start.30 = (bf16[3072,128]{1,0:T(8,128)(2,1)S(1)}, bf16[3072,128]{1,0:T(8,128)(2,1)S(1)}, u32[]{:S(2)}, u32[]{:S(2)}) collective-permute-start(bf16[3072,128]{1,0:T(8,128)(2,1)S(1)} %add_convert_fusion.1), channel_id=1, source_target_pairs={{0,3},{1,0},{2,1},{3,2},{4,7},{5,4},{6,5},{7,6},{8,11},{9,8},{10,9... | collective-permute-start | bytes 2359304 | tf_op jit(solution)/shard_map/ppermute | solution.py:474
  213.2 16.3 %collective-permute-done.30 = bf16[3072,128]{1,0:T(8,128)(2,1)S(1)} collective-permute-done((bf16[3072,128]{1,0:T(8,128)(2,1)S(1)}, bf16[3072,128]{1,0:T(8,128)(2,1)S(1)}, u32[]{:S(2)}, u32[]{:S(2)}) %collective-permute-start.30) | collective-permute-done | bytes 786464 | tf_op jit(solution)/shard_map/ppermute | solution.py:474
  229.5 1.1 add_convert_fusion
  230.6 3.7 %collective-permute-start.31 = (bf16[3072,128]{1,0:T(8,128)(2,1)}, bf16[3072,128]{1,0:T(8,128)(2,1)S(1)}, u32[]{:S(2)}, u32[]{:S(2)}) collective-permute-start(bf16[3072,128]{1,0:T(8,128)(2,1)} %add_convert_fusion), channel_id=1, source_target_pairs={{0,3},{1,0},{2,1},{3,2},{4,7},{5,4},{6,5},{7,6},{8,11},{9,8},{10,9... | collective-permute-start | bytes 2359304 | tf_op jit(solution)/shard_map/ppermute | solution.py:476
  234.3 1.1 add_convert_fusion.2
  235.5 0.7 all_to_all.17
  236.1 8.3 %all-to-all-start.1 = ((f32[32,1,24]{2,1,0:T(1,128)}), f32[32,1,24]{2,1,0:T(1,128)S(1)}, u32[]{:S(2)}, u32[]{:S(2)}) async-start(f32[32,1,24]{2,1,0:T(1,128)} %bitcast.33), calls=%async_computation.1 | async-start | bytes 32768 | tf_op jit(solution)/shard_map/all_to_all | solution.py:462
  244.4 5.9 %collective-permute-done.31.in_b = bf16[3072,128]{1,0:T(8,128)(2,1)S(1)} collective-permute-done((bf16[3072,128]{1,0:T(8,128)(2,1)}, bf16[3072,128]{1,0:T(8,128)(2,1)S(1)}, u32[]{:S(2)}, u32[]{:S(2)}) %collective-permute-start.31) | collective-permute-done | bytes 786464 | tf_op jit(solution)/shard_map/ppermute | solution.py:476
  250.3 4.4 %collective-permute-done.28.in_a = bf16[3072,128]{1,0:T(8,128)(2,1)S(1)} collective-permute-done((bf16[3072,128]{1,0:T(8,128)(2,1)}, bf16[3072,128]{1,0:T(8,128)(2,1)S(1)}, u32[]{:S(2)}, u32[]{:S(2)}) %collective-permute-start.28) | collective-permute-done | bytes 786464 | tf_op jit(solution)/shard_map/ppermute | solution.py:476
  254.8 3.9 %slots.1 = bf16[6144,128]{1,0:T(8,128)(2,1)} custom-call(s32[768]{0:T(1024)S(1)} %copy-done.22, bf16[3072,128]{1,0:T(8,128)(2,1)S(1)} %collective-permute-done.28.in_a, bf16[3072,128]{1,0:T(8,128)(2,1)S(1)} %get-tuple-element.37.own_a, bf16[3072,128]{1,0:T(8,128)(2,1)S(1)} %collective-permute-done.31.in_b, bf16[3072,128]{1,0:T(8,128)(2,1)S(1)} %get-tuple-element.41.own_b), custom_call_target="tpu_custom_call" | custom-call | tf_op jit(solution)/shard_map/slots/pallas_call | solution.py:480
  258.7 4.1 %all-to-all-start.2 = ((bf16[32,192,128]{2,1,0:T(8,128)(2,1)}), bf16[32,192,128]{2,1,0:T(8,128)(2,1)S(1)}, u32[]{:S(2)}, u32[]{:S(2)}) async-start(bf16[32,192,128]{2,1,0:T(8,128)(2,1)} %bitcast.34), calls=%async_computation.2 | async-start | bytes 3145728 | tf_op jit(solution)/shard_map/all_to_all | solution.py:489
  264.2 1.9 gather_fusion
  267.4 19.4 %all-to-all-done.2 = bf16[32,192,128]{2,1,0:T(8,128)(2,1)S(1)} async-done(((bf16[32,192,128]{2,1,0:T(8,128)(2,1)}), bf16[32,192,128]{2,1,0:T(8,128)(2,1)S(1)}, u32[]{:S(2)}, u32[]{:S(2)}) %all-to-all-start.2) | async-done | bytes 1572896 | tf_op jit(solution)/shard_map/all_to_all | solution.py:489
  286.7 1.6 gradients.1
  288.4 12.5 %all_gather.3 = bf16[4,48,8,128]{3,2,1,0:T(8,128)(2,1)S(1)} all-gather(bf16[1,48,8,128]{3,2,1,0:T(8,128)(2,1)S(1)} %bitcast.59), channel_id=1, replica_groups=mesh['index'=32,'rep'=4] {'rep'}, dimensions={0}, use_global_device_ids=true | all-gather | bytes 491520 | tf_op jit(solution)/shard_map/all_gather | solution.py:501
  300.9 0.8 copy.20
  (120 shorter events, 12.3 us)
Async XLA Ops:
  1.7 1.5 collective-permute-start
  3.3 9.1 %collective-permute-start.5 = (bf16[2,24,32,128]{3,2,1,0:T(8,128)(2,1)S(1)}, bf16[2,24,32,128]{3,2,1,0:T(8,128)(2,1)S(1)}, u32[]{:S(2)}, u32[]{:S(2)}) collective-permute-start(bf16[2,24,32,128]{3,2,1,0:T(8,128)(2,1)S(1)} %maximum_select_fusion), channel_id=1, source_target_pairs={{0,8},{4,36},{8,16},{12,44},{16,24},{20,52},{24,0},{28,60},{32,40}... | collective-permute-start | bytes 1179656 | tf_op jit(solution)/shard_map/ppermute | solution.py:62
  5.0 7.9 %collective-permute-start.6 = (bf16[2,24,32,128]{3,2,1,0:T(8,128)(2,1)S(1)}, bf16[2,24,32,128]{3,2,1,0:T(8,128)(2,1)S(1)}, u32[]{:S(2)}, u32[]{:S(2)}) collective-permute-start(bf16[2,24,32,128]{3,2,1,0:T(8,128)(2,1)S(1)} %maximum_select_fusion), channel_id=1, source_target_pairs={{0,24},{4,100},{8,0},{12,108},{16,8},{20,116},{24,16},{28,124},{32... | collective-permute-start | bytes 1179656 | tf_op jit(solution)/shard_map/ppermute | solution.py:63
  12.4 6.9 %collective-permute-start.7 = (bf16[1,24,32,128]{3,2,1,0:T(8,128)(2,1)S(1)}, bf16[1,24,32,128]{3,2,1,0:T(8,128)(2,1)S(1)}, u32[]{:S(2)}, u32[]{:S(2)}) collective-permute-start(bf16[1,24,32,128]{3,2,1,0:T(8,128)(2,1)S(1)} %slice.68), channel_id=1, source_target_pairs={{0,8},{4,36},{8,16},{12,44},{16,24},{20,52},{24,0},{28,60},{32,40}... | collective-permute-start | bytes 589832 | tf_op jit(solution)/shard_map/ppermute | solution.py:64
  12.9 7.1 %collective-permute-start.8 = (bf16[1,24,32,128]{3,2,1,0:T(8,128)(2,1)S(1)}, bf16[1,24,32,128]{3,2,1,0:T(8,128)(2,1)S(1)}, u32[]{:S(2)}, u32[]{:S(2)}) collective-permute-start(bf16[1,24,32,128]{3,2,1,0:T(8,128)(2,1)S(1)} %slice.69), channel_id=1, source_target_pairs={{0,24},{4,100},{8,0},{12,108},{16,8},{20,116},{24,16},{28,124},{32... | collective-permute-start | bytes 589832 | tf_op jit(solution)/shard_map/ppermute | solution.py:65
  20.7 30.2 %collective-permute-start.9 = (bf16[6,24,32,128]{3,2,1,0:T(8,128)(2,1)}, bf16[6,24,32,128]{3,2,1,0:T(8,128)(2,1)}, u32[]{:S(2)}, u32[]{:S(2)}) collective-permute-start(bf16[6,24,32,128]{3,2,1,0:T(8,128)(2,1)} %constant_dynamic-update-slice_fusion), channel_id=1, source_target_pairs={{0,32},{4,12},{8,40},{12,20},{16,48},{20,28},{24,56},{28,4},{32,64... | collective-permute-start | bytes 3538952 | tf_op jit(solution)/shard_map/ppermute | solution.py:62
  22.7 28.3 %collective-permute-start.10 = (bf16[6,24,32,128]{3,2,1,0:T(8,128)(2,1)}, bf16[6,24,32,128]{3,2,1,0:T(8,128)(2,1)}, u32[]{:S(2)}, u32[]{:S(2)}) collective-permute-start(bf16[6,24,32,128]{3,2,1,0:T(8,128)(2,1)} %constant_dynamic-update-slice_fusion), channel_id=1, source_target_pairs={{0,96},{4,28},{8,104},{12,4},{16,112},{20,12},{24,120},{28,20},{32... | collective-permute-start | bytes 3538952 | tf_op jit(solution)/shard_map/ppermute | solution.py:63
  24.8 18.6 %collective-permute-start.1 = (bf16[2,24,32,128]{3,2,1,0:T(8,128)(2,1)S(1)}, bf16[2,24,32,128]{3,2,1,0:T(8,128)(2,1)S(1)}, u32[]{:S(2)}, u32[]{:S(2)}) collective-permute-start(bf16[2,24,32,128]{3,2,1,0:T(8,128)(2,1)S(1)} %maximum_select_fusion), channel_id=1, source_target_pairs={{0,32},{4,12},{8,40},{12,20},{16,48},{20,28},{24,56},{28,4},{32,64... | collective-permute-start | bytes 1179656 | tf_op jit(solution)/shard_map/ppermute | solution.py:62
  24.8 18.7 %collective-permute-start.2 = (bf16[2,24,32,128]{3,2,1,0:T(8,128)(2,1)S(1)}, bf16[2,24,32,128]{3,2,1,0:T(8,128)(2,1)S(1)}, u32[]{:S(2)}, u32[]{:S(2)}) collective-permute-start(bf16[2,24,32,128]{3,2,1,0:T(8,128)(2,1)S(1)} %maximum_select_fusion), channel_id=1, source_target_pairs={{0,96},{4,28},{8,104},{12,4},{16,112},{20,12},{24,120},{28,20},{32... | collective-permute-start | bytes 1179656 | tf_op jit(solution)/shard_map/ppermute | solution.py:63
  43.4 7.0 %collective-permute-start.3 = (bf16[1,24,32,128]{3,2,1,0:T(8,128)(2,1)S(1)}, bf16[1,24,32,128]{3,2,1,0:T(8,128)(2,1)S(1)}, u32[]{:S(2)}, u32[]{:S(2)}) collective-permute-start(bf16[1,24,32,128]{3,2,1,0:T(8,128)(2,1)S(1)} %slice.66), channel_id=1, source_target_pairs={{0,32},{4,12},{8,40},{12,20},{16,48},{20,28},{24,56},{28,4},{32,64... | collective-permute-start | bytes 589832 | tf_op jit(solution)/shard_map/ppermute | solution.py:64
  43.5 23.3 %copy-start.26 = (s32[48,8]{0,1:T(8,128)S(1)}, s32[48,8]{0,1:T(8,128)}, u32[]{:S(2)}) copy-start(s32[48,8]{0,1:T(8,128)} %param.6) | copy-start | bytes 4612
  43.5 40.7 %copy-start.28 = (s32[64]{0:T(128)S(1)}, s32[64]{0:T(128)}, u32[]{:S(2)}) copy-start(s32[64]{0:T(128)} %param.8) | copy-start | bytes 772
  43.6 6.8 %collective-permute-start.4 = (bf16[1,24,32,128]{3,2,1,0:T(8,128)(2,1)S(1)}, bf16[1,24,32,128]{3,2,1,0:T(8,128)(2,1)S(1)}, u32[]{:S(2)}, u32[]{:S(2)}) collective-permute-start(bf16[1,24,32,128]{3,2,1,0:T(8,128)(2,1)S(1)} %slice.67), channel_id=1, source_target_pairs={{0,96},{4,28},{8,104},{12,4},{16,112},{20,12},{24,120},{28,20},{32... | collective-permute-start | bytes 589832 | tf_op jit(solution)/shard_map/ppermute | solution.py:65
  46.8 6.8 %collective-permute-start.13 = (bf16[2,24,32,128]{3,2,1,0:T(8,128)(2,1)S(1)}, bf16[2,24,32,128]{3,2,1,0:T(8,128)(2,1)S(1)}, u32[]{:S(2)}, u32[]{:S(2)}) collective-permute-start(bf16[2,24,32,128]{3,2,1,0:T(8,128)(2,1)S(1)} %maximum_select_fusion), channel_id=1, source_target_pairs={{0,4},{4,0},{8,12},{12,8},{16,20},{20,16},{24,28},{28,24},{32,36},... | collective-permute-start | bytes 1179656 | tf_op jit(solution)/shard_map/ppermute | solution.py:50
  50.4 3.3 %copy-start.10 = (bf16[1,24,32,128]{3,2,1,0:T(8,128)(2,1)}, bf16[1,24,32,128]{3,2,1,0:T(8,128)(2,1)S(1)}, u32[]{:S(2)}) copy-start(bf16[1,24,32,128]{3,2,1,0:T(8,128)(2,1)S(1)} %collective-permute-done.3) | copy-start | bytes 589828
  50.4 8.8 %collective-permute-start.14 = (bf16[2,24,32,128]{3,2,1,0:T(8,128)(2,1)S(1)}, bf16[2,24,32,128]{3,2,1,0:T(8,128)(2,1)S(1)}, u32[]{:S(2)}, u32[]{:S(2)}) collective-permute-start(bf16[2,24,32,128]{3,2,1,0:T(8,128)(2,1)S(1)} %collective-permute-done.1), channel_id=1, source_target_pairs={{0,4},{4,0},{8,12},{12,8},{16,20},{20,16},{24,28},{28,24},{32,36},... | collective-permute-start | bytes 1179656 | tf_op jit(solution)/shard_map/ppermute | solution.py:50
  50.4 3.3 %copy-start.12 = (bf16[1,24,32,128]{3,2,1,0:T(8,128)(2,1)}, bf16[1,24,32,128]{3,2,1,0:T(8,128)(2,1)S(1)}, u32[]{:S(2)}) copy-start(bf16[1,24,32,128]{3,2,1,0:T(8,128)(2,1)S(1)} %collective-permute-done.4) | copy-start | bytes 589828
  50.4 9.5 %collective-permute-start.15 = (bf16[2,24,32,128]{3,2,1,0:T(8,128)(2,1)S(1)}, bf16[2,24,32,128]{3,2,1,0:T(8,128)(2,1)S(1)}, u32[]{:S(2)}, u32[]{:S(2)}) collective-permute-start(bf16[2,24,32,128]{3,2,1,0:T(8,128)(2,1)S(1)} %collective-permute-done.2), channel_id=1, source_target_pairs={{0,4},{4,0},{8,12},{12,8},{16,20},{20,16},{24,28},{28,24},{32,36},... | collective-permute-start | bytes 1179656 | tf_op jit(solution)/shard_map/ppermute | solution.py:50
  50.9 3.6 %collective-permute-start.16 = (bf16[1,24,32,128]{3,2,1,0:T(8,128)(2,1)S(1)}, bf16[1,24,32,128]{3,2,1,0:T(8,128)(2,1)S(1)}, u32[]{:S(2)}, u32[]{:S(2)}) collective-permute-start(bf16[1,24,32,128]{3,2,1,0:T(8,128)(2,1)S(1)} %collective-permute-done.3), channel_id=1, source_target_pairs={{0,4},{4,0},{8,12},{12,8},{16,20},{20,16},{24,28},{28,24},{32,36},... | collective-permute-start | bytes 589832 | tf_op jit(solution)/shard_map/ppermute | solution.py:50
  51.0 4.8 %collective-permute-start.17 = (bf16[1,24,32,128]{3,2,1,0:T(8,128)(2,1)S(1)}, bf16[1,24,32,128]{3,2,1,0:T(8,128)(2,1)S(1)}, u32[]{:S(2)}, u32[]{:S(2)}) collective-permute-start(bf16[1,24,32,128]{3,2,1,0:T(8,128)(2,1)S(1)} %collective-permute-done.4), channel_id=1, source_target_pairs={{0,4},{4,0},{8,12},{12,8},{16,20},{20,16},{24,28},{28,24},{32,36},... | collective-permute-start | bytes 589832 | tf_op jit(solution)/shard_map/ppermute | solution.py:50
  53.7 0.7 copy-start.4
  54.4 66.3 %collective-permute-start.18 = (bf16[6,24,32,128]{3,2,1,0:T(8,128)(2,1)}, bf16[6,24,32,128]{3,2,1,0:T(8,128)(2,1)}, u32[]{:S(2)}, u32[]{:S(2)}) collective-permute-start(bf16[6,24,32,128]{3,2,1,0:T(8,128)(2,1)} %constant_dynamic-update-slice_fusion), channel_id=1, source_target_pairs={{0,4},{4,0},{8,12},{12,8},{16,20},{20,16},{24,28},{28,24},{32,36},... | collective-permute-start | bytes 3538952 | tf_op jit(solution)/shard_map/ppermute | solution.py:50
  54.5 0.7 copy-start.14
  55.2 11.1 %collective-permute-start.11 = (bf16[3,24,32,128]{3,2,1,0:T(8,128)(2,1)S(1)}, bf16[3,24,32,128]{3,2,1,0:T(8,128)(2,1)S(1)}, u32[]{:S(2)}, u32[]{:S(2)}) collective-permute-start(bf16[3,24,32,128]{3,2,1,0:T(8,128)(2,1)S(1)} %slice.70), channel_id=1, source_target_pairs={{0,32},{4,12},{8,40},{12,20},{16,48},{20,28},{24,56},{28,4},{32,64... | collective-permute-start | bytes 1769480 | tf_op jit(solution)/shard_map/ppermute | solution.py:64
  55.8 0.7 copy-start.16
  56.5 10.0 %collective-permute-start.12 = (bf16[3,24,32,128]{3,2,1,0:T(8,128)(2,1)S(1)}, bf16[3,24,32,128]{3,2,1,0:T(8,128)(2,1)S(1)}, u32[]{:S(2)}, u32[]{:S(2)}) collective-permute-start(bf16[3,24,32,128]{3,2,1,0:T(8,128)(2,1)S(1)} %slice.71), channel_id=1, source_target_pairs={{0,96},{4,28},{8,104},{12,4},{16,112},{20,12},{24,120},{28,20},{32... | collective-permute-start | bytes 1769480 | tf_op jit(solution)/shard_map/ppermute | solution.py:65
  59.1 0.7 copy-start.6
  59.9 60.9 %collective-permute-start.19 = (bf16[6,24,32,128]{3,2,1,0:T(8,128)(2,1)}, bf16[6,24,32,128]{3,2,1,0:T(8,128)(2,1)}, u32[]{:S(2)}, u32[]{:S(2)}) collective-permute-start(bf16[6,24,32,128]{3,2,1,0:T(8,128)(2,1)} %collective-permute-done.9), channel_id=1, source_target_pairs={{0,4},{4,0},{8,12},{12,8},{16,20},{20,16},{24,28},{28,24},{32,36},... | collective-permute-start | bytes 3538952 | tf_op jit(solution)/shard_map/ppermute | solution.py:50
  59.9 0.8 copy-start.8
  60.6 60.1 %collective-permute-start.20 = (bf16[6,24,32,128]{3,2,1,0:T(8,128)(2,1)}, bf16[6,24,32,128]{3,2,1,0:T(8,128)(2,1)}, u32[]{:S(2)}, u32[]{:S(2)}) collective-permute-start(bf16[6,24,32,128]{3,2,1,0:T(8,128)(2,1)} %collective-permute-done.10), channel_id=1, source_target_pairs={{0,4},{4,0},{8,12},{12,8},{16,20},{20,16},{24,28},{28,24},{32,36},... | collective-permute-start | bytes 3538952 | tf_op jit(solution)/shard_map/ppermute | solution.py:50
  66.3 54.4 %collective-permute-start.21 = (bf16[3,24,32,128]{3,2,1,0:T(8,128)(2,1)S(1)}, bf16[3,24,32,128]{3,2,1,0:T(8,128)(2,1)S(1)}, u32[]{:S(2)}, u32[]{:S(2)}) collective-permute-start(bf16[3,24,32,128]{3,2,1,0:T(8,128)(2,1)S(1)} %collective-permute-done.11), channel_id=1, source_target_pairs={{0,4},{4,0},{8,12},{12,8},{16,20},{20,16},{24,28},{28,24},{32,36},... | collective-permute-start | bytes 1769480 | tf_op jit(solution)/shard_map/ppermute | solution.py:50
  66.5 54.2 %collective-permute-start.22 = (bf16[3,24,32,128]{3,2,1,0:T(8,128)(2,1)S(1)}, bf16[3,24,32,128]{3,2,1,0:T(8,128)(2,1)S(1)}, u32[]{:S(2)}, u32[]{:S(2)}) collective-permute-start(bf16[3,24,32,128]{3,2,1,0:T(8,128)(2,1)S(1)} %collective-permute-done.12), channel_id=1, source_target_pairs={{0,4},{4,0},{8,12},{12,8},{16,20},{20,16},{24,28},{28,24},{32,36},... | collective-permute-start | bytes 1769480 | tf_op jit(solution)/shard_map/ppermute | solution.py:50
  76.6 15.0 %all-to-all-start = ((s32[32,1,24]{2,1,0:T(1,128)}), s32[32,1,24]{2,1,0:T(1,128)}, u32[]{:S(2)}, u32[]{:S(2)}) async-start(s32[32,1,24]{2,1,0:T(1,128)} %bitcast), calls=%async_computation | async-start | bytes 32768 | tf_op jit(solution)/shard_map/all_to_all | solution.py:399
  120.8 1.0 copy-start.5
  121.8 1.0 copy-start.7
  122.7 1.0 copy-start.9
  123.7 0.9 copy-start.11
  124.7 0.9 copy-start.13
  125.6 0.9 copy-start.15
  126.5 0.9 copy-start.17
  127.5 0.7 copy-start.18
  128.2 0.7 copy-start.20
  128.8 0.7 copy-start.24
  129.5 33.5 %copy-start.27 = (s32[1728]{0:T(1024)S(1)}, s32[1728]{0:T(1024)}, u32[]{:S(2)}) copy-start(s32[1728]{0:T(1024)} %get-tuple-element.25) | copy-start | bytes 20740
  158.7 4.3 %copy-start = (f32[240,128]{1,0:T(8,128)}, f32[240,128]{1,0:T(8,128)S(1)}, u32[]{:S(2)}) copy-start(f32[240,128]{1,0:T(8,128)S(1)} %get-tuple-element.28.refs_0_) | copy-start | bytes 368644
  158.7 4.3 %copy-start.2 = (f32[240,128]{1,0:T(8,128)}, f32[240,128]{1,0:T(8,128)S(1)}, u32[]{:S(2)}) copy-start(f32[240,128]{1,0:T(8,128)S(1)} %get-tuple-element.29.refs_4_) | copy-start | bytes 368644
  158.7 15.8 %copy-start.21 = (s32[240]{0:T(256)S(1)}, s32[240]{0:T(256)}, u32[]{:S(2)}) copy-start(s32[240]{0:T(256)} %get-tuple-element.23.block_at) | copy-start | bytes 2884
  158.7 15.8 %copy-start.23 = (s32[2]{0:T(128)S(1)}, s32[2]{0:T(128)}, u32[]{:S(2)}) copy-start(s32[2]{0:T(128)} %pad_add_fusion.me) | copy-start | bytes 28
  158.7 10.3 %collective-permute-start.25 = (f32[2,240,128]{2,1,0:T(8,128)S(1)}, f32[2,240,128]{2,1,0:T(8,128)S(1)}, u32[]{:S(2)}, u32[]{:S(2)}) collective-permute-start(f32[2,240,128]{2,1,0:T(8,128)S(1)} %pad_maximum_fusion), channel_id=1, source_target_pairs={{0,2},{1,3},{2,0},{3,1},{4,6},{5,7},{6,4},{7,5},{8,10},{9,11},{10,... | collective-permute-start | bytes 737288 | tf_op jit(solution)/shard_map/ppermute | solution.py:438
  161.8 12.5 %collective-permute-start.24 = (f32[2,240,128]{2,1,0:T(8,128)S(1)}, f32[2,240,128]{2,1,0:T(8,128)S(1)}, u32[]{:S(2)}, u32[]{:S(2)}) collective-permute-start(f32[2,240,128]{2,1,0:T(8,128)S(1)} %pad_maximum_fusion), channel_id=1, source_target_pairs={{0,3},{1,0},{2,1},{3,2},{4,7},{5,4},{6,5},{7,6},{8,11},{9,8},{10,9... | collective-permute-start | bytes 737288 | tf_op jit(solution)/shard_map/ppermute | solution.py:438
  163.0 11.5 %copy-start.1 = (f32[240,128]{1,0:T(8,128)S(1)}, f32[240,128]{1,0:T(8,128)}, u32[]{:S(2)}) copy-start(f32[240,128]{1,0:T(8,128)} %copy-done) | copy-start | bytes 368644
  163.0 11.5 %copy-start.3 = (f32[240,128]{1,0:T(8,128)S(1)}, f32[240,128]{1,0:T(8,128)}, u32[]{:S(2)}) copy-start(f32[240,128]{1,0:T(8,128)} %copy-done.2) | copy-start | bytes 368644
  163.2 11.3 %collective-permute-start.23 = (f32[2,240,128]{2,1,0:T(8,128)S(1)}, f32[2,240,128]{2,1,0:T(8,128)S(1)}, u32[]{:S(2)}, u32[]{:S(2)}) collective-permute-start(f32[2,240,128]{2,1,0:T(8,128)S(1)} %pad_maximum_fusion), channel_id=1, source_target_pairs={{0,1},{1,2},{2,3},{3,0},{4,5},{5,6},{6,7},{7,4},{8,9},{9,10},{10,1... | collective-permute-start | bytes 737288 | tf_op jit(solution)/shard_map/ppermute | solution.py:438
  188.8 20.2 %collective-permute-start.29 = (bf16[3072,128]{1,0:T(8,128)(2,1)S(1)}, bf16[3072,128]{1,0:T(8,128)(2,1)S(1)}, u32[]{:S(2)}, u32[]{:S(2)}) collective-permute-start(bf16[3072,128]{1,0:T(8,128)(2,1)S(1)} %get-tuple-element.38), channel_id=1, source_target_pairs={{0,3},{1,0},{2,1},{3,2},{4,7},{5,4},{6,5},{7,6},{8,11},{9,8},{10,9... | collective-permute-start | bytes 2359304 | tf_op jit(solution)/shard_map/ppermute | solution.py:474
  191.6 21.4 %collective-permute-start.26 = (bf16[3072,128]{1,0:T(8,128)(2,1)}, bf16[3072,128]{1,0:T(8,128)(2,1)S(1)}, u32[]{:S(2)}, u32[]{:S(2)}) collective-permute-start(bf16[3072,128]{1,0:T(8,128)(2,1)} %get-tuple-element.34), channel_id=1, source_target_pairs={{0,1},{1,2},{2,3},{3,0},{4,5},{5,6},{6,7},{7,4},{8,9},{9,10},{10,1... | collective-permute-start | bytes 2359304 | tf_op jit(solution)/shard_map/ppermute | solution.py:474
  209.2 20.4 %collective-permute-start.30 = (bf16[3072,128]{1,0:T(8,128)(2,1)S(1)}, bf16[3072,128]{1,0:T(8,128)(2,1)S(1)}, u32[]{:S(2)}, u32[]{:S(2)}) collective-permute-start(bf16[3072,128]{1,0:T(8,128)(2,1)S(1)} %add_convert_fusion.1), channel_id=1, source_target_pairs={{0,3},{1,0},{2,1},{3,2},{4,7},{5,4},{6,5},{7,6},{8,11},{9,8},{10,9... | collective-permute-start | bytes 2359304 | tf_op jit(solution)/shard_map/ppermute | solution.py:474
  212.9 16.6 %copy-start.25 = (bf16[3072,128]{1,0:T(8,128)(2,1)S(1)}, bf16[3072,128]{1,0:T(8,128)(2,1)}, u32[]{:S(2)}) copy-start(bf16[3072,128]{1,0:T(8,128)(2,1)} %get-tuple-element.40) | copy-start | bytes 2359300
  213.2 21.2 %collective-permute-start.27 = (bf16[3072,128]{1,0:T(8,128)(2,1)S(1)}, bf16[3072,128]{1,0:T(8,128)(2,1)S(1)}, u32[]{:S(2)}, u32[]{:S(2)}) collective-permute-start(bf16[3072,128]{1,0:T(8,128)(2,1)S(1)} %add_convert_fusion.3), channel_id=1, source_target_pairs={{0,1},{1,2},{2,3},{3,0},{4,5},{5,6},{6,7},{7,4},{8,9},{9,10},{10,1... | collective-permute-start | bytes 2359304 | tf_op jit(solution)/shard_map/ppermute | solution.py:474
  230.6 19.7 %collective-permute-start.31 = (bf16[3072,128]{1,0:T(8,128)(2,1)}, bf16[3072,128]{1,0:T(8,128)(2,1)S(1)}, u32[]{:S(2)}, u32[]{:S(2)}) collective-permute-start(bf16[3072,128]{1,0:T(8,128)(2,1)} %add_convert_fusion), channel_id=1, source_target_pairs={{0,3},{1,0},{2,1},{3,2},{4,7},{5,4},{6,5},{7,6},{8,11},{9,8},{10,9... | collective-permute-start | bytes 2359304 | tf_op jit(solution)/shard_map/ppermute | solution.py:476
  234.3 20.5 %copy-start.22 = (s32[768]{0:T(1024)S(1)}, s32[768]{0:T(1024)}, u32[]{:S(2)}) copy-start(s32[768]{0:T(1024)} %get-tuple-element.33.slot_at) | copy-start | bytes 9220
  235.5 19.3 %collective-permute-start.28 = (bf16[3072,128]{1,0:T(8,128)(2,1)}, bf16[3072,128]{1,0:T(8,128)(2,1)S(1)}, u32[]{:S(2)}, u32[]{:S(2)}) collective-permute-start(bf16[3072,128]{1,0:T(8,128)(2,1)} %add_convert_fusion.2), channel_id=1, source_target_pairs={{0,1},{1,2},{2,3},{3,0},{4,5},{5,6},{6,7},{7,4},{8,9},{9,10},{10,1... | collective-permute-start | bytes 2359304 | tf_op jit(solution)/shard_map/ppermute | solution.py:476
  236.1 22.5 %all-to-all-start.1 = ((f32[32,1,24]{2,1,0:T(1,128)}), f32[32,1,24]{2,1,0:T(1,128)S(1)}, u32[]{:S(2)}, u32[]{:S(2)}) async-start(f32[32,1,24]{2,1,0:T(1,128)} %bitcast.33), calls=%async_computation.1 | async-start | bytes 32768 | tf_op jit(solution)/shard_map/all_to_all | solution.py:462
  258.7 4.2 %copy-start.19 = (s32[384]{0:T(512)S(1)}, s32[384]{0:T(512)}, u32[]{:S(2)}) copy-start(s32[384]{0:T(512)} %get-tuple-element.32.place) | copy-start | bytes 4612
  258.7 28.0 %all-to-all-start.2 = ((bf16[32,192,128]{2,1,0:T(8,128)(2,1)}), bf16[32,192,128]{2,1,0:T(8,128)(2,1)S(1)}, u32[]{:S(2)}, u32[]{:S(2)}) async-start(bf16[32,192,128]{2,1,0:T(8,128)(2,1)} %bitcast.34), calls=%async_computation.2 | async-start | bytes 3145728 | tf_op jit(solution)/shard_map/all_to_all | solution.py:489

commit v2 on v0

v2 whole, which is shorter than its diff:
```python
import functools
import math

import jax
import jax.numpy as jnp
from jax import lax
from jax.experimental import pallas as pl
from jax.experimental.pallas import tpu as pltpu
from jax.sharding import PartitionSpec as P

TAU = 0.1
LOSS_SCALE = 32.0
NEG = -1e30
BLOCK = 4
UNROLL = 16
CHUNKS = 2
LANES = 128
STRIDE = 256
PIECES = 3
RING = 4
F32 = jnp.float32
BF16 = jnp.bfloat16

SMEM = pl.BlockSpec(memory_space=pltpu.SMEM)
VMEM = pl.BlockSpec(memory_space=pltpu.VMEM)
ANY = pl.BlockSpec(memory_space=pl.ANY)


def params(mib):
    return pltpu.CompilerParams(vmem_limit_bytes=mib * 1024 * 1024)


def place_of(z, y, core):
    return ((z % RING) * RING + (y % RING)) * 2 + core


def ring_pairs(second, step):
    pairs = []
    for z in range(RING):
        for y in range(RING):
            for core in range(2):
                if (core == 0) != second:
                    there = place_of(z, y + step, core)
                else:
                    there = place_of(z + step, y, core)
                pairs.append((place_of(z, y, core), there))
    return pairs


CORE_PAIRS = [(i, i ^ 1) for i in range(2 * RING * RING)]


def across(x):
    return lax.ppermute(x, "index", CORE_PAIRS)


def gather_queries(queries, core):
    half = queries.shape[0] // 2
    keep = lax.dynamic_slice_in_dim(queries, core * half, half, 0)
    give = lax.dynamic_slice_in_dim(queries, (1 - core) * half, half, 0)
    got = across(give)
    own = jnp.where(core == 0, jnp.stack([keep, got]), jnp.stack([got, keep]))

    def spread(x, second):
        n = x.shape[0] // 2
        right = lax.ppermute(x, "index", ring_pairs(second, 1))
        left = lax.ppermute(x, "index", ring_pairs(second, -1))
        far_a = lax.ppermute(right[:n], "index", ring_pairs(second, 1))
        far_b = lax.ppermute(left[n:], "index", ring_pairs(second, -1))
        return right, left, far_a, far_b

    right, left, far_a, far_b = spread(own, False)
    own_spread = spread(own, True)
    rest = jnp.concatenate([right, left, far_a, far_b], axis=0)
    rest_spread = spread(rest, True)
    pieces = []
    for p, x in enumerate((own, own_spread[0], own_spread[1])):
        pieces.append((x, 8 * p))
    pieces.append((own_spread[2], 24))
    pieces.append((own_spread[3], 25))
    for p, x in enumerate((rest, rest_spread[0], rest_spread[1])):
        pieces.append((x, 8 * p + 2))
    pieces.append((rest_spread[2], 26))
    pieces.append((rest_spread[3], 29))
    swapped = [(across(x), 32 + at) for x, at in pieces]
    return pieces + swapped


def route_kernel(capacity, page_bits, list_len, listed, page_slot, table, place, used):
    slots = table.shape[0]
    pairs = listed.shape[0]
    groups = used.shape[0]
    sub = capacity // CHUNKS

    def clear(i, _):
        for k in range(16):
            table[i * 16 + k] = -1
        return 0

    lax.fori_loop(0, slots // 16, clear, 0)
    for i in range(groups):
        used[i] = 0

    def step(q, _):
        for k in range(list_len):
            i = q * list_len + k
            row = page_slot[listed[i]]
            owner = lax.shift_right_logical(row, page_bits)
            n = jnp.minimum(used[owner], capacity - 1)
            used[owner] = n + 1
            chunk = n & 1
            j = lax.shift_right_logical(n, 1)
            table[owner * capacity + chunk * sub + j] = lax.shift_left(q, page_bits) + (row & ((1 << page_bits) - 1))
            place[i] = chunk * (groups * sub) + owner * sub + j
        return 0

    lax.fori_loop(0, pairs // list_len, step, 0)


def sort_kernel(capacity, page_bits, half, blocks, arrived, me, order, block_page, block_count, count, first):
    slots = arrived.shape[0]
    groups = slots // capacity
    sub = capacity // CHUNKS
    pages = 1 << page_bits
    z = lax.shift_right_logical(me[0], 3)
    y = lax.shift_right_logical(me[0], 1) & (RING - 1)
    core = me[0] & 1
    nothing = (groups // 2) * sub * 2048

    def clear(i, _):
        for k in range(16):
            order[i * 16 + k] = nothing
        return 0

    lax.fori_loop(0, CHUNKS * blocks * BLOCK // 16, clear, 0)

    def clear_blocks(i, _):
        for k in range(16):
            block_page[i * 16 + k] = 0
        return 0

    lax.fori_loop(0, CHUNKS * blocks // 16, clear_blocks, 0)
    for i in range(CHUNKS * pages + 1):
        count[i] = 0

    def tally(s, _):
        for chunk in range(CHUNKS):
            for j in range(sub):
                code = arrived[s * capacity + chunk * sub + j]
                p = jnp.where(code < 0, CHUNKS * pages, (code & (pages - 1)) + chunk * pages)
                count[p] = count[p] + 1
        return 0

    lax.fori_loop(0, groups, tally, 0)

    for chunk in range(CHUNKS):

        def lay(p, b):
            n = count[chunk * pages + p]
            first[chunk * pages + p] = b * BLOCK
            count[chunk * pages + p] = 0
            steps = lax.shift_right_logical(n + BLOCK - 1, 2)

            def one(k, _):
                block_page[b + k] = p
                return 0

            lax.fori_loop(0, steps, one, 0)
            return b + steps

        total = lax.fori_loop(0, pages, lay, jnp.int32(chunk * blocks))
        block_count[chunk] = total - chunk * blocks
    first[CHUNKS * pages] = CHUNKS * blocks * BLOCK
    count[CHUNKS * pages] = 0

    def rank(there, mine):
        apart = (there - mine) & (RING - 1)
        return jnp.where(apart == 0, 0, jnp.where(apart == RING - 1, 1, jnp.where(apart == 1, 2, 3)))

    def source(s, _):
        dz = rank(lax.shift_right_logical(s, 3), z)
        dy = rank(lax.shift_right_logical(s, 1) & (RING - 1), y)
        sc = s & 1
        low = ((jnp.where(core == 0, 0, RING) + dz) * RING + dy) * 2 + sc
        high = ((jnp.where(core == 1, 0, RING) + dy) * RING + dz) * 2 + sc
        side = lax.shift_right_logical(s, 4)
        slot = side * STRIDE + (s & 15) * sub
        low_base = low * half + slot * 2048
        high_base = high * half - half + slot * 2048
        for chunk in range(CHUNKS):
            for j in range(sub):
                code = arrived[s * capacity + chunk * sub + j]
                p = jnp.where(code < 0, CHUNKS * pages, (code & (pages - 1)) + chunk * pages)
                q = lax.shift_right_logical(jnp.maximum(code, 0), page_bits)
                r = count[p]
                count[p] = r + 1
                order[first[p] + r] = q + jnp.where(q < half, low_base, high_base) + j * 2048
        return 0

    lax.fori_loop(0, groups, source, 0)


def split(x):
    parts = []
    for _ in range(PIECES):
        part = x.astype(BF16)
        parts.append(part)
        x = x - part.astype(F32)
    return parts


def pair_kernel(chunk, blocks, places, scale, order, block_page, block_count, limits, me, *refs):
    n_pieces = len(places)
    store = refs[0]
    pieces = refs[1 : 1 + n_pieces]
    outs = refs[1 + n_pieces : 9 + n_pieces]
    held, pages, wide, stats, sems = refs[9 + n_pieces :]
    copies = [pltpu.make_async_copy(store, pages, sems.at[n_pieces])]
    for k, (ref, at) in enumerate(zip(pieces, places, strict=True)):
        copies.append(pltpu.make_async_copy(ref, held.at[pl.ds(at, ref.shape[0])], sems.at[k]))
    for c in copies:
        c.start()
    for c in copies:
        c.wait()
    part = pages.shape[1]
    tokens = held.shape[1]
    share = tokens // 4
    power = scale * math.log2(math.e)
    lane = lax.broadcasted_iota(jnp.int32, (1, part), 1)
    lanes = lax.broadcasted_iota(jnp.int32, (tokens, LANES), 1)

    def step(it, _):
        for u in range(UNROLL):
            b = chunk * blocks + it * UNROLL + u
            p = block_page[b]
            codes = [order[b * BLOCK + i] for i in range(BLOCK)]
            block = jnp.concatenate([held[c & 2047] for c in codes], axis=0)
            page = pages[p]
            raw = lax.dot_general(block, page, (((1,), (1,)), ((), ())), preferred_element_type=F32)
            raw = jnp.where(lane < limits[p], raw, NEG)
            top = jnp.max(raw, axis=1, keepdims=True)
            weights = jnp.exp2((raw - top) * power)
            total = jnp.sum(weights, axis=1, keepdims=True)
            out = jnp.dot(weights.astype(BF16), page, preferred_element_type=F32)
            peak = jnp.maximum(top * scale, NEG)
            for i in range(BLOCK):
                slot = lax.shift_right_logical(codes[i], 11)
                for t in range(4):
                    first = i * tokens + t * share
                    wide[t, pl.ds(pl.multiple_of(slot * share, share), share), :] = out[first : first + share]
                here = lanes == (slot & (LANES - 1))
                at = lax.shift_right_logical(slot, 7)
                rows = slice(i * tokens, (i + 1) * tokens)
                stats[0, at] = jnp.where(here, peak[rows], stats[0, at])
                stats[1, at] = jnp.where(here, total[rows], stats[1, at])
        return 0

    lax.fori_loop(0, (block_count[chunk] + UNROLL - 1) // UNROLL, step, 0)

    rep = me[1]
    length = outs[0].shape[0] - 2 * PIECES * 2 * share
    piece = 128
    for p in range(4):
        t = (rep + p) & 3
        for h in range(2):
            out = outs[p * 2 + h]

            def narrow(i, _):
                at = pl.multiple_of(i * piece, piece)
                out[pl.ds(at, piece), :] = wide[t, pl.ds(at + h * STRIDE * share, piece), :].astype(BF16)
                return 0

            lax.fori_loop(0, length // piece, narrow, 0)
            for s in range(2):
                rows = pl.ds(pl.multiple_of(t * share, share), share)
                both = jnp.concatenate([stats[s, h * 2, rows, :], stats[s, h * 2 + 1, rows, :]], axis=0)
                for k, x in enumerate(split(both)):
                    at = length + (s * PIECES + k) * 2 * share
                    out[at : at + 2 * share, :] = x


def merge_kernel(last, root, share, *refs):
    ins = refs[:4]
    outs = refs[4:]
    length = ins[0].shape[0] - 2 * PIECES * 2 * share
    for h in range(2):
        came, own = ins[2 * h], ins[2 * h + 1]

        def joined(ref, s):
            at = length + s * PIECES * 2 * share
            tiles = [ref[at + k * 2 * share : at + (k + 1) * 2 * share, :].astype(F32) for k in range(PIECES)]
            return tiles[0] + (tiles[1] + tiles[2])

        peak_a, total_a, peak_b, total_b = joined(came, 0), joined(came, 1), joined(own, 0), joined(own, 1)
        peak = jnp.maximum(peak_a, peak_b)
        part_a, part_b = jnp.exp(peak_a - peak), jnp.exp(peak_b - peak)
        total = total_a * part_a + total_b * part_b
        if last:
            part_a, part_b = part_a / (total * root), part_b / (total * root)
            logs = TAU * (peak + jnp.log(total))
            for k in range(2):
                row = jnp.sum(logs[k * share : (k + 1) * share], axis=0, keepdims=True)
                outs[1][2 * h + k : 2 * h + k + 1, :] = row
            out, base = outs[0], h * length
        else:
            out, base = outs[h], 0
            for s, x in enumerate((peak, total)):
                for k, tile in enumerate(split(x)):
                    at = length + (s * PIECES + k) * 2 * share
                    out[at : at + 2 * share, :] = tile
        for pair in range(length // (2 * share)):
            at = pair * 2 * share

            def factor(x):
                columns = []
                for slot in (2 * pair, 2 * pair + 1):
                    k, n = slot // LANES, slot % LANES
                    columns.append(jnp.broadcast_to(x[k * share : (k + 1) * share, n : n + 1], (share, LANES)))
                return jnp.concatenate(columns, axis=0)

            rows = slice(at, at + 2 * share)
            value = came[rows, :].astype(F32) * factor(part_a) + own[rows, :].astype(F32) * factor(part_b)
            out[base + at : base + at + 2 * share, :] = value.astype(BF16)


def gradient_kernel(share, list_len, place, weight, first, second, out, wide):
    length = first.shape[0]
    for h, x in enumerate((first, second)):

        def widen(i, _):
            at = pl.multiple_of(i * 128, 128)
            wide[pl.ds(h * length + at, 128), :] = x[pl.ds(at, 128), :].astype(F32)
            return 0

        lax.fori_loop(0, length // 128, widen, 0)

    def step(i, _):
        parts = []
        for s in range(2):
            total = jnp.zeros((share, out.shape[1]), F32)
            for k in range(list_len):
                e = (i * 2 + s) * list_len + k
                at = pl.multiple_of(place[e] * share, share)
                total = total + weight[e] * wide[pl.ds(at, share), :]
            parts.append(total)
        out[pl.ds(pl.multiple_of(i * 2 * share, 2 * share), 2 * share), :] = jnp.concatenate(parts, axis=0).astype(BF16)
        return 0

    lax.fori_loop(0, out.shape[0] // share // 2, step, 0)


def ints(*shape):
    return jax.ShapeDtypeStruct(shape, jnp.int32)


def per_device(queries, listed, page_slot, counts, page_store):
    groups = lax.axis_size("index")
    index = lax.axis_index("index").astype(jnp.int32)
    rep = lax.axis_index("rep").astype(jnp.int32)
    reps = lax.axis_size("rep")
    query_count, query_len, feature = queries.shape
    list_len = listed.shape[1]
    pages, part, _ = page_store.shape
    page_bits = pages.bit_length() - 1
    pairs = query_count * list_len
    capacity = 2 * pairs // groups
    sub = capacity // CHUNKS
    slots = groups * capacity
    half = query_count // 2
    share = query_len // reps
    blocks = (groups * sub + (BLOCK - 1) * pages) // BLOCK
    blocks = (blocks + UNROLL - 1) // UNROLL * UNROLL
    me = jnp.stack([index, rep])
    root = math.sqrt(feature)
    scale = 1.0 / (root * TAU)

    table, place = pl.pallas_call(
        functools.partial(route_kernel, capacity, page_bits, list_len),
        out_shape=(ints(slots), ints(pairs)),
        in_specs=[SMEM, SMEM],
        out_specs=(SMEM, SMEM),
        scratch_shapes=[pltpu.SMEM((groups,), jnp.int32)],
        name="route",
    )(listed.reshape(pairs), page_slot)
    arrived = lax.all_to_all(table.reshape(groups, capacity), "index", split_axis=0, concat_axis=0, tiled=True)

    pieces = gather_queries(queries, index % 2)

    order, block_page, block_count = pl.pallas_call(
        functools.partial(sort_kernel, capacity, page_bits, half, blocks),
        out_shape=(ints(CHUNKS * blocks * BLOCK + slots), ints(CHUNKS * blocks), ints(CHUNKS)),
        in_specs=[SMEM, SMEM],
        out_specs=(SMEM,) * 3,
        scratch_shapes=[pltpu.SMEM((CHUNKS * pages + 1,), jnp.int32)] * 2,
        cost_estimate=pl.CostEstimate(flops=0, bytes_accessed=40_000_000, transcendentals=0),
        name="sort_pairs",
    )(arrived.reshape(slots), me)

    limits = counts - rep * part
    flat = [x.reshape((-1,) + x.shape[-2:]) for x, _ in pieces]
    places = [at * half for _, at in pieces]

    length = groups // 2 * sub * share
    packed = length + 2 * PIECES * 2 * share

    def rep_pairs(step):
        return [(i, (i + step) % reps) for i in range(reps)]

    def travel(x, step):
        return lax.ppermute(x, "rep", rep_pairs(step))

    returned, scores = [], []
    for chunk in range(CHUNKS):
        parts = pl.pallas_call(
            functools.partial(pair_kernel, chunk, blocks, places, scale),
            out_shape=(jax.ShapeDtypeStruct((packed, feature), BF16),) * 8,
            in_specs=[SMEM] * 5 + [ANY] * (1 + len(flat)),
            out_specs=(VMEM,) * 8,
            scratch_shapes=[
                pltpu.VMEM((groups * query_count, query_len, feature), BF16),
                pltpu.VMEM((pages, part, feature), BF16),
                pltpu.VMEM((4, 2 * STRIDE * share, feature), F32),
                pltpu.VMEM((2, 2 * STRIDE // LANES, query_len, LANES), F32),
                pltpu.SemaphoreType.DMA((len(flat) + 1,)),
            ],
            compiler_params=params(48),
            cost_estimate=pl.CostEstimate(flops=0, bytes_accessed=60_000_000, transcendentals=0),
            name="pairs",
        )(order, block_page, block_count, limits, me, page_store, *flat)

        held = [parts[3 * 2], parts[1 * 2 + 1]]
        for hop in range(3):
            came = [travel(held[0], 1), travel(held[1], -1)]
            own = [parts[(2, 1, 0)[hop] * 2], parts[(2, 3, 0)[hop] * 2 + 1]]
            last = hop == 2
            if last:
                out_shape = (jax.ShapeDtypeStruct((2 * length, feature), BF16), jax.ShapeDtypeStruct((4, LANES), F32))
            else:
                out_shape = (jax.ShapeDtypeStruct((packed, feature), BF16),) * 2
            held = pl.pallas_call(
                functools.partial(merge_kernel, last, root, share),
                out_shape=out_shape,
                in_specs=[VMEM] * 4,
                out_specs=(VMEM,) * 2,
                compiler_params=params(24),
                cost_estimate=pl.CostEstimate(flops=0, bytes_accessed=8_000_000, transcendentals=0),
                name="merge",
            )(came[0], own[0], came[1], own[1])
        directions, logs = held
        returned.append(
            lax.all_to_all(directions.reshape(groups, sub * share, feature), "index", split_axis=0, concat_axis=0, tiled=True)
        )
        logs = logs + travel(logs, 1) + travel(logs, -1) + travel(logs, 2)
        logs = logs.reshape(2, STRIDE)[:, : groups // 2 * sub].reshape(groups, sub)
        scores.append(lax.all_to_all(logs, "index", split_axis=0, concat_axis=0, tiled=True))

    pair_scores = jnp.stack(scores).reshape(slots)[place].reshape(query_count, list_len)
    highest = jnp.max(pair_scores, axis=1, keepdims=True)
    log_total = highest[:, 0] + jnp.log(jnp.sum(jnp.exp(pair_scores - highest), axis=1))
    losses = log_total - pair_scores[:, 0]
    probability = jnp.exp(pair_scores - log_total[:, None])
    target = (jnp.arange(list_len) == 0).astype(F32)
    coefficient = LOSS_SCALE * (probability - target[None, :])

    quarter = pl.pallas_call(
        functools.partial(gradient_kernel, share, list_len),
        out_shape=jax.ShapeDtypeStruct((query_count * share, feature), BF16),
        in_specs=[SMEM, SMEM, VMEM, VMEM],
        out_specs=VMEM,
        scratch_shapes=[pltpu.VMEM((slots * share, feature), F32)],
        compiler_params=params(32),
        name="gradients",
    )(place, coefficient.reshape(pairs), *[x.reshape(-1, feature) for x in returned])
    gathered = lax.all_gather(quarter.reshape(query_count, share, feature), "rep")
    gradients = jnp.transpose(gathered, (1, 0, 2, 3)).reshape(query_count, query_len, feature)
    return (losses, gradients)


def solution(mesh):
    return jax.shard_map(
        per_device,
        mesh=mesh,
        in_specs=(
            P("index", None, None),
            P("index", None),
            P(),
            P("index"),
            P("index", "rep", None),
        ),
        out_specs=(P("index"), P("index", None, None)),
        check_vma=False,
    )
```

time: 716 us -> 267 us (0.37)
  waiting for transfers between devices: 270 us -> 89.1 us
  local copies, waits for them, and re-layouts: 197 us -> 16.3 us
  matrix products: 121 us -> 0 us
  Pallas kernels: 0 us -> 65 us
  other arithmetic: 45.1 us -> 2.26 us
  starting transfers between devices: 28.6 us -> 70.6 us
  between operations: 14.3 us -> 1.1 us
  blocking collectives: 33.8 us -> 23.5 us
    gather x100 -> x1, local copies, waits for them, and re-layouts: 186 us -> 1.89 us  [per_device(): jnp.stack(scores).reshape(slots)[place].reshape(query_count, list_len)]
    dot_general x96 -> x0, matrix products: 121 us -> none  [the longest x48 69.7 us: part_stats(): jnp.einsum('btw,bpw->btp', block_tokens, picked, preferred_element_type=j...]
    psum x1 -> x0, waiting for transfers between devices: 120 us -> none  [per_device(): summed = lax.psum(terms.astype(jnp.bfloat16), 'rep').astype(jnp.float32)]
    all_to_all x4, waiting for transfers between devices: 150 us -> 39.5 us  [the longest x2 25.7 us: per_device(): lax.all_to_all(directions.reshape(groups, sub * share, feature), 'index',...]
    pallas_call x0 -> x11, Pallas kernels: none -> 65 us  [the longest x2 34.7 us: per_device(): pl.pallas_call(functools.partial(pair_kernel, chunk, blocks, places, scal...]
    ppermute x0 -> x41, starting transfers between devices: none -> 52.1 us  [the longest x18 29.1 us: travel(): return lax.ppermute(x, 'rep', rep_pairs(step))]
    ppermute x0 -> x41, waiting for transfers between devices: none -> 49.7 us  [the longest x3 21.1 us: spread(): right = lax.ppermute(x, 'index', ring_pairs(second, 1))]
    all_gather x2 -> x1, blocking collectives: 33.8 us -> 12.8 us  [per_device(): lax.all_gather(quarter.reshape(query_count, share, feature), 'rep')]
  transfers between devices with their start and end apart: 5 -> 45, of which waited for: 3 -> 13; matrix products, arithmetic and copies ran while one was open for 3% -> 4% of each run, Pallas kernels for 0% -> 17%
where the time goes in v2:
time: 267 us; the launch traced here: 268 us
  waiting for transfers between devices  89.1 us (33%)
  starting transfers between devices  70.6 us (26%)
  Pallas kernels  65 us (24%)
  blocking collectives  23.5 us (9%)
  local copies, waits for them, and re-layouts  16.3 us (6%)
    pallas_call x2, Pallas kernels, per_device(): pl.pallas_call(functools.partial(pair_kernel, chunk, blocks, places, scal...  34.7 us
    ppermute x18, starting transfers between devices, travel(): return lax.ppermute(x, 'rep', rep_pairs(step))  29.1 us
    all_to_all x2, waiting for transfers between devices, per_device(): lax.all_to_all(directions.reshape(groups, sub * share, feature), 'index',...  25.7 us
    ppermute x3, waiting for transfers between devices, spread(): right = lax.ppermute(x, 'index', ring_pairs(second, 1))  21.1 us
    ppermute x18, waiting for transfers between devices, travel(): return lax.ppermute(x, 'rep', rep_pairs(step))  14.2 us
    pallas_call x1, Pallas kernels, per_device(): pl.pallas_call(functools.partial(sort_kernel, capacity, page_bits, half,...  13.6 us
    ppermute x3, waiting for transfers between devices, spread(): far_a = lax.ppermute(right[:n], 'index', ring_pairs(second, 1))  12.9 us
    all_gather x1, blocking collectives, per_device(): lax.all_gather(quarter.reshape(query_count, share, feature), 'rep')  12.8 us
  transfers between devices with their start and end apart: 45, of which 13 were waited for; matrix products, arithmetic and copies ran while one was open for 4% of the time, Pallas kernels for 17%

profile of v2, /device:TPU:0, one launch (start us, length us, event | category | flops | bytes accessed | tf_op | source)
XLA Modules:
  0.0 267.8 jit_solution(2941886053090187254)
XLA Ops:
  0.7 1.1 dynamic-slice_bitcast_fusion
  1.8 1.4 collective-permute-done
  3.3 1.7 collective-permute-start.5
  5.0 1.6 collective-permute-start.6
  6.6 5.8 %collective-permute-done.5 = bf16[2,24,32,128]{3,2,1,0:T(8,128)(2,1)S(1)} collective-permute-done((bf16[2,24,32,128]{3,2,1,0:T(8,128)(2,1)S(1)}, bf16[2,24,32,128]{3,2,1,0:T(8,128)(2,1)S(1)}, u32[]{:S(2)}, u32[]{:S(2)}) %collective-permute-start.5) | collective-permute-done | bytes 393248 | tf_op jit(solution)/shard_map/ppermute | solution.py:66
  12.9 2.9 %collective-permute-start.8 = (bf16[1,24,32,128]{3,2,1,0:T(8,128)(2,1)S(1)}, bf16[1,24,32,128]{3,2,1,0:T(8,128)(2,1)S(1)}, u32[]{:S(2)}, u32[]{:S(2)}) collective-permute-start(bf16[1,24,32,128]{3,2,1,0:T(8,128)(2,1)S(1)} %slice.41), channel_id=1, source_target_pairs={{0,24},{4,100},{8,0},{12,108},{16,8},{20,116},{24,16},{28,124},{32... | collective-permute-start | bytes 589832 | tf_op jit(solution)/shard_map/ppermute | solution.py:69
  15.8 0.8 constant_dynamic-update-slice_fusion.3
  16.5 0.8 constant_dynamic-update-slice_fusion.2
  17.3 2.0 collective-permute-done.7
  19.3 0.7 constant_dynamic-update-slice_fusion.1
  20.0 0.7 constant_dynamic-update-slice_fusion
  20.7 2.0 collective-permute-start.9
  22.7 2.1 collective-permute-start.10
  24.8 3.2 %collective-permute-start.2 = (bf16[2,24,32,128]{3,2,1,0:T(8,128)(2,1)S(1)}, bf16[2,24,32,128]{3,2,1,0:T(8,128)(2,1)S(1)}, u32[]{:S(2)}, u32[]{:S(2)}) collective-permute-start(bf16[2,24,32,128]{3,2,1,0:T(8,128)(2,1)S(1)} %maximum_select_fusion), channel_id=1, source_target_pairs={{0,96},{4,28},{8,104},{12,4},{16,112},{20,12},{24,120},{28,20},{32... | collective-permute-start | bytes 1179656 | tf_op jit(solution)/shard_map/ppermute | solution.py:67
  28.0 15.4 %collective-permute-done.1 = bf16[2,24,32,128]{3,2,1,0:T(8,128)(2,1)S(1)} collective-permute-done((bf16[2,24,32,128]{3,2,1,0:T(8,128)(2,1)S(1)}, bf16[2,24,32,128]{3,2,1,0:T(8,128)(2,1)S(1)}, u32[]{:S(2)}, u32[]{:S(2)}) %collective-permute-start.1) | collective-permute-done | bytes 393248 | tf_op jit(solution)/shard_map/ppermute | solution.py:66
  43.6 3.3 %collective-permute-start.4 = (bf16[1,24,32,128]{3,2,1,0:T(8,128)(2,1)S(1)}, bf16[1,24,32,128]{3,2,1,0:T(8,128)(2,1)S(1)}, u32[]{:S(2)}, u32[]{:S(2)}) collective-permute-start(bf16[1,24,32,128]{3,2,1,0:T(8,128)(2,1)S(1)} %slice.39), channel_id=1, source_target_pairs={{0,96},{4,28},{8,104},{12,4},{16,112},{20,12},{24,120},{28,20},{32... | collective-permute-start | bytes 589832 | tf_op jit(solution)/shard_map/ppermute | solution.py:69
  46.8 3.5 %collective-permute-done.3 = bf16[1,24,32,128]{3,2,1,0:T(8,128)(2,1)S(1)} collective-permute-done((bf16[1,24,32,128]{3,2,1,0:T(8,128)(2,1)S(1)}, bf16[1,24,32,128]{3,2,1,0:T(8,128)(2,1)S(1)}, u32[]{:S(2)}, u32[]{:S(2)}) %collective-permute-start.3) | collective-permute-done | bytes 196640 | tf_op jit(solution)/shard_map/ppermute | solution.py:68
  51.4 1.1 slice.42
  52.5 1.1 slice.43
  54.4 2.7 %collective-permute-start.12 = (bf16[3,24,32,128]{3,2,1,0:T(8,128)(2,1)S(1)}, bf16[3,24,32,128]{3,2,1,0:T(8,128)(2,1)}, u32[]{:S(2)}, u32[]{:S(2)}) collective-permute-start(bf16[3,24,32,128]{3,2,1,0:T(8,128)(2,1)S(1)} %slice.43), channel_id=1, source_target_pairs={{0,96},{4,28},{8,104},{12,4},{16,112},{20,12},{24,120},{28,20},{32... | collective-permute-start | bytes 1769480 | tf_op jit(solution)/shard_map/ppermute | solution.py:69
  57.7 7.4 %collective-permute-done.11 = bf16[3,24,32,128]{3,2,1,0:T(8,128)(2,1)} collective-permute-done((bf16[3,24,32,128]{3,2,1,0:T(8,128)(2,1)S(1)}, bf16[3,24,32,128]{3,2,1,0:T(8,128)(2,1)}, u32[]{:S(2)}, u32[]{:S(2)}) %collective-permute-start.11) | collective-permute-done | bytes 589856 | tf_op jit(solution)/shard_map/ppermute | solution.py:68
  65.6 0.7 reshape.129.listed
  66.3 5.0 %route.1 = (s32[768]{0:T(1024)}, s32[384]{0:T(512)}) custom-call(s32[384]{0:T(512)} %reshape.129.listed, s32[2048]{0:T(1024)} %page_slot.1), custom_call_target="tpu_custom_call" | custom-call | tf_op jit(solution)/shard_map/route/pallas_call | solution.py:377
  71.3 1.4 all_to_all.24
  72.7 6.8 %all-to-all-start = ((s32[32,1,24]{2,1,0:T(1,128)}), s32[32,1,24]{2,1,0:T(1,128)S(1)}, u32[]{:S(2)}, u32[]{:S(2)}) async-start(s32[32,1,24]{2,1,0:T(1,128)} %bitcast), calls=%async_computation | async-start | bytes 32768 | tf_op jit(solution)/shard_map/all_to_all | solution.py:385
  80.2 6.6 %all-to-all-done = s32[32,1,24]{2,1,0:T(1,128)S(1)} async-done(((s32[32,1,24]{2,1,0:T(1,128)}), s32[32,1,24]{2,1,0:T(1,128)S(1)}, u32[]{:S(2)}, u32[]{:S(2)}) %all-to-all-start) | async-done | bytes 3104 | tf_op jit(solution)/shard_map/all_to_all | solution.py:385
  87.3 0.7 reduce.5
  88.7 13.6 %sort_pairs.1 = (s32[1920]{0:T(1024)}, s32[288]{0:T(512)}, s32[2]{0:T(128)}) custom-call(s32[768]{0:T(1024)} %reshape.130.arrived, s32[2]{0:T(128)} %pad_add_fusion.me), custom_call_target="tpu_custom_call" | custom-call | bytes 40000000 | tf_op jit(solution)/shard_map/sort_pairs/pallas_call | solution.py:389
  102.4 0.7 copy-done.2
  105.1 17.3 %pairs.2 = (bf16[1632,128]{1,0:T(8,128)(2,1)S(1)}, bf16[1632,128]{1,0:T(8,128)(2,1)S(1)}, bf16[1632,128]{1,0:T(8,128)(2,1)S(1)}, bf16[1632,128]{1,0:T(8,128)(2,1...) custom-call(s32[1920]{0:T(1024)S(1)} %copy-done.2, ...), custom_call_target="tpu_custom_call" | custom-call | bytes 60000000 | tf_op jit(solution)/shard_map/pairs/pallas_call | solution.py:414
  122.4 1.6 collective-permute-start.23
  124.0 1.7 collective-permute-start.24
  125.7 17.4 %pairs.3 = (bf16[1632,128]{1,0:T(8,128)(2,1)S(1)}, bf16[1632,128]{1,0:T(8,128)(2,1)S(1)}, bf16[1632,128]{1,0:T(8,128)(2,1)S(1)}, bf16[1632,128]{1,0:T(8,128)(2,1...) custom-call(s32[1920]{0:T(1024)S(1)} %copy-done.2, ...), custom_call_target="tpu_custom_call" | custom-call | bytes 60000000 | tf_op jit(solution)/shard_map/pairs/pallas_call | solution.py:414
  143.5 3.0 %collective-permute-start.33 = (bf16[1632,128]{1,0:T(8,128)(2,1)S(1)}, bf16[1632,128]{1,0:T(8,128)(2,1)S(1)}, u32[]{:S(2)}, u32[]{:S(2)}) collective-permute-start(bf16[1632,128]{1,0:T(8,128)(2,1)S(1)} %get-tuple-element.54), channel_id=1, source_target_pairs={{0,3},{1,0},{2,1},{3,2},{4,7},{5,4},{6,5},{7,6},{8,11},{9,8},{10,9... | collective-permute-start | bytes 1253384 | tf_op jit(solution)/shard_map/ppermute | solution.py:410
  146.4 1.4 merge.6
  147.9 3.2 %collective-permute-start.26 = (bf16[1632,128]{1,0:T(8,128)(2,1)S(1)}, bf16[1632,128]{1,0:T(8,128)(2,1)S(1)}, u32[]{:S(2)}, u32[]{:S(2)}) collective-permute-start(bf16[1632,128]{1,0:T(8,128)(2,1)S(1)} %get-tuple-element.45), channel_id=1, source_target_pairs={{0,3},{1,0},{2,1},{3,2},{4,7},{5,4},{6,5},{7,6},{8,11},{9,8},{10,9... | collective-permute-start | bytes 1253384 | tf_op jit(solution)/shard_map/ppermute | solution.py:410
  151.1 5.8 %collective-permute-done.32.refs_0_ = bf16[1632,128]{1,0:T(8,128)(2,1)S(1)} collective-permute-done((bf16[1632,128]{1,0:T(8,128)(2,1)S(1)}, bf16[1632,128]{1,0:T(8,128)(2,1)S(1)}, u32[]{:S(2)}, u32[]{:S(2)}) %collective-permute-start.32) | collective-permute-done | bytes 417824 | tf_op jit(solution)/shard_map/ppermute | solution.py:410
  156.9 1.4 merge.9
  158.4 3.2 %collective-permute-start.35 = (bf16[1632,128]{1,0:T(8,128)(2,1)S(1)}, bf16[1632,128]{1,0:T(8,128)(2,1)S(1)}, u32[]{:S(2)}, u32[]{:S(2)}) collective-permute-start(bf16[1632,128]{1,0:T(8,128)(2,1)S(1)} %get-tuple-element.58), channel_id=1, source_target_pairs={{0,3},{1,0},{2,1},{3,2},{4,7},{5,4},{6,5},{7,6},{8,11},{9,8},{10,9... | collective-permute-start | bytes 1253384 | tf_op jit(solution)/shard_map/ppermute | solution.py:410
  161.7 4.2 %collective-permute-done.25.refs_0_ = bf16[1632,128]{1,0:T(8,128)(2,1)S(1)} collective-permute-done((bf16[1632,128]{1,0:T(8,128)(2,1)S(1)}, bf16[1632,128]{1,0:T(8,128)(2,1)S(1)}, u32[]{:S(2)}, u32[]{:S(2)}) %collective-permute-start.25) | collective-permute-done | bytes 417824 | tf_op jit(solution)/shard_map/ppermute | solution.py:410
  165.9 1.4 merge.7
  167.4 3.2 %collective-permute-start.28 = (bf16[1632,128]{1,0:T(8,128)(2,1)S(1)}, bf16[1632,128]{1,0:T(8,128)(2,1)S(1)}, u32[]{:S(2)}, u32[]{:S(2)}) collective-permute-start(bf16[1632,128]{1,0:T(8,128)(2,1)S(1)} %get-tuple-element.49), channel_id=1, source_target_pairs={{0,3},{1,0},{2,1},{3,2},{4,7},{5,4},{6,5},{7,6},{8,11},{9,8},{10,9... | collective-permute-start | bytes 1253384 | tf_op jit(solution)/shard_map/ppermute | solution.py:410
  170.6 4.2 %collective-permute-done.34.refs_0_ = bf16[1632,128]{1,0:T(8,128)(2,1)S(1)} collective-permute-done((bf16[1632,128]{1,0:T(8,128)(2,1)S(1)}, bf16[1632,128]{1,0:T(8,128)(2,1)S(1)}, u32[]{:S(2)}, u32[]{:S(2)}) %collective-permute-start.34) | collective-permute-done | bytes 417824 | tf_op jit(solution)/shard_map/ppermute | solution.py:410
  174.8 1.4 merge.10
  176.3 3.1 %collective-permute-start.37 = (bf16[1632,128]{1,0:T(8,128)(2,1)S(1)}, bf16[1632,128]{1,0:T(8,128)(2,1)S(1)}, u32[]{:S(2)}, u32[]{:S(2)}) collective-permute-start(bf16[1632,128]{1,0:T(8,128)(2,1)S(1)} %get-tuple-element.62), channel_id=1, source_target_pairs={{0,3},{1,0},{2,1},{3,2},{4,7},{5,4},{6,5},{7,6},{8,11},{9,8},{10,9... | collective-permute-start | bytes 1253384 | tf_op jit(solution)/shard_map/ppermute | solution.py:410
  179.5 2.2 merge.8
  182.1 2.8 %collective-permute-start.30 = (f32[4,128]{1,0:T(4,128)S(1)}, f32[4,128]{1,0:T(4,128)S(1)}, u32[]{:S(2)}, u32[]{:S(2)}) collective-permute-start(f32[4,128]{1,0:T(4,128)S(1)} %get-tuple-element.51), channel_id=1, source_target_pairs={{0,3},{1,0},{2,1},{3,2},{4,7},{5,4},{6,5},{7,6},{8,11},{9,8},{10,9... | collective-permute-start | bytes 6152 | tf_op jit(solution)/shard_map/ppermute | solution.py:410
  184.9 1.1 collective-permute-start.31
  186.0 2.3 merge.11
  188.3 1.4 collective-permute-start.38
  189.7 1.8 collective-permute-start.39
  191.6 1.6 collective-permute-start.40
  193.1 0.7 all_to_all.26
  193.8 3.8 %all-to-all-start.1 = ((f32[32,1,12]{2,1,0:T(1,128)}), f32[32,1,12]{2,1,0:T(1,128)S(1)}, u32[]{:S(2)}, u32[]{:S(2)}) async-start(f32[32,1,12]{2,1,0:T(1,128)} %bitcast.25), calls=%async_computation.1 | async-start | bytes 32768 | tf_op jit(solution)/shard_map/all_to_all | solution.py:455
  197.8 7.1 %all-to-all-done.1 = f32[32,1,12]{2,1,0:T(1,128)S(1)} async-done(((f32[32,1,12]{2,1,0:T(1,128)}), f32[32,1,12]{2,1,0:T(1,128)S(1)}, u32[]{:S(2)}, u32[]{:S(2)}) %all-to-all-start.1) | async-done | bytes 1568 | tf_op jit(solution)/shard_map/all_to_all | solution.py:455
  205.0 10.6 %all_to_all.37 = f32[32,1,12]{2,1,0:T(1,128)S(1)} all-to-all(f32[32,1,12]{2,1,0:T(1,128)S(1)} %bitcast.67), channel_id=1, replica_groups=mesh['index'=32,'rep'=4] {'index'}, dimensions={0} | all-to-all | bytes 3072 | tf_op jit(solution)/shard_map/all_to_all | solution.py:455
  215.6 3.9 %all-to-all-start.3 = ((bf16[32,96,128]{2,1,0:T(8,128)(2,1)}), bf16[32,96,128]{2,1,0:T(8,128)(2,1)S(1)}, u32[]{:S(2)}, u32[]{:S(2)}) async-start(bf16[32,96,128]{2,1,0:T(8,128)(2,1)} %bitcast.29), calls=%async_computation.3 | async-start | bytes 1572864 | tf_op jit(solution)/shard_map/all_to_all | solution.py:451
  219.7 14.4 %all-to-all-done.3 = bf16[32,96,128]{2,1,0:T(8,128)(2,1)S(1)} async-done(((bf16[32,96,128]{2,1,0:T(8,128)(2,1)}), bf16[32,96,128]{2,1,0:T(8,128)(2,1)S(1)}, u32[]{:S(2)}, u32[]{:S(2)}) %all-to-all-start.3) | async-done | bytes 786464 | tf_op jit(solution)/shard_map/all_to_all | solution.py:451
  234.1 3.9 %all-to-all-start.4 = ((bf16[32,96,128]{2,1,0:T(8,128)(2,1)}), bf16[32,96,128]{2,1,0:T(8,128)(2,1)S(1)}, u32[]{:S(2)}, u32[]{:S(2)}) async-start(bf16[32,96,128]{2,1,0:T(8,128)(2,1)} %bitcast.31), calls=%async_computation.4 | async-start | bytes 1572864 | tf_op jit(solution)/shard_map/all_to_all | solution.py:451
  238.1 1.9 gather_fusion
  241.2 11.3 %all-to-all-done.4 = bf16[32,96,128]{2,1,0:T(8,128)(2,1)S(1)} async-done(((bf16[32,96,128]{2,1,0:T(8,128)(2,1)}), bf16[32,96,128]{2,1,0:T(8,128)(2,1)S(1)}, u32[]{:S(2)}, u32[]{:S(2)}) %all-to-all-start.4) | async-done | bytes 786464 | tf_op jit(solution)/shard_map/all_to_all | solution.py:451
  252.6 1.6 gradients.1
  254.2 12.8 %all_gather.3 = bf16[4,48,8,128]{3,2,1,0:T(8,128)(2,1)S(1)} all-gather(bf16[1,48,8,128]{3,2,1,0:T(8,128)(2,1)S(1)} %bitcast.64), channel_id=1, replica_groups=mesh['index'=32,'rep'=4] {'rep'}, dimensions={0}, use_global_device_ids=true | all-gather | bytes 491520 | tf_op jit(solution)/shard_map/all_gather | solution.py:474
  267.0 0.8 copy.33
  (102 shorter events, 10.6 us)
Async XLA Ops:
  1.7 1.5 collective-permute-start
  3.3 9.1 %collective-permute-start.5 = (bf16[2,24,32,128]{3,2,1,0:T(8,128)(2,1)S(1)}, bf16[2,24,32,128]{3,2,1,0:T(8,128)(2,1)S(1)}, u32[]{:S(2)}, u32[]{:S(2)}) collective-permute-start(bf16[2,24,32,128]{3,2,1,0:T(8,128)(2,1)S(1)} %maximum_select_fusion), channel_id=1, source_target_pairs={{0,8},{4,36},{8,16},{12,44},{16,24},{20,52},{24,0},{28,60},{32,40}... | collective-permute-start | bytes 1179656 | tf_op jit(solution)/shard_map/ppermute | solution.py:66
  5.0 7.9 %collective-permute-start.6 = (bf16[2,24,32,128]{3,2,1,0:T(8,128)(2,1)S(1)}, bf16[2,24,32,128]{3,2,1,0:T(8,128)(2,1)S(1)}, u32[]{:S(2)}, u32[]{:S(2)}) collective-permute-start(bf16[2,24,32,128]{3,2,1,0:T(8,128)(2,1)S(1)} %maximum_select_fusion), channel_id=1, source_target_pairs={{0,24},{4,100},{8,0},{12,108},{16,8},{20,116},{24,16},{28,124},{32... | collective-permute-start | bytes 1179656 | tf_op jit(solution)/shard_map/ppermute | solution.py:67
  12.4 6.9 %collective-permute-start.7 = (bf16[1,24,32,128]{3,2,1,0:T(8,128)(2,1)S(1)}, bf16[1,24,32,128]{3,2,1,0:T(8,128)(2,1)S(1)}, u32[]{:S(2)}, u32[]{:S(2)}) collective-permute-start(bf16[1,24,32,128]{3,2,1,0:T(8,128)(2,1)S(1)} %slice.40), channel_id=1, source_target_pairs={{0,8},{4,36},{8,16},{12,44},{16,24},{20,52},{24,0},{28,60},{32,40}... | collective-permute-start | bytes 589832 | tf_op jit(solution)/shard_map/ppermute | solution.py:68
  12.9 7.1 %collective-permute-start.8 = (bf16[1,24,32,128]{3,2,1,0:T(8,128)(2,1)S(1)}, bf16[1,24,32,128]{3,2,1,0:T(8,128)(2,1)S(1)}, u32[]{:S(2)}, u32[]{:S(2)}) collective-permute-start(bf16[1,24,32,128]{3,2,1,0:T(8,128)(2,1)S(1)} %slice.41), channel_id=1, source_target_pairs={{0,24},{4,100},{8,0},{12,108},{16,8},{20,116},{24,16},{28,124},{32... | collective-permute-start | bytes 589832 | tf_op jit(solution)/shard_map/ppermute | solution.py:69
  20.7 30.2 %collective-permute-start.9 = (bf16[6,24,32,128]{3,2,1,0:T(8,128)(2,1)}, bf16[6,24,32,128]{3,2,1,0:T(8,128)(2,1)}, u32[]{:S(2)}, u32[]{:S(2)}) collective-permute-start(bf16[6,24,32,128]{3,2,1,0:T(8,128)(2,1)} %constant_dynamic-update-slice_fusion), channel_id=1, source_target_pairs={{0,32},{4,12},{8,40},{12,20},{16,48},{20,28},{24,56},{28,4},{32,64... | collective-permute-start | bytes 3538952 | tf_op jit(solution)/shard_map/ppermute | solution.py:66
  22.7 28.3 %collective-permute-start.10 = (bf16[6,24,32,128]{3,2,1,0:T(8,128)(2,1)}, bf16[6,24,32,128]{3,2,1,0:T(8,128)(2,1)}, u32[]{:S(2)}, u32[]{:S(2)}) collective-permute-start(bf16[6,24,32,128]{3,2,1,0:T(8,128)(2,1)} %constant_dynamic-update-slice_fusion), channel_id=1, source_target_pairs={{0,96},{4,28},{8,104},{12,4},{16,112},{20,12},{24,120},{28,20},{32... | collective-permute-start | bytes 3538952 | tf_op jit(solution)/shard_map/ppermute | solution.py:67
  24.8 18.6 %collective-permute-start.1 = (bf16[2,24,32,128]{3,2,1,0:T(8,128)(2,1)S(1)}, bf16[2,24,32,128]{3,2,1,0:T(8,128)(2,1)S(1)}, u32[]{:S(2)}, u32[]{:S(2)}) collective-permute-start(bf16[2,24,32,128]{3,2,1,0:T(8,128)(2,1)S(1)} %maximum_select_fusion), channel_id=1, source_target_pairs={{0,32},{4,12},{8,40},{12,20},{16,48},{20,28},{24,56},{28,4},{32,64... | collective-permute-start | bytes 1179656 | tf_op jit(solution)/shard_map/ppermute | solution.py:66
  24.8 18.7 %collective-permute-start.2 = (bf16[2,24,32,128]{3,2,1,0:T(8,128)(2,1)S(1)}, bf16[2,24,32,128]{3,2,1,0:T(8,128)(2,1)S(1)}, u32[]{:S(2)}, u32[]{:S(2)}) collective-permute-start(bf16[2,24,32,128]{3,2,1,0:T(8,128)(2,1)S(1)} %maximum_select_fusion), channel_id=1, source_target_pairs={{0,96},{4,28},{8,104},{12,4},{16,112},{20,12},{24,120},{28,20},{32... | collective-permute-start | bytes 1179656 | tf_op jit(solution)/shard_map/ppermute | solution.py:67
  43.4 7.0 %collective-permute-start.3 = (bf16[1,24,32,128]{3,2,1,0:T(8,128)(2,1)S(1)}, bf16[1,24,32,128]{3,2,1,0:T(8,128)(2,1)S(1)}, u32[]{:S(2)}, u32[]{:S(2)}) collective-permute-start(bf16[1,24,32,128]{3,2,1,0:T(8,128)(2,1)S(1)} %slice.38), channel_id=1, source_target_pairs={{0,32},{4,12},{8,40},{12,20},{16,48},{20,28},{24,56},{28,4},{32,64... | collective-permute-start | bytes 589832 | tf_op jit(solution)/shard_map/ppermute | solution.py:68
  43.5 22.0 %copy-start.8 = (s32[48,8]{0,1:T(8,128)S(1)}, s32[48,8]{0,1:T(8,128)}, u32[]{:S(2)}) copy-start(s32[48,8]{0,1:T(8,128)} %param.6) | copy-start | bytes 4612
  43.6 36.0 %copy-start.9 = (s32[64]{0:T(128)S(1)}, s32[64]{0:T(128)}, u32[]{:S(2)}) copy-start(s32[64]{0:T(128)} %param.8) | copy-start | bytes 772
  43.6 6.8 %collective-permute-start.4 = (bf16[1,24,32,128]{3,2,1,0:T(8,128)(2,1)S(1)}, bf16[1,24,32,128]{3,2,1,0:T(8,128)(2,1)S(1)}, u32[]{:S(2)}, u32[]{:S(2)}) collective-permute-start(bf16[1,24,32,128]{3,2,1,0:T(8,128)(2,1)S(1)} %slice.39), channel_id=1, source_target_pairs={{0,96},{4,28},{8,104},{12,4},{16,112},{20,12},{24,120},{28,20},{32... | collective-permute-start | bytes 589832 | tf_op jit(solution)/shard_map/ppermute | solution.py:69
  46.8 6.8 %collective-permute-start.13 = (bf16[2,24,32,128]{3,2,1,0:T(8,128)(2,1)S(1)}, bf16[2,24,32,128]{3,2,1,0:T(8,128)(2,1)S(1)}, u32[]{:S(2)}, u32[]{:S(2)}) collective-permute-start(bf16[2,24,32,128]{3,2,1,0:T(8,128)(2,1)S(1)} %maximum_select_fusion), channel_id=1, source_target_pairs={{0,4},{4,0},{8,12},{12,8},{16,20},{20,16},{24,28},{28,24},{32,36},... | collective-permute-start | bytes 1179656 | tf_op jit(solution)/shard_map/ppermute | solution.py:54
  50.4 6.8 %collective-permute-start.14 = (bf16[2,24,32,128]{3,2,1,0:T(8,128)(2,1)S(1)}, bf16[2,24,32,128]{3,2,1,0:T(8,128)(2,1)S(1)}, u32[]{:S(2)}, u32[]{:S(2)}) collective-permute-start(bf16[2,24,32,128]{3,2,1,0:T(8,128)(2,1)S(1)} %collective-permute-done.1), channel_id=1, source_target_pairs={{0,4},{4,0},{8,12},{12,8},{16,20},{20,16},{24,28},{28,24},{32,36},... | collective-permute-start | bytes 1179656 | tf_op jit(solution)/shard_map/ppermute | solution.py:54
  50.4 6.8 %collective-permute-start.15 = (bf16[2,24,32,128]{3,2,1,0:T(8,128)(2,1)S(1)}, bf16[2,24,32,128]{3,2,1,0:T(8,128)(2,1)S(1)}, u32[]{:S(2)}, u32[]{:S(2)}) collective-permute-start(bf16[2,24,32,128]{3,2,1,0:T(8,128)(2,1)S(1)} %collective-permute-done.2), channel_id=1, source_target_pairs={{0,4},{4,0},{8,12},{12,8},{16,20},{20,16},{24,28},{28,24},{32,36},... | collective-permute-start | bytes 1179656 | tf_op jit(solution)/shard_map/ppermute | solution.py:54
  50.9 2.9 %collective-permute-start.16 = (bf16[1,24,32,128]{3,2,1,0:T(8,128)(2,1)S(1)}, bf16[1,24,32,128]{3,2,1,0:T(8,128)(2,1)S(1)}, u32[]{:S(2)}, u32[]{:S(2)}) collective-permute-start(bf16[1,24,32,128]{3,2,1,0:T(8,128)(2,1)S(1)} %collective-permute-done.3), channel_id=1, source_target_pairs={{0,4},{4,0},{8,12},{12,8},{16,20},{20,16},{24,28},{28,24},{32,36},... | collective-permute-start | bytes 589832 | tf_op jit(solution)/shard_map/ppermute | solution.py:54
  51.0 3.5 %collective-permute-start.17 = (bf16[1,24,32,128]{3,2,1,0:T(8,128)(2,1)S(1)}, bf16[1,24,32,128]{3,2,1,0:T(8,128)(2,1)S(1)}, u32[]{:S(2)}, u32[]{:S(2)}) collective-permute-start(bf16[1,24,32,128]{3,2,1,0:T(8,128)(2,1)S(1)} %collective-permute-done.4), channel_id=1, source_target_pairs={{0,4},{4,0},{8,12},{12,8},{16,20},{20,16},{24,28},{28,24},{32,36},... | collective-permute-start | bytes 589832 | tf_op jit(solution)/shard_map/ppermute | solution.py:54
  53.6 48.7 %collective-permute-start.18 = (bf16[6,24,32,128]{3,2,1,0:T(8,128)(2,1)}, bf16[6,24,32,128]{3,2,1,0:T(8,128)(2,1)}, u32[]{:S(2)}, u32[]{:S(2)}) collective-permute-start(bf16[6,24,32,128]{3,2,1,0:T(8,128)(2,1)} %constant_dynamic-update-slice_fusion), channel_id=1, source_target_pairs={{0,4},{4,0},{8,12},{12,8},{16,20},{20,16},{24,28},{28,24},{32,36},... | collective-permute-start | bytes 3538952 | tf_op jit(solution)/shard_map/ppermute | solution.py:54
  53.8 11.2 %collective-permute-start.11 = (bf16[3,24,32,128]{3,2,1,0:T(8,128)(2,1)S(1)}, bf16[3,24,32,128]{3,2,1,0:T(8,128)(2,1)}, u32[]{:S(2)}, u32[]{:S(2)}) collective-permute-start(bf16[3,24,32,128]{3,2,1,0:T(8,128)(2,1)S(1)} %slice.42), channel_id=1, source_target_pairs={{0,32},{4,12},{8,40},{12,20},{16,48},{20,28},{24,56},{28,4},{32,64... | collective-permute-start | bytes 1769480 | tf_op jit(solution)/shard_map/ppermute | solution.py:68
  54.4 10.6 %collective-permute-start.12 = (bf16[3,24,32,128]{3,2,1,0:T(8,128)(2,1)S(1)}, bf16[3,24,32,128]{3,2,1,0:T(8,128)(2,1)}, u32[]{:S(2)}, u32[]{:S(2)}) collective-permute-start(bf16[3,24,32,128]{3,2,1,0:T(8,128)(2,1)S(1)} %slice.43), channel_id=1, source_target_pairs={{0,96},{4,28},{8,104},{12,4},{16,112},{20,12},{24,120},{28,20},{32... | collective-permute-start | bytes 1769480 | tf_op jit(solution)/shard_map/ppermute | solution.py:69
  57.1 45.2 %collective-permute-start.19 = (bf16[6,24,32,128]{3,2,1,0:T(8,128)(2,1)}, bf16[6,24,32,128]{3,2,1,0:T(8,128)(2,1)}, u32[]{:S(2)}, u32[]{:S(2)}) collective-permute-start(bf16[6,24,32,128]{3,2,1,0:T(8,128)(2,1)} %collective-permute-done.9), channel_id=1, source_target_pairs={{0,4},{4,0},{8,12},{12,8},{16,20},{20,16},{24,28},{28,24},{32,36},... | collective-permute-start | bytes 3538952 | tf_op jit(solution)/shard_map/ppermute | solution.py:54
  57.1 45.2 %collective-permute-start.20 = (bf16[6,24,32,128]{3,2,1,0:T(8,128)(2,1)}, bf16[6,24,32,128]{3,2,1,0:T(8,128)(2,1)}, u32[]{:S(2)}, u32[]{:S(2)}) collective-permute-start(bf16[6,24,32,128]{3,2,1,0:T(8,128)(2,1)} %collective-permute-done.10), channel_id=1, source_target_pairs={{0,4},{4,0},{8,12},{12,8},{16,20},{20,16},{24,28},{28,24},{32,36},... | collective-permute-start | bytes 3538952 | tf_op jit(solution)/shard_map/ppermute | solution.py:54
  65.0 37.3 %collective-permute-start.21 = (bf16[3,24,32,128]{3,2,1,0:T(8,128)(2,1)}, bf16[3,24,32,128]{3,2,1,0:T(8,128)(2,1)}, u32[]{:S(2)}, u32[]{:S(2)}) collective-permute-start(bf16[3,24,32,128]{3,2,1,0:T(8,128)(2,1)} %collective-permute-done.11), channel_id=1, source_target_pairs={{0,4},{4,0},{8,12},{12,8},{16,20},{20,16},{24,28},{28,24},{32,36},... | collective-permute-start | bytes 1769480 | tf_op jit(solution)/shard_map/ppermute | solution.py:54
  65.0 37.3 %collective-permute-start.22 = (bf16[3,24,32,128]{3,2,1,0:T(8,128)(2,1)}, bf16[3,24,32,128]{3,2,1,0:T(8,128)(2,1)}, u32[]{:S(2)}, u32[]{:S(2)}) collective-permute-start(bf16[3,24,32,128]{3,2,1,0:T(8,128)(2,1)} %collective-permute-done.12), channel_id=1, source_target_pairs={{0,4},{4,0},{8,12},{12,8},{16,20},{20,16},{24,28},{28,24},{32,36},... | collective-permute-start | bytes 1769480 | tf_op jit(solution)/shard_map/ppermute | solution.py:54
  72.7 14.1 %all-to-all-start = ((s32[32,1,24]{2,1,0:T(1,128)}), s32[32,1,24]{2,1,0:T(1,128)S(1)}, u32[]{:S(2)}, u32[]{:S(2)}) async-start(s32[32,1,24]{2,1,0:T(1,128)} %bitcast), calls=%async_computation | async-start | bytes 32768 | tf_op jit(solution)/shard_map/all_to_all | solution.py:385
  102.4 0.7 copy-start.2
  103.1 0.7 copy-start.3
  103.7 0.7 copy-start.5
  104.4 0.7 copy-start.6
  105.1 20.7 %copy-start.7 = (s32[2]{0:T(128)S(1)}, s32[2]{0:T(128)}, u32[]{:S(2)}) copy-start(s32[2]{0:T(128)} %get-tuple-element.38.block_count) | copy-start | bytes 28
  122.4 24.0 %collective-permute-start.23 = (bf16[1632,128]{1,0:T(8,128)(2,1)S(1)}, bf16[1632,128]{1,0:T(8,128)(2,1)S(1)}, u32[]{:S(2)}, u32[]{:S(2)}) collective-permute-start(bf16[1632,128]{1,0:T(8,128)(2,1)S(1)} %get-tuple-element.39), channel_id=1, source_target_pairs={{0,1},{1,2},{2,3},{3,0},{4,5},{5,6},{6,7},{7,4},{8,9},{9,10},{10,1... | collective-permute-start | bytes 1253384 | tf_op jit(solution)/shard_map/ppermute | solution.py:410
  124.0 22.4 %collective-permute-start.24 = (bf16[1632,128]{1,0:T(8,128)(2,1)S(1)}, bf16[1632,128]{1,0:T(8,128)(2,1)S(1)}, u32[]{:S(2)}, u32[]{:S(2)}) collective-permute-start(bf16[1632,128]{1,0:T(8,128)(2,1)S(1)} %get-tuple-element.41), channel_id=1, source_target_pairs={{0,3},{1,0},{2,1},{3,2},{4,7},{5,4},{6,5},{7,6},{8,11},{9,8},{10,9... | collective-permute-start | bytes 1253384 | tf_op jit(solution)/shard_map/ppermute | solution.py:410
  143.1 13.8 %collective-permute-start.32 = (bf16[1632,128]{1,0:T(8,128)(2,1)S(1)}, bf16[1632,128]{1,0:T(8,128)(2,1)S(1)}, u32[]{:S(2)}, u32[]{:S(2)}) collective-permute-start(bf16[1632,128]{1,0:T(8,128)(2,1)S(1)} %get-tuple-element.52), channel_id=1, source_target_pairs={{0,1},{1,2},{2,3},{3,0},{4,5},{5,6},{6,7},{7,4},{8,9},{9,10},{10,1... | collective-permute-start | bytes 1253384 | tf_op jit(solution)/shard_map/ppermute | solution.py:410
  143.5 13.4 %collective-permute-start.33 = (bf16[1632,128]{1,0:T(8,128)(2,1)S(1)}, bf16[1632,128]{1,0:T(8,128)(2,1)S(1)}, u32[]{:S(2)}, u32[]{:S(2)}) collective-permute-start(bf16[1632,128]{1,0:T(8,128)(2,1)S(1)} %get-tuple-element.54), channel_id=1, source_target_pairs={{0,3},{1,0},{2,1},{3,2},{4,7},{5,4},{6,5},{7,6},{8,11},{9,8},{10,9... | collective-permute-start | bytes 1253384 | tf_op jit(solution)/shard_map/ppermute | solution.py:410
  147.8 18.1 %copy-start.1 = (bf16[1632,128]{1,0:T(8,128)(2,1)S(1)}, bf16[1632,128]{1,0:T(8,128)(2,1)}, u32[]{:S(2)}) copy-start(bf16[1632,128]{1,0:T(8,128)(2,1)} %get-tuple-element.46.refs_3_) | copy-start | bytes 1253380
  147.8 18.1 %collective-permute-start.25 = (bf16[1632,128]{1,0:T(8,128)(2,1)S(1)}, bf16[1632,128]{1,0:T(8,128)(2,1)S(1)}, u32[]{:S(2)}, u32[]{:S(2)}) collective-permute-start(bf16[1632,128]{1,0:T(8,128)(2,1)S(1)} %get-tuple-element.43), channel_id=1, source_target_pairs={{0,1},{1,2},{2,3},{3,0},{4,5},{5,6},{6,7},{7,4},{8,9},{9,10},{10,1... | collective-permute-start | bytes 1253384 | tf_op jit(solution)/shard_map/ppermute | solution.py:410
  147.9 18.0 %collective-permute-start.26 = (bf16[1632,128]{1,0:T(8,128)(2,1)S(1)}, bf16[1632,128]{1,0:T(8,128)(2,1)S(1)}, u32[]{:S(2)}, u32[]{:S(2)}) collective-permute-start(bf16[1632,128]{1,0:T(8,128)(2,1)S(1)} %get-tuple-element.45), channel_id=1, source_target_pairs={{0,3},{1,0},{2,1},{3,2},{4,7},{5,4},{6,5},{7,6},{8,11},{9,8},{10,9... | collective-permute-start | bytes 1253384 | tf_op jit(solution)/shard_map/ppermute | solution.py:410
  158.3 16.5 %copy-start = (bf16[1632,128]{1,0:T(8,128)(2,1)S(1)}, bf16[1632,128]{1,0:T(8,128)(2,1)}, u32[]{:S(2)}) copy-start(bf16[1632,128]{1,0:T(8,128)(2,1)} %get-tuple-element.59.refs_3_) | copy-start | bytes 1253380
  158.3 16.5 %collective-permute-start.34 = (bf16[1632,128]{1,0:T(8,128)(2,1)S(1)}, bf16[1632,128]{1,0:T(8,128)(2,1)S(1)}, u32[]{:S(2)}, u32[]{:S(2)}) collective-permute-start(bf16[1632,128]{1,0:T(8,128)(2,1)S(1)} %get-tuple-element.56), channel_id=1, source_target_pairs={{0,1},{1,2},{2,3},{3,0},{4,5},{5,6},{6,7},{7,4},{8,9},{9,10},{10,1... | collective-permute-start | bytes 1253384 | tf_op jit(solution)/shard_map/ppermute | solution.py:410
  158.4 16.3 %collective-permute-start.35 = (bf16[1632,128]{1,0:T(8,128)(2,1)S(1)}, bf16[1632,128]{1,0:T(8,128)(2,1)S(1)}, u32[]{:S(2)}, u32[]{:S(2)}) collective-permute-start(bf16[1632,128]{1,0:T(8,128)(2,1)S(1)} %get-tuple-element.58), channel_id=1, source_target_pairs={{0,3},{1,0},{2,1},{3,2},{4,7},{5,4},{6,5},{7,6},{8,11},{9,8},{10,9... | collective-permute-start | bytes 1253384 | tf_op jit(solution)/shard_map/ppermute | solution.py:410
  167.2 12.2 %collective-permute-start.27 = (bf16[1632,128]{1,0:T(8,128)(2,1)S(1)}, bf16[1632,128]{1,0:T(8,128)(2,1)S(1)}, u32[]{:S(2)}, u32[]{:S(2)}) collective-permute-start(bf16[1632,128]{1,0:T(8,128)(2,1)S(1)} %get-tuple-element.47), channel_id=1, source_target_pairs={{0,1},{1,2},{2,3},{3,0},{4,5},{5,6},{6,7},{7,4},{8,9},{9,10},{10,1... | collective-permute-start | bytes 1253384 | tf_op jit(solution)/shard_map/ppermute | solution.py:410
  167.4 12.1 %collective-permute-start.28 = (bf16[1632,128]{1,0:T(8,128)(2,1)S(1)}, bf16[1632,128]{1,0:T(8,128)(2,1)S(1)}, u32[]{:S(2)}, u32[]{:S(2)}) collective-permute-start(bf16[1632,128]{1,0:T(8,128)(2,1)S(1)} %get-tuple-element.49), channel_id=1, source_target_pairs={{0,3},{1,0},{2,1},{3,2},{4,7},{5,4},{6,5},{7,6},{8,11},{9,8},{10,9... | collective-permute-start | bytes 1253384 | tf_op jit(solution)/shard_map/ppermute | solution.py:410
  176.1 9.9 %collective-permute-start.36 = (bf16[1632,128]{1,0:T(8,128)(2,1)S(1)}, bf16[1632,128]{1,0:T(8,128)(2,1)S(1)}, u32[]{:S(2)}, u32[]{:S(2)}) collective-permute-start(bf16[1632,128]{1,0:T(8,128)(2,1)S(1)} %get-tuple-element.60), channel_id=1, source_target_pairs={{0,1},{1,2},{2,3},{3,0},{4,5},{5,6},{6,7},{7,4},{8,9},{9,10},{10,1... | collective-permute-start | bytes 1253384 | tf_op jit(solution)/shard_map/ppermute | solution.py:410
  176.3 9.7 %collective-permute-start.37 = (bf16[1632,128]{1,0:T(8,128)(2,1)S(1)}, bf16[1632,128]{1,0:T(8,128)(2,1)S(1)}, u32[]{:S(2)}, u32[]{:S(2)}) collective-permute-start(bf16[1632,128]{1,0:T(8,128)(2,1)S(1)} %get-tuple-element.62), channel_id=1, source_target_pairs={{0,3},{1,0},{2,1},{3,2},{4,7},{5,4},{6,5},{7,6},{8,11},{9,8},{10,9... | collective-permute-start | bytes 1253384 | tf_op jit(solution)/shard_map/ppermute | solution.py:410
  181.7 9.9 %collective-permute-start.29 = (f32[4,128]{1,0:T(4,128)S(1)}, f32[4,128]{1,0:T(4,128)S(1)}, u32[]{:S(2)}, u32[]{:S(2)}) collective-permute-start(f32[4,128]{1,0:T(4,128)S(1)} %get-tuple-element.51), channel_id=1, source_target_pairs={{0,1},{1,2},{2,3},{3,0},{4,5},{5,6},{6,7},{7,4},{8,9},{9,10},{10,1... | collective-permute-start | bytes 6152 | tf_op jit(solution)/shard_map/ppermute | solution.py:410
  182.1 11.0 %collective-permute-start.30 = (f32[4,128]{1,0:T(4,128)S(1)}, f32[4,128]{1,0:T(4,128)S(1)}, u32[]{:S(2)}, u32[]{:S(2)}) collective-permute-start(f32[4,128]{1,0:T(4,128)S(1)} %get-tuple-element.51), channel_id=1, source_target_pairs={{0,3},{1,0},{2,1},{3,2},{4,7},{5,4},{6,5},{7,6},{8,11},{9,8},{10,9... | collective-permute-start | bytes 6152 | tf_op jit(solution)/shard_map/ppermute | solution.py:410
  184.9 8.2 %collective-permute-start.31 = (f32[4,128]{1,0:T(4,128)S(1)}, f32[4,128]{1,0:T(4,128)S(1)}, u32[]{:S(2)}, u32[]{:S(2)}) collective-permute-start(f32[4,128]{1,0:T(4,128)S(1)} %get-tuple-element.51), channel_id=1, source_target_pairs={{0,2},{1,3},{2,0},{3,1},{4,6},{5,7},{6,4},{7,5},{8,10},{9,11},{10,... | collective-permute-start | bytes 6152 | tf_op jit(solution)/shard_map/ppermute | solution.py:410
  188.3 31.3 %copy-start.4 = (s32[384]{0:T(512)S(1)}, s32[384]{0:T(512)}, u32[]{:S(2)}) copy-start(s32[384]{0:T(512)} %get-tuple-element.65.place) | copy-start | bytes 4612
  188.3 9.4 %collective-permute-start.38 = (f32[4,128]{1,0:T(4,128)S(1)}, f32[4,128]{1,0:T(4,128)S(1)}, u32[]{:S(2)}, u32[]{:S(2)}) collective-permute-start(f32[4,128]{1,0:T(4,128)S(1)} %get-tuple-element.64), channel_id=1, source_target_pairs={{0,1},{1,2},{2,3},{3,0},{4,5},{5,6},{6,7},{7,4},{8,9},{9,10},{10,1... | collective-permute-start | bytes 6152 | tf_op jit(solution)/shard_map/ppermute | solution.py:410
  189.7 8.0 %collective-permute-start.39 = (f32[4,128]{1,0:T(4,128)S(1)}, f32[4,128]{1,0:T(4,128)S(1)}, u32[]{:S(2)}, u32[]{:S(2)}) collective-permute-start(f32[4,128]{1,0:T(4,128)S(1)} %get-tuple-element.64), channel_id=1, source_target_pairs={{0,3},{1,0},{2,1},{3,2},{4,7},{5,4},{6,5},{7,6},{8,11},{9,8},{10,9... | collective-permute-start | bytes 6152 | tf_op jit(solution)/shard_map/ppermute | solution.py:410
  191.6 6.1 %collective-permute-start.40 = (f32[4,128]{1,0:T(4,128)S(1)}, f32[4,128]{1,0:T(4,128)S(1)}, u32[]{:S(2)}, u32[]{:S(2)}) collective-permute-start(f32[4,128]{1,0:T(4,128)S(1)} %get-tuple-element.64), channel_id=1, source_target_pairs={{0,2},{1,3},{2,0},{3,1},{4,6},{5,7},{6,4},{7,5},{8,10},{9,11},{10,... | collective-permute-start | bytes 6152 | tf_op jit(solution)/shard_map/ppermute | solution.py:410
  193.8 11.1 %all-to-all-start.1 = ((f32[32,1,12]{2,1,0:T(1,128)}), f32[32,1,12]{2,1,0:T(1,128)S(1)}, u32[]{:S(2)}, u32[]{:S(2)}) async-start(f32[32,1,12]{2,1,0:T(1,128)} %bitcast.25), calls=%async_computation.1 | async-start | bytes 32768 | tf_op jit(solution)/shard_map/all_to_all | solution.py:455
  215.6 18.5 %all-to-all-start.3 = ((bf16[32,96,128]{2,1,0:T(8,128)(2,1)}), bf16[32,96,128]{2,1,0:T(8,128)(2,1)S(1)}, u32[]{:S(2)}, u32[]{:S(2)}) async-start(bf16[32,96,128]{2,1,0:T(8,128)(2,1)} %bitcast.29), calls=%async_computation.3 | async-start | bytes 1572864 | tf_op jit(solution)/shard_map/all_to_all | solution.py:451
  234.1 18.5 %all-to-all-start.4 = ((bf16[32,96,128]{2,1,0:T(8,128)(2,1)}), bf16[32,96,128]{2,1,0:T(8,128)(2,1)S(1)}, u32[]{:S(2)}, u32[]{:S(2)}) async-start(bf16[32,96,128]{2,1,0:T(8,128)(2,1)} %bitcast.31), calls=%async_computation.4 | async-start | bytes 1572864 | tf_op jit(solution)/shard_map/all_to_all | solution.py:451

commit v3 on v2

v3 whole, which is shorter than its diff:
```python
import functools
import math

import jax
import jax.numpy as jnp
from jax import lax
from jax.experimental import pallas as pl
from jax.experimental.pallas import tpu as pltpu
from jax.sharding import PartitionSpec as P

TAU = 0.1
LOSS_SCALE = 32.0
NEG = -1e30
BLOCK = 4
UNROLL = 16
CHUNKS = 2
LANES = 128
STRIDE = 256
PIECES = 3
F32 = jnp.float32
BF16 = jnp.bfloat16

SMEM = pl.BlockSpec(memory_space=pltpu.SMEM)
VMEM = pl.BlockSpec(memory_space=pltpu.VMEM)
ANY = pl.BlockSpec(memory_space=pl.ANY)


def params(mib):
    return pltpu.CompilerParams(vmem_limit_bytes=mib * 1024 * 1024)


def route_kernel(capacity, page_bits, list_len, listed, page_slot, table, place, tile, used):
    slots = table.shape[0]
    pairs = listed.shape[0]
    groups = used.shape[0]
    sub = capacity // CHUNKS

    def clear(i, _):
        for k in range(16):
            table[i * 16 + k] = -1
        return 0

    lax.fori_loop(0, slots // 16, clear, 0)
    for i in range(groups):
        used[i] = 0

    def step(q, _):
        for k in range(list_len):
            i = q * list_len + k
            row = page_slot[listed[i]]
            owner = lax.shift_right_logical(row, page_bits)
            n = jnp.minimum(used[owner], capacity - 1)
            used[owner] = n + 1
            chunk = n & 1
            j = lax.shift_right_logical(n, 1)
            table[owner * capacity + chunk * sub + j] = lax.shift_left(q, page_bits) + (row & ((1 << page_bits) - 1))
            place[i] = owner * capacity + chunk * sub + j
            tile[i] = owner * (capacity + 2) + chunk * sub + j
        return 0

    lax.fori_loop(0, pairs // list_len, step, 0)


def sort_kernel(capacity, page_bits, query_count, blocks, arrived, order, block_page, block_count, count, first):
    slots = arrived.shape[0]
    groups = slots // capacity
    sub = capacity // CHUNKS
    pages = 1 << page_bits
    nothing = (groups // 2) * sub * 2048

    def clear(i, _):
        for k in range(16):
            order[i * 16 + k] = nothing
        return 0

    lax.fori_loop(0, CHUNKS * blocks * BLOCK // 16, clear, 0)

    def clear_blocks(i, _):
        for k in range(16):
            block_page[i * 16 + k] = 0
        return 0

    lax.fori_loop(0, CHUNKS * blocks // 16, clear_blocks, 0)
    for i in range(CHUNKS * pages + 1):
        count[i] = 0

    def tally(s, _):
        for chunk in range(CHUNKS):
            for j in range(sub):
                code = arrived[s * capacity + chunk * sub + j]
                p = jnp.where(code < 0, CHUNKS * pages, (code & (pages - 1)) + chunk * pages)
                count[p] = count[p] + 1
        return 0

    lax.fori_loop(0, groups, tally, 0)

    for chunk in range(CHUNKS):

        def lay(p, b):
            n = count[chunk * pages + p]
            first[chunk * pages + p] = b * BLOCK
            count[chunk * pages + p] = 0
            steps = lax.shift_right_logical(n + BLOCK - 1, 2)

            def one(k, _):
                block_page[b + k] = p
                return 0

            lax.fori_loop(0, steps, one, 0)
            return b + steps

        total = lax.fori_loop(0, pages, lay, jnp.int32(chunk * blocks))
        block_count[chunk] = total - chunk * blocks
    first[CHUNKS * pages] = CHUNKS * blocks * BLOCK
    count[CHUNKS * pages] = 0

    def source(s, _):
        side = lax.shift_right_logical(s, 4)
        slot = side * STRIDE + (s & 15) * sub
        base = s * query_count + slot * 2048
        for chunk in range(CHUNKS):
            for j in range(sub):
                code = arrived[s * capacity + chunk * sub + j]
                p = jnp.where(code < 0, CHUNKS * pages, (code & (pages - 1)) + chunk * pages)
                q = lax.shift_right_logical(jnp.maximum(code, 0), page_bits)
                r = count[p]
                count[p] = r + 1
                order[first[p] + r] = q + base + j * 2048
        return 0

    lax.fori_loop(0, groups, source, 0)


def split(x):
    parts = []
    for _ in range(PIECES):
        part = x.astype(BF16)
        parts.append(part)
        x = x - part.astype(F32)
    return parts


def pair_kernel(chunk, blocks, scale, order, block_page, block_count, limits, me, *refs):
    store, queries = refs[:2]
    outs = refs[2:10]
    held, pages, wide, stats, sems = refs[10:]
    copies = [pltpu.make_async_copy(queries, held, sems.at[0]), pltpu.make_async_copy(store, pages, sems.at[1])]
    for c in copies:
        c.start()
    for c in copies:
        c.wait()
    part = pages.shape[1]
    tokens = held.shape[1]
    share = tokens // 4
    power = scale * math.log2(math.e)
    lane = lax.broadcasted_iota(jnp.int32, (1, part), 1)
    lanes = lax.broadcasted_iota(jnp.int32, (tokens, LANES), 1)

    def step(it, _):
        for u in range(UNROLL):
            b = chunk * blocks + it * UNROLL + u
            p = block_page[b]
            codes = [order[b * BLOCK + i] for i in range(BLOCK)]
            block = jnp.concatenate([held[c & 2047] for c in codes], axis=0)
            page = pages[p]
            raw = lax.dot_general(block, page, (((1,), (1,)), ((), ())), preferred_element_type=F32)
            raw = jnp.where(lane < limits[p], raw, NEG)
            top = jnp.max(raw, axis=1, keepdims=True)
            weights = jnp.exp2((raw - top) * power)
            total = jnp.sum(weights, axis=1, keepdims=True)
            out = jnp.dot(weights.astype(BF16), page, preferred_element_type=F32)
            peak = jnp.maximum(top * scale, NEG)
            for i in range(BLOCK):
                slot = lax.shift_right_logical(codes[i], 11)
                for t in range(4):
                    first = i * tokens + t * share
                    wide[t, pl.ds(pl.multiple_of(slot * share, share), share), :] = out[first : first + share]
                here = lanes == (slot & (LANES - 1))
                at = lax.shift_right_logical(slot, 7)
                rows = slice(i * tokens, (i + 1) * tokens)
                stats[0, at] = jnp.where(here, peak[rows], stats[0, at])
                stats[1, at] = jnp.where(here, total[rows], stats[1, at])
        return 0

    lax.fori_loop(0, (block_count[chunk] + UNROLL - 1) // UNROLL, step, 0)

    rep = me[0]
    length = outs[0].shape[0] - 2 * PIECES * 2 * share
    piece = 128
    for p in range(4):
        t = (rep + p) & 3
        for h in range(2):
            out = outs[p * 2 + h]

            def narrow(i, _):
                at = pl.multiple_of(i * piece, piece)
                out[pl.ds(at, piece), :] = wide[t, pl.ds(at + h * STRIDE * share, piece), :].astype(BF16)
                return 0

            lax.fori_loop(0, length // piece, narrow, 0)
            for s in range(2):
                rows = pl.ds(pl.multiple_of(t * share, share), share)
                both = jnp.concatenate([stats[s, h * 2, rows, :], stats[s, h * 2 + 1, rows, :]], axis=0)
                for k, x in enumerate(split(both)):
                    at = length + (s * PIECES + k) * 2 * share
                    out[at : at + 2 * share, :] = x


def merge_kernel(last, root, share, sub, *refs):
    n_in = 4 * CHUNKS if last else 4
    ins = refs[:n_in]
    outs = refs[n_in:]
    length = ins[0].shape[0] - 2 * PIECES * 2 * share
    span = 2 * sub * share + 2 * share
    for n in range(n_in // 2):
        chunk, h = n // 2, n % 2
        came, own = ins[2 * n], ins[2 * n + 1]

        def joined(ref, s):
            at = length + s * PIECES * 2 * share
            tiles = [ref[at + k * 2 * share : at + (k + 1) * 2 * share, :].astype(F32) for k in range(PIECES)]
            return tiles[0] + (tiles[1] + tiles[2])

        peak_a, total_a, peak_b, total_b = joined(came, 0), joined(came, 1), joined(own, 0), joined(own, 1)
        peak = jnp.maximum(peak_a, peak_b)
        part_a, part_b = jnp.exp(peak_a - peak), jnp.exp(peak_b - peak)
        total = total_a * part_a + total_b * part_b
        if last:
            part_a, part_b = part_a / (total * root), part_b / (total * root)
            logs = TAU * (peak + jnp.log(total))
            rows = [jnp.sum(logs[k * share : (k + 1) * share], axis=0, keepdims=True) for k in range(2)]
            if chunk == 0:
                kept = {**(kept if h else {}), h: rows}
            else:
                both = jnp.concatenate(kept[h] + rows, axis=0)
                tile = jnp.concatenate([x.astype(F32) for x in split(both)] + [both * 0.0], axis=0).astype(BF16)
                sources = length // (sub * share)
                for source in range(sources):
                    at = (h * sources + source) * span + 2 * sub * share
                    outs[0][at : at + 2 * share, :] = tile
        else:
            for s, x in enumerate((peak, total)):
                for k, tile in enumerate(split(x)):
                    at = length + (s * PIECES + k) * 2 * share
                    outs[h][at : at + 2 * share, :] = tile
        for pair in range(length // (2 * share)):
            at = pair * 2 * share

            def factor(x):
                columns = []
                for slot in (2 * pair, 2 * pair + 1):
                    k, lane = slot // LANES, slot % LANES
                    columns.append(jnp.broadcast_to(x[k * share : (k + 1) * share, lane : lane + 1], (share, LANES)))
                return jnp.concatenate(columns, axis=0)

            rows = slice(at, at + 2 * share)
            value = came[rows, :].astype(F32) * factor(part_a) + own[rows, :].astype(F32) * factor(part_b)
            if last:
                source, j = 2 * pair // sub, 2 * pair % sub
                to = (h * (length // (sub * share)) + source) * span + (chunk * sub + j) * share
                outs[0][to : to + 2 * share, :] = value.astype(BF16)
            else:
                outs[h][rows, :] = value.astype(BF16)


def gradient_kernel(share, list_len, place, weight, directions, out, wide):
    def widen(i, _):
        at = pl.multiple_of(i * 128, 128)
        wide[pl.ds(at, 128), :] = directions[pl.ds(at, 128), :].astype(F32)
        return 0

    lax.fori_loop(0, directions.shape[0] // 128, widen, 0)

    def step(i, _):
        parts = []
        for s in range(2):
            total = jnp.zeros((share, out.shape[1]), F32)
            for k in range(list_len):
                e = (i * 2 + s) * list_len + k
                at = pl.multiple_of(place[e] * share, share)
                total = total + weight[e] * wide[pl.ds(at, share), :]
            parts.append(total)
        out[pl.ds(pl.multiple_of(i * 2 * share, 2 * share), 2 * share), :] = jnp.concatenate(parts, axis=0).astype(BF16)
        return 0

    lax.fori_loop(0, out.shape[0] // share // 2, step, 0)


def ints(*shape):
    return jax.ShapeDtypeStruct(shape, jnp.int32)


def per_device(queries, listed, page_slot, counts, page_store):
    groups = lax.axis_size("index")
    index = lax.axis_index("index").astype(jnp.int32)
    rep = lax.axis_index("rep").astype(jnp.int32)
    reps = lax.axis_size("rep")
    query_count, query_len, feature = queries.shape
    list_len = listed.shape[1]
    pages, part, _ = page_store.shape
    page_bits = pages.bit_length() - 1
    pairs = query_count * list_len
    capacity = 2 * pairs // groups
    sub = capacity // CHUNKS
    slots = groups * capacity
    share = query_len // reps
    blocks = (groups * sub + (BLOCK - 1) * pages) // BLOCK
    blocks = (blocks + UNROLL - 1) // UNROLL * UNROLL
    root = math.sqrt(feature)
    scale = 1.0 / (root * TAU)

    table, place, tile = pl.pallas_call(
        functools.partial(route_kernel, capacity, page_bits, list_len),
        out_shape=(ints(slots), ints(pairs), ints(pairs)),
        in_specs=[SMEM, SMEM],
        out_specs=(SMEM,) * 3,
        scratch_shapes=[pltpu.SMEM((groups,), jnp.int32)],
        name="route",
    )(listed.reshape(pairs), page_slot)
    arrived = lax.all_to_all(table.reshape(groups, capacity), "index", split_axis=0, concat_axis=0, tiled=True)

    everyone = lax.all_gather(queries, "index", tiled=True)

    order, block_page, block_count = pl.pallas_call(
        functools.partial(sort_kernel, capacity, page_bits, query_count, blocks),
        out_shape=(ints(CHUNKS * blocks * BLOCK + slots), ints(CHUNKS * blocks), ints(CHUNKS)),
        in_specs=[SMEM],
        out_specs=(SMEM,) * 3,
        scratch_shapes=[pltpu.SMEM((CHUNKS * pages + 1,), jnp.int32)] * 2,
        cost_estimate=pl.CostEstimate(flops=0, bytes_accessed=40_000_000, transcendentals=0),
        name="sort_pairs",
    )(arrived.reshape(slots))

    limits = counts - rep * part
    me = rep[None]

    length = groups // 2 * sub * share
    packed = length + 2 * PIECES * 2 * share

    def rep_pairs(step):
        return [(i, (i + step) % reps) for i in range(reps)]

    def travel(x, step):
        return lax.ppermute(x, "rep", rep_pairs(step))

    finals = []
    for chunk in range(CHUNKS):
        parts = pl.pallas_call(
            functools.partial(pair_kernel, chunk, blocks, scale),
            out_shape=(jax.ShapeDtypeStruct((packed, feature), BF16),) * 8,
            in_specs=[SMEM] * 5 + [ANY] * 2,
            out_specs=(VMEM,) * 8,
            scratch_shapes=[
                pltpu.VMEM((groups * query_count, query_len, feature), BF16),
                pltpu.VMEM((pages, part, feature), BF16),
                pltpu.VMEM((4, 2 * STRIDE * share, feature), F32),
                pltpu.VMEM((2, 2 * STRIDE // LANES, query_len, LANES), F32),
                pltpu.SemaphoreType.DMA((2,)),
            ],
            compiler_params=params(48),
            cost_estimate=pl.CostEstimate(flops=0, bytes_accessed=60_000_000, transcendentals=0),
            name="pairs",
        )(order, block_page, block_count, limits, me, page_store, everyone)

        held = [parts[3 * 2], parts[1 * 2 + 1]]
        for hop in range(3):
            came = [travel(held[0], 1), travel(held[1], -1)]
            own = [parts[(2, 1, 0)[hop] * 2], parts[(2, 3, 0)[hop] * 2 + 1]]
            if hop == 2:
                finals += [came[0], own[0], came[1], own[1]]
                break
            held = pl.pallas_call(
                functools.partial(merge_kernel, False, root, share, sub),
                out_shape=(jax.ShapeDtypeStruct((packed, feature), BF16),) * 2,
                in_specs=[VMEM] * 4,
                out_specs=(VMEM,) * 2,
                compiler_params=params(24),
                cost_estimate=pl.CostEstimate(flops=0, bytes_accessed=8_000_000, transcendentals=0),
                name="merge",
            )(came[0], own[0], came[1], own[1])
    span = 2 * sub * share + 2 * share
    outgoing = pl.pallas_call(
        functools.partial(merge_kernel, True, root, share, sub),
        out_shape=jax.ShapeDtypeStruct((groups * span, feature), BF16),
        in_specs=[VMEM] * (4 * CHUNKS),
        out_specs=VMEM,
        compiler_params=params(24),
        name="merge_last",
    )(*finals)
    returned = lax.all_to_all(outgoing.reshape(groups, span, feature), "index", split_axis=0, concat_axis=0, tiled=True)

    logs = returned[:, capacity * share : capacity * share + 4 * PIECES].astype(F32)
    logs = jnp.sum(logs.reshape(groups, PIECES, CHUNKS, STRIDE), axis=1)
    logs = lax.dynamic_slice_in_dim(logs, (index % (groups // 2)) * sub, sub, 2).reshape(slots)
    logs = logs + travel(logs, 1) + travel(logs, -1) + travel(logs, 2)
    pair_scores = logs[place].reshape(query_count, list_len)
    highest = jnp.max(pair_scores, axis=1, keepdims=True)
    log_total = highest[:, 0] + jnp.log(jnp.sum(jnp.exp(pair_scores - highest), axis=1))
    losses = log_total - pair_scores[:, 0]
    probability = jnp.exp(pair_scores - log_total[:, None])
    target = (jnp.arange(list_len) == 0).astype(F32)
    coefficient = LOSS_SCALE * (probability - target[None, :])

    quarter = pl.pallas_call(
        functools.partial(gradient_kernel, share, list_len),
        out_shape=jax.ShapeDtypeStruct((query_count * share, feature), BF16),
        in_specs=[SMEM, SMEM, VMEM],
        out_specs=VMEM,
        scratch_shapes=[pltpu.VMEM((groups * span, feature), F32)],
        compiler_params=params(32),
        name="gradients",
    )(tile, coefficient.reshape(pairs), returned.reshape(groups * span, feature))
    gathered = lax.all_gather(quarter.reshape(query_count, share, feature), "rep")
    gradients = jnp.transpose(gathered, (1, 0, 2, 3)).reshape(query_count, query_len, feature)
    return (losses, gradients)


def solution(mesh):
    return jax.shard_map(
        per_device,
        mesh=mesh,
        in_specs=(
            P("index", None, None),
            P("index", None),
            P(),
            P("index"),
            P("index", "rep", None),
        ),
        out_specs=(P("index"), P("index", None, None)),
        check_vma=False,
    )
```

time: 267 us -> 225 us (0.84)
  starting transfers between devices: 70.6 us -> 38.3 us
  between operations: 1.1 us -> 14.3 us
  blocking collectives: 23.5 us -> 12.5 us
  Pallas kernels: 65 us -> 55.1 us
  local copies, waits for them, and re-layouts: 16.3 us -> 9.5 us
  waiting for transfers between devices: 89.1 us -> 92.7 us
    ppermute x23 -> x0, waiting for transfers between devices: 35.5 us -> none  [the longest x3 21.1 us: spread(): right = lax.ppermute(x, 'index', ring_pairs(second, 1))]
    all_gather x0 -> x1, waiting for transfers between devices: none -> 30.3 us  [per_device(): everyone = lax.all_gather(queries, 'index', tiled=True)]
    ppermute x23 -> x0, starting transfers between devices: 23 us -> none  [the longest x3 8.83 us: spread(): far_b = lax.ppermute(left[n:], 'index', ring_pairs(second, -1))]
    ppermute x18 -> x15, waiting for transfers between devices: 14.2 us -> 29.7 us  [travel(): return lax.ppermute(x, 'rep', rep_pairs(step))]
    all_to_all x1 -> x0, blocking collectives: 10.6 us -> none  [per_device(): lax.all_to_all(logs, 'index', split_axis=0, concat_axis=0, tiled=True)]
    pallas_call x9 -> x8, Pallas kernels: 58.3 us -> 48.3 us  [the longest x2 26.9 us: per_device(): pl.pallas_call(functools.partial(pair_kernel, chunk, blocks, scale), out_...]
    all_to_all x3 -> x1, waiting for transfers between devices: 32.9 us -> 25.3 us  [per_device(): lax.all_to_all(outgoing.reshape(groups, span, feature), 'index', split_ax...]
    all_to_all x3 -> x1, starting transfers between devices: 11.7 us -> 5.56 us  [per_device(): lax.all_to_all(outgoing.reshape(groups, span, feature), 'index', split_ax...]
  transfers between devices with their start and end apart: 45 -> 18, of which waited for: 13 -> 11; matrix products, arithmetic and copies ran while one was open for 4% -> 2% of each run, Pallas kernels for 17% -> 16%
where the time goes in v3:
time: 225 us
  waiting for transfers between devices  92.7 us (41%)
  Pallas kernels  55.1 us (24%)
  starting transfers between devices  38.3 us (17%)
  between operations  14.3 us (6%)
  blocking collectives  12.5 us (6%)
  local copies, waits for them, and re-layouts  9.5 us (4%)
  other arithmetic  2.33 us (1%)
    all_gather x1, waiting for transfers between devices, per_device(): everyone = lax.all_gather(queries, 'index', tiled=True)  30.3 us
    ppermute x15, waiting for transfers between devices, travel(): return lax.ppermute(x, 'rep', rep_pairs(step))  29.7 us
    pallas_call x2, Pallas kernels, per_device(): pl.pallas_call(functools.partial(pair_kernel, chunk, blocks, scale), out_...  26.9 us
    all_to_all x1, waiting for transfers between devices, per_device(): lax.all_to_all(outgoing.reshape(groups, span, feature), 'index', split_ax...  25.3 us
    ppermute x15, starting transfers between devices, travel(): return lax.ppermute(x, 'rep', rep_pairs(step))  24.3 us
    all_gather x1, blocking collectives, per_device(): lax.all_gather(quarter.reshape(query_count, share, feature), 'rep')  12.5 us
    pallas_call x1, Pallas kernels, per_device(): pl.pallas_call(functools.partial(sort_kernel, capacity, page_bits, query_...  12.1 us
    all_to_all x1, starting transfers between devices, per_device(): lax.all_to_all(table.reshape(groups, capacity), 'index', split_axis=0, co...  8.42 us
  transfers between devices with their start and end apart: 18, of which 11 were waited for; matrix products, arithmetic and copies ran while one was open for 2% of the time, Pallas kernels for 16%

profile of v3, /device:TPU:0, one launch (start us, length us, event | category | flops | bytes accessed | tf_op | source)
XLA Modules:
  0.0 224.7 jit_solution(6059587554072100681)
XLA Ops:
  7.2 0.7 all-gather.2.cloned.1.call-update
  7.9 0.8 copy.14
  8.7 0.7 reshape.51.listed
  9.3 5.1 %route.1 = (s32[768]{0:T(1024)}, s32[384]{0:T(512)}, s32[384]{0:T(512)}) custom-call(s32[384]{0:T(512)} %reshape.51.listed, s32[2048]{0:T(1024)} %page_slot.1), custom_call_target="tpu_custom_call" | custom-call | tf_op jit(solution)/shard_map/route/pallas_call | solution.py:312
  14.5 1.4 all_to_all.9
  15.8 8.4 %all-to-all-start = ((s32[32,1,24]{2,1,0:T(1,128)}), s32[32,1,24]{2,1,0:T(1,128)S(1)}, u32[]{:S(2)}, u32[]{:S(2)}) async-start(s32[32,1,24]{2,1,0:T(1,128)} %bitcast), calls=%async_computation | async-start | bytes 32768 | tf_op jit(solution)/shard_map/all_to_all | solution.py:320
  24.3 0.7 broadcast_subtract_fusion.limits
  24.9 6.6 %all-to-all-done = s32[32,1,24]{2,1,0:T(1,128)S(1)} async-done(((s32[32,1,24]{2,1,0:T(1,128)}), s32[32,1,24]{2,1,0:T(1,128)S(1)}, u32[]{:S(2)}, u32[]{:S(2)}) %all-to-all-start) | async-done | bytes 3104 | tf_op jit(solution)/shard_map/all_to_all | solution.py:320
  31.6 0.5 broadcast.22
  32.1 0.7 reduce.5
  32.8 0.7 reshape.52.arrived
  33.5 12.1 %sort_pairs.1 = (s32[1920]{0:T(1024)}, s32[288]{0:T(512)}, s32[2]{0:T(128)}) custom-call(s32[768]{0:T(1024)} %reshape.52.arrived), custom_call_target="tpu_custom_call" | custom-call | bytes 40000000 | tf_op jit(solution)/shard_map/sort_pairs/pallas_call | solution.py:324
  45.6 30.3 %all-gather.2.cloned.1.call-done.refs_1_ = bf16[1536,32,128]{2,1,0:T(8,128)(2,1)} async-done(((bf16[48,32,128]{2,1,0:T(8,128)(2,1)}), bf16[1536,32,128]{2,1,0:T(8,128)(2,1)}) %all-gather.2.cloned.1.call-update) | async-done | bytes 12582928 | tf_op jit(solution)/shard_map/all_gather | solution.py:322
  75.9 0.7 copy-done
  76.6 0.7 copy-done.1
  77.2 0.7 copy-done.2
  77.9 13.4 %pairs.2 = (bf16[1632,128]{1,0:T(8,128)(2,1)S(1)}, bf16[1632,128]{1,0:T(8,128)(2,1)S(1)}, bf16[1632,128]{1,0:T(8,128)(2,1)S(1)}, bf16[1632,128]{1,0:T(8,128)(2,1...) custom-call(s32[1920]{0:T(1024)S(1)} %copy-done, ...), custom_call_target="tpu_custom_call" | custom-call | bytes 60000000 | tf_op jit(solution)/shard_map/pairs/pallas_call | solution.py:348
  91.3 1.5 collective-permute-start
  92.9 1.8 collective-permute-start.1
  94.6 13.4 %pairs.3 = (bf16[1632,128]{1,0:T(8,128)(2,1)S(1)}, bf16[1632,128]{1,0:T(8,128)(2,1)S(1)}, bf16[1632,128]{1,0:T(8,128)(2,1)S(1)}, bf16[1632,128]{1,0:T(8,128)(2,1...) custom-call(s32[1920]{0:T(1024)S(1)} %copy-done, ...), custom_call_target="tpu_custom_call" | custom-call | bytes 60000000 | tf_op jit(solution)/shard_map/pairs/pallas_call | solution.py:348
  108.1 0.3 collective-permute-start.6
  108.4 3.0 %collective-permute-start.7 = (bf16[1632,128]{1,0:T(8,128)(2,1)S(1)}, bf16[1632,128]{1,0:T(8,128)(2,1)S(1)}, u32[]{:S(2)}, u32[]{:S(2)}) collective-permute-start(bf16[1632,128]{1,0:T(8,128)(2,1)S(1)} %get-tuple-element.50), channel_id=1, source_target_pairs={{0,3},{1,0},{2,1},{3,2},{4,7},{5,4},{6,5},{7,6},{8,11},{9,8},{10,9... | collective-permute-start | bytes 1253384 | tf_op jit(solution)/shard_map/ppermute | solution.py:344
  111.4 1.4 merge.4
  112.8 0.1 collective-permute-start.2
  112.8 3.2 %collective-permute-start.3 = (bf16[1632,128]{1,0:T(8,128)(2,1)S(1)}, bf16[1632,128]{1,0:T(8,128)(2,1)S(1)}, u32[]{:S(2)}, u32[]{:S(2)}) collective-permute-start(bf16[1632,128]{1,0:T(8,128)(2,1)S(1)} %get-tuple-element.42), channel_id=1, source_target_pairs={{0,3},{1,0},{2,1},{3,2},{4,7},{5,4},{6,5},{7,6},{8,11},{9,8},{10,9... | collective-permute-start | bytes 1253384 | tf_op jit(solution)/shard_map/ppermute | solution.py:344
  116.1 5.8 %collective-permute-done.6.refs_0_ = bf16[1632,128]{1,0:T(8,128)(2,1)S(1)} collective-permute-done((bf16[1632,128]{1,0:T(8,128)(2,1)S(1)}, bf16[1632,128]{1,0:T(8,128)(2,1)S(1)}, u32[]{:S(2)}, u32[]{:S(2)}) %collective-permute-start.6) | collective-permute-done | bytes 417824 | tf_op jit(solution)/shard_map/ppermute | solution.py:344
  121.9 1.4 merge.6
  123.3 0.6 collective-permute-start.8
  123.9 2.8 %collective-permute-start.9 = (bf16[1632,128]{1,0:T(8,128)(2,1)S(1)}, bf16[1632,128]{1,0:T(8,128)(2,1)S(1)}, u32[]{:S(2)}, u32[]{:S(2)}) collective-permute-start(bf16[1632,128]{1,0:T(8,128)(2,1)S(1)} %get-tuple-element.54), channel_id=1, source_target_pairs={{0,3},{1,0},{2,1},{3,2},{4,7},{5,4},{6,5},{7,6},{8,11},{9,8},{10,9... | collective-permute-start | bytes 1253384 | tf_op jit(solution)/shard_map/ppermute | solution.py:344
  126.7 4.2 %collective-permute-done.2.refs_0_ = bf16[1632,128]{1,0:T(8,128)(2,1)S(1)} collective-permute-done((bf16[1632,128]{1,0:T(8,128)(2,1)S(1)}, bf16[1632,128]{1,0:T(8,128)(2,1)S(1)}, u32[]{:S(2)}, u32[]{:S(2)}) %collective-permute-start.2) | collective-permute-done | bytes 417824 | tf_op jit(solution)/shard_map/ppermute | solution.py:344
  130.9 1.4 merge.5
  132.2 0.6 collective-permute-start.4
  132.8 3.0 %collective-permute-start.5 = (bf16[1632,128]{1,0:T(8,128)(2,1)S(1)}, bf16[1632,128]{1,0:T(8,128)(2,1)S(1)}, u32[]{:S(2)}, u32[]{:S(2)}) collective-permute-start(bf16[1632,128]{1,0:T(8,128)(2,1)S(1)} %get-tuple-element.46), channel_id=1, source_target_pairs={{0,3},{1,0},{2,1},{3,2},{4,7},{5,4},{6,5},{7,6},{8,11},{9,8},{10,9... | collective-permute-start | bytes 1253384 | tf_op jit(solution)/shard_map/ppermute | solution.py:344
  135.8 4.0 %collective-permute-done.8.refs_0_ = bf16[1632,128]{1,0:T(8,128)(2,1)S(1)} collective-permute-done((bf16[1632,128]{1,0:T(8,128)(2,1)S(1)}, bf16[1632,128]{1,0:T(8,128)(2,1)S(1)}, u32[]{:S(2)}, u32[]{:S(2)}) %collective-permute-start.8) | collective-permute-done | bytes 417824 | tf_op jit(solution)/shard_map/ppermute | solution.py:344
  139.8 1.4 merge.7
  141.2 0.6 collective-permute-start.10
  141.8 2.8 %collective-permute-start.11 = (bf16[1632,128]{1,0:T(8,128)(2,1)S(1)}, bf16[1632,128]{1,0:T(8,128)(2,1)S(1)}, u32[]{:S(2)}, u32[]{:S(2)}) collective-permute-start(bf16[1632,128]{1,0:T(8,128)(2,1)S(1)} %get-tuple-element.58), channel_id=1, source_target_pairs={{0,3},{1,0},{2,1},{3,2},{4,7},{5,4},{6,5},{7,6},{8,11},{9,8},{10,9... | collective-permute-start | bytes 1253384 | tf_op jit(solution)/shard_map/ppermute | solution.py:344
  144.6 4.2 %collective-permute-done.4.refs_0_ = bf16[1632,128]{1,0:T(8,128)(2,1)S(1)} collective-permute-done((bf16[1632,128]{1,0:T(8,128)(2,1)S(1)}, bf16[1632,128]{1,0:T(8,128)(2,1)S(1)}, u32[]{:S(2)}, u32[]{:S(2)}) %collective-permute-start.4) | collective-permute-done | bytes 417824 | tf_op jit(solution)/shard_map/ppermute | solution.py:344
  148.8 7.7 %collective-permute-done.10.refs_4_ = bf16[1632,128]{1,0:T(8,128)(2,1)S(1)} collective-permute-done((bf16[1632,128]{1,0:T(8,128)(2,1)S(1)}, bf16[1632,128]{1,0:T(8,128)(2,1)S(1)}, u32[]{:S(2)}, u32[]{:S(2)}) %collective-permute-start.10) | collective-permute-done | bytes 417824 | tf_op jit(solution)/shard_map/ppermute | solution.py:344
  156.4 3.9 %merge_last.1 = bf16[6656,128]{1,0:T(8,128)(2,1)} custom-call(bf16[1632,128]{1,0:T(8,128)(2,1)S(1)} %collective-permute-done.4.refs_0_, bf16[1632,128]{1,0:T(8,128)(2,1)S(1)} %get-tuple-element.45.refs_1_, bf16[1632,128]{1,0:T(8,128)(2,1)S(1)} %collective-permute-done.5.refs_2_, bf16[1632,128]{1,0:T(8,128)(2,1)S(1)} %get-tuple-element.47.refs_3_, ...), custom_call_target="tpu_custom_call" | custom-call | tf_op jit(solution)/shard_map/merge_last/pallas_call | solution.py:382
  160.3 5.6 %all-to-all-start.1 = ((bf16[32,208,128]{2,1,0:T(8,128)(2,1)}), bf16[32,208,128]{2,1,0:T(8,128)(2,1)S(1)}, u32[]{:S(2)}, u32[]{:S(2)}) async-start(bf16[32,208,128]{2,1,0:T(8,128)(2,1)} %bitcast.2), calls=%async_computation.1 | async-start | bytes 3407872 | tf_op jit(solution)/shard_map/all_to_all | solution.py:390
  166.0 25.3 %all-to-all-done.1 = bf16[32,208,128]{2,1,0:T(8,128)(2,1)S(1)} async-done(((bf16[32,208,128]{2,1,0:T(8,128)(2,1)}), bf16[32,208,128]{2,1,0:T(8,128)(2,1)S(1)}, u32[]{:S(2)}, u32[]{:S(2)}) %all-to-all-start.1) | async-done | bytes 1703968 | tf_op jit(solution)/shard_map/all_to_all | solution.py:390
  191.3 0.1 reshape.61
  191.5 0.1 reduce_sum.18
  191.6 0.1 constant_dynamic-slice_fusion
  191.7 0.1 reshape.56
  191.8 1.9 collective-permute-start.14
  193.7 1.2 collective-permute-start.13
  194.9 0.8 collective-permute-start.12
  195.7 0.1 sub.48
  195.8 1.2 collective-permute-done.14
  197.0 0.3 collective-permute-done.13
  197.3 2.4 %collective-permute-done.12 = f32[768]{0:T(1024)S(1)} collective-permute-done((f32[768]{0:T(1024)S(1)}, f32[768]{0:T(1024)S(1)}, u32[]{:S(2)}, u32[]{:S(2)}) %collective-permute-start.12) | collective-permute-done | bytes 3104 | tf_op jit(solution)/shard_map/ppermute | solution.py:344
  199.7 1.9 gather_fusion
  201.6 0.1 reshape.57
  201.7 0.1 slice_reduce_fusion
  201.8 0.1 reduce_max.9
  201.9 0.2 exponential_reduce_fusion
  202.1 0.5 fusion
  202.7 0.1 sub.44
  202.7 0.1 sub.45
  202.8 1.7 gradients.1
  204.5 12.5 %all_gather.7 = bf16[4,48,8,128]{3,2,1,0:T(8,128)(2,1)S(1)} all-gather(bf16[1,48,8,128]{3,2,1,0:T(8,128)(2,1)S(1)} %bitcast.11), channel_id=1, replica_groups=mesh['index'=32,'rep'=4] {'rep'}, dimensions={0}, use_global_device_ids=true | all-gather | bytes 491520 | tf_op jit(solution)/shard_map/all_gather | solution.py:413
  217.1 0.8 copy.18
  (22 shorter events, 0.1 us)
Async XLA Ops:
  7.2 68.7 %all-gather.2.cloned.1.call-start = ((), (), s32[]{:S(2)}) async-start(), calls=%async_computation.2 | async-start | bytes 12976128 | tf_op jit(solution)/shard_map/all_gather | solution.py:322
  15.8 15.7 %all-to-all-start = ((s32[32,1,24]{2,1,0:T(1,128)}), s32[32,1,24]{2,1,0:T(1,128)S(1)}, u32[]{:S(2)}, u32[]{:S(2)}) async-start(s32[32,1,24]{2,1,0:T(1,128)} %bitcast), calls=%async_computation | async-start | bytes 32768 | tf_op jit(solution)/shard_map/all_to_all | solution.py:320
  75.9 0.7 copy-start
  76.6 0.7 copy-start.1
  77.2 0.7 copy-start.2
  91.3 20.1 %collective-permute-start = (bf16[1632,128]{1,0:T(8,128)(2,1)S(1)}, bf16[1632,128]{1,0:T(8,128)(2,1)S(1)}, u32[]{:S(2)}, u32[]{:S(2)}) collective-permute-start(bf16[1632,128]{1,0:T(8,128)(2,1)S(1)} %get-tuple-element.36), channel_id=1, source_target_pairs={{0,1},{1,2},{2,3},{3,0},{4,5},{5,6},{6,7},{7,4},{8,9},{9,10},{10,1... | collective-permute-start | bytes 1253384 | tf_op jit(solution)/shard_map/ppermute | solution.py:344
  92.9 18.5 %collective-permute-start.1 = (bf16[1632,128]{1,0:T(8,128)(2,1)S(1)}, bf16[1632,128]{1,0:T(8,128)(2,1)S(1)}, u32[]{:S(2)}, u32[]{:S(2)}) collective-permute-start(bf16[1632,128]{1,0:T(8,128)(2,1)S(1)} %get-tuple-element.38), channel_id=1, source_target_pairs={{0,3},{1,0},{2,1},{3,2},{4,7},{5,4},{6,5},{7,6},{8,11},{9,8},{10,9... | collective-permute-start | bytes 1253384 | tf_op jit(solution)/shard_map/ppermute | solution.py:344
  108.1 13.8 %collective-permute-start.6 = (bf16[1632,128]{1,0:T(8,128)(2,1)S(1)}, bf16[1632,128]{1,0:T(8,128)(2,1)S(1)}, u32[]{:S(2)}, u32[]{:S(2)}) collective-permute-start(bf16[1632,128]{1,0:T(8,128)(2,1)S(1)} %get-tuple-element.48), channel_id=1, source_target_pairs={{0,1},{1,2},{2,3},{3,0},{4,5},{5,6},{6,7},{7,4},{8,9},{9,10},{10,1... | collective-permute-start | bytes 1253384 | tf_op jit(solution)/shard_map/ppermute | solution.py:344
  108.4 13.5 %collective-permute-start.7 = (bf16[1632,128]{1,0:T(8,128)(2,1)S(1)}, bf16[1632,128]{1,0:T(8,128)(2,1)S(1)}, u32[]{:S(2)}, u32[]{:S(2)}) collective-permute-start(bf16[1632,128]{1,0:T(8,128)(2,1)S(1)} %get-tuple-element.50), channel_id=1, source_target_pairs={{0,3},{1,0},{2,1},{3,2},{4,7},{5,4},{6,5},{7,6},{8,11},{9,8},{10,9... | collective-permute-start | bytes 1253384 | tf_op jit(solution)/shard_map/ppermute | solution.py:344
  112.8 18.1 %collective-permute-start.2 = (bf16[1632,128]{1,0:T(8,128)(2,1)S(1)}, bf16[1632,128]{1,0:T(8,128)(2,1)S(1)}, u32[]{:S(2)}, u32[]{:S(2)}) collective-permute-start(bf16[1632,128]{1,0:T(8,128)(2,1)S(1)} %get-tuple-element.40), channel_id=1, source_target_pairs={{0,1},{1,2},{2,3},{3,0},{4,5},{5,6},{6,7},{7,4},{8,9},{9,10},{10,1... | collective-permute-start | bytes 1253384 | tf_op jit(solution)/shard_map/ppermute | solution.py:344
  112.8 18.0 %collective-permute-start.3 = (bf16[1632,128]{1,0:T(8,128)(2,1)S(1)}, bf16[1632,128]{1,0:T(8,128)(2,1)S(1)}, u32[]{:S(2)}, u32[]{:S(2)}) collective-permute-start(bf16[1632,128]{1,0:T(8,128)(2,1)S(1)} %get-tuple-element.42), channel_id=1, source_target_pairs={{0,3},{1,0},{2,1},{3,2},{4,7},{5,4},{6,5},{7,6},{8,11},{9,8},{10,9... | collective-permute-start | bytes 1253384 | tf_op jit(solution)/shard_map/ppermute | solution.py:344
  123.3 16.5 %collective-permute-start.8 = (bf16[1632,128]{1,0:T(8,128)(2,1)S(1)}, bf16[1632,128]{1,0:T(8,128)(2,1)S(1)}, u32[]{:S(2)}, u32[]{:S(2)}) collective-permute-start(bf16[1632,128]{1,0:T(8,128)(2,1)S(1)} %get-tuple-element.52), channel_id=1, source_target_pairs={{0,1},{1,2},{2,3},{3,0},{4,5},{5,6},{6,7},{7,4},{8,9},{9,10},{10,1... | collective-permute-start | bytes 1253384 | tf_op jit(solution)/shard_map/ppermute | solution.py:344
  123.9 15.9 %collective-permute-start.9 = (bf16[1632,128]{1,0:T(8,128)(2,1)S(1)}, bf16[1632,128]{1,0:T(8,128)(2,1)S(1)}, u32[]{:S(2)}, u32[]{:S(2)}) collective-permute-start(bf16[1632,128]{1,0:T(8,128)(2,1)S(1)} %get-tuple-element.54), channel_id=1, source_target_pairs={{0,3},{1,0},{2,1},{3,2},{4,7},{5,4},{6,5},{7,6},{8,11},{9,8},{10,9... | collective-permute-start | bytes 1253384 | tf_op jit(solution)/shard_map/ppermute | solution.py:344
  132.2 16.5 %collective-permute-start.4 = (bf16[1632,128]{1,0:T(8,128)(2,1)S(1)}, bf16[1632,128]{1,0:T(8,128)(2,1)S(1)}, u32[]{:S(2)}, u32[]{:S(2)}) collective-permute-start(bf16[1632,128]{1,0:T(8,128)(2,1)S(1)} %get-tuple-element.44), channel_id=1, source_target_pairs={{0,1},{1,2},{2,3},{3,0},{4,5},{5,6},{6,7},{7,4},{8,9},{9,10},{10,1... | collective-permute-start | bytes 1253384 | tf_op jit(solution)/shard_map/ppermute | solution.py:344
  132.8 15.9 %collective-permute-start.5 = (bf16[1632,128]{1,0:T(8,128)(2,1)S(1)}, bf16[1632,128]{1,0:T(8,128)(2,1)S(1)}, u32[]{:S(2)}, u32[]{:S(2)}) collective-permute-start(bf16[1632,128]{1,0:T(8,128)(2,1)S(1)} %get-tuple-element.46), channel_id=1, source_target_pairs={{0,3},{1,0},{2,1},{3,2},{4,7},{5,4},{6,5},{7,6},{8,11},{9,8},{10,9... | collective-permute-start | bytes 1253384 | tf_op jit(solution)/shard_map/ppermute | solution.py:344
  141.2 15.2 %collective-permute-start.10 = (bf16[1632,128]{1,0:T(8,128)(2,1)S(1)}, bf16[1632,128]{1,0:T(8,128)(2,1)S(1)}, u32[]{:S(2)}, u32[]{:S(2)}) collective-permute-start(bf16[1632,128]{1,0:T(8,128)(2,1)S(1)} %get-tuple-element.56), channel_id=1, source_target_pairs={{0,1},{1,2},{2,3},{3,0},{4,5},{5,6},{6,7},{7,4},{8,9},{9,10},{10,1... | collective-permute-start | bytes 1253384 | tf_op jit(solution)/shard_map/ppermute | solution.py:344
  141.8 14.6 %collective-permute-start.11 = (bf16[1632,128]{1,0:T(8,128)(2,1)S(1)}, bf16[1632,128]{1,0:T(8,128)(2,1)S(1)}, u32[]{:S(2)}, u32[]{:S(2)}) collective-permute-start(bf16[1632,128]{1,0:T(8,128)(2,1)S(1)} %get-tuple-element.58), channel_id=1, source_target_pairs={{0,3},{1,0},{2,1},{3,2},{4,7},{5,4},{6,5},{7,6},{8,11},{9,8},{10,9... | collective-permute-start | bytes 1253384 | tf_op jit(solution)/shard_map/ppermute | solution.py:344
  160.3 5.6 %copy-start.4 = (s32[384]{0:T(512)S(1)}, s32[384]{0:T(512)}, u32[]{:S(2)}) copy-start(s32[384]{0:T(512)} %get-tuple-element.60) | copy-start | bytes 4612
  160.3 31.0 %all-to-all-start.1 = ((bf16[32,208,128]{2,1,0:T(8,128)(2,1)}), bf16[32,208,128]{2,1,0:T(8,128)(2,1)S(1)}, u32[]{:S(2)}, u32[]{:S(2)}) async-start(bf16[32,208,128]{2,1,0:T(8,128)(2,1)} %bitcast.2), calls=%async_computation.1 | async-start | bytes 3407872 | tf_op jit(solution)/shard_map/all_to_all | solution.py:390
  166.0 36.9 %copy-start.3 = (s32[384]{0:T(512)S(1)}, s32[384]{0:T(512)}, u32[]{:S(2)}) copy-start(s32[384]{0:T(512)} %get-tuple-element.61.place) | copy-start | bytes 4612
  191.8 5.2 %collective-permute-start.14 = (f32[768]{0:T(1024)S(1)}, f32[768]{0:T(1024)S(1)}, u32[]{:S(2)}, u32[]{:S(2)}) collective-permute-start(f32[768]{0:T(1024)S(1)} %reshape.56), channel_id=1, source_target_pairs={{0,2},{1,3},{2,0},{3,1},{4,6},{5,7},{6,4},{7,5},{8,10},{9,11},{10,... | collective-permute-start | bytes 9224 | tf_op jit(solution)/shard_map/ppermute | solution.py:344
  193.7 3.6 %collective-permute-start.13 = (f32[768]{0:T(1024)S(1)}, f32[768]{0:T(1024)S(1)}, u32[]{:S(2)}, u32[]{:S(2)}) collective-permute-start(f32[768]{0:T(1024)S(1)} %reshape.56), channel_id=1, source_target_pairs={{0,3},{1,0},{2,1},{3,2},{4,7},{5,4},{6,5},{7,6},{8,11},{9,8},{10,9... | collective-permute-start | bytes 9224 | tf_op jit(solution)/shard_map/ppermute | solution.py:344
  194.9 4.8 %collective-permute-start.12 = (f32[768]{0:T(1024)S(1)}, f32[768]{0:T(1024)S(1)}, u32[]{:S(2)}, u32[]{:S(2)}) collective-permute-start(f32[768]{0:T(1024)S(1)} %reshape.56), channel_id=1, source_target_pairs={{0,1},{1,2},{2,3},{3,0},{4,5},{5,6},{6,7},{7,4},{8,9},{9,10},{10,1... | collective-permute-start | bytes 9224 | tf_op jit(solution)/shard_map/ppermute | solution.py:344
Sparse Core Ops, SparseCore 0:
  10.2 65.5 all-gather.1

commit v4 on v3

--- a/solution.py
+++ b/solution.py
@@ -61,7 +61,9 @@
     lax.fori_loop(0, pairs // list_len, step, 0)
 
 
-def sort_kernel(capacity, page_bits, query_count, blocks, arrived, order, block_page, block_count, count, first):
+def sort_kernel(capacity, page_bits, query_count, blocks, arrived, order, count, first):
+    page_base = CHUNKS * blocks * BLOCK
+    total_base = page_base + CHUNKS * blocks
     slots = arrived.shape[0]
     groups = slots // capacity
     sub = capacity // CHUNKS
@@ -77,7 +79,7 @@
 
     def clear_blocks(i, _):
         for k in range(16):
-            block_page[i * 16 + k] = 0
+            order[page_base + i * 16 + k] = 0
         return 0
 
     lax.fori_loop(0, CHUNKS * blocks // 16, clear_blocks, 0)
@@ -103,15 +105,15 @@
             steps = lax.shift_right_logical(n + BLOCK - 1, 2)
 
             def one(k, _):
-                block_page[b + k] = p
+                order[page_base + b + k] = p
                 return 0
 
             lax.fori_loop(0, steps, one, 0)
             return b + steps
 
         total = lax.fori_loop(0, pages, lay, jnp.int32(chunk * blocks))
-        block_count[chunk] = total - chunk * blocks
-    first[CHUNKS * pages] = CHUNKS * blocks * BLOCK
+        order[total_base + chunk] = total - chunk * blocks
+    first[CHUNKS * pages] = total_base + 8
     count[CHUNKS * pages] = 0
 
     def source(s, _):
@@ -140,15 +142,12 @@
     return parts
 
 
-def pair_kernel(chunk, blocks, scale, order, block_page, block_count, limits, me, *refs):
-    store, queries = refs[:2]
+def pair_kernel(chunk, blocks, scale, order, limits, me, *refs):
+    page_base = CHUNKS * blocks * BLOCK
+    total_base = page_base + CHUNKS * blocks
+    pages, held = refs[:2]
     outs = refs[2:10]
-    held, pages, wide, stats, sems = refs[10:]
-    copies = [pltpu.make_async_copy(queries, held, sems.at[0]), pltpu.make_async_copy(store, pages, sems.at[1])]
-    for c in copies:
-        c.start()
-    for c in copies:
-        c.wait()
+    wide, stats = refs[10:]
     part = pages.shape[1]
     tokens = held.shape[1]
     share = tokens // 4
@@ -159,7 +158,7 @@
     def step(it, _):
         for u in range(UNROLL):
             b = chunk * blocks + it * UNROLL + u
-            p = block_page[b]
+            p = order[page_base + b]
             codes = [order[b * BLOCK + i] for i in range(BLOCK)]
             block = jnp.concatenate([held[c & 2047] for c in codes], axis=0)
             page = pages[p]
@@ -182,11 +181,11 @@
                 stats[1, at] = jnp.where(here, total[rows], stats[1, at])
         return 0
 
-    lax.fori_loop(0, (block_count[chunk] + UNROLL - 1) // UNROLL, step, 0)
+    lax.fori_loop(0, (order[total_base + chunk] + UNROLL - 1) // UNROLL, step, 0)
 
     rep = me[0]
     length = outs[0].shape[0] - 2 * PIECES * 2 * share
-    piece = 128
+    piece = 512
     for p in range(4):
         t = (rep + p) & 3
         for h in range(2):
@@ -321,11 +320,11 @@
 
     everyone = lax.all_gather(queries, "index", tiled=True)
 
-    order, block_page, block_count = pl.pallas_call(
+    order = pl.pallas_call(
         functools.partial(sort_kernel, capacity, page_bits, query_count, blocks),
-        out_shape=(ints(CHUNKS * blocks * BLOCK + slots), ints(CHUNKS * blocks), ints(CHUNKS)),
+        out_shape=ints(CHUNKS * blocks * (BLOCK + 1) + 8 + slots),
         in_specs=[SMEM],
-        out_specs=(SMEM,) * 3,
+        out_specs=SMEM,
         scratch_shapes=[pltpu.SMEM((CHUNKS * pages + 1,), jnp.int32)] * 2,
         cost_estimate=pl.CostEstimate(flops=0, bytes_accessed=40_000_000, transcendentals=0),
         name="sort_pairs",
@@ -348,19 +347,16 @@
         parts = pl.pallas_call(
             functools.partial(pair_kernel, chunk, blocks, scale),
             out_shape=(jax.ShapeDtypeStruct((packed, feature), BF16),) * 8,
-            in_specs=[SMEM] * 5 + [ANY] * 2,
+            in_specs=[SMEM] * 3 + [VMEM] * 2,
             out_specs=(VMEM,) * 8,
             scratch_shapes=[
-                pltpu.VMEM((groups * query_count, query_len, feature), BF16),
-                pltpu.VMEM((pages, part, feature), BF16),
                 pltpu.VMEM((4, 2 * STRIDE * share, feature), F32),
                 pltpu.VMEM((2, 2 * STRIDE // LANES, query_len, LANES), F32),
-                pltpu.SemaphoreType.DMA((2,)),
             ],
-            compiler_params=params(48),
+            compiler_params=params(28),
             cost_estimate=pl.CostEstimate(flops=0, bytes_accessed=60_000_000, transcendentals=0),
             name="pairs",
-        )(order, block_page, block_count, limits, me, page_store, everyone)
+        )(order, limits, me, page_store, everyone)
 
         held = [parts[3 * 2], parts[1 * 2 + 1]]
         for hop in range(3):

time: 225 us -> 220 us (0.978)
  Pallas kernels: 55.1 us -> 43.2 us
  local copies, waits for them, and re-layouts: 9.5 us -> 15 us
    pallas_call x2, Pallas kernels: 26.9 us -> 14.9 us  [per_device(): pl.pallas_call(functools.partial(pair_kernel, chunk, blocks, scale), out_...]
    unnamed x11, local copies, waits for them, and re-layouts: 2.8 us -> 8.24 us
  transfers between devices with their start and end apart: 18 -> 18, of which waited for: 11 -> 11; matrix products, arithmetic and copies ran while one was open for 2% -> 2% of each run, Pallas kernels for 16% -> 14%
where the time goes in v4:
time: 220 us; the launch traced here: 218 us
  waiting for transfers between devices  92.7 us (42%)
  Pallas kernels  43.2 us (20%)
  starting transfers between devices  38.3 us (17%)
  local copies, waits for them, and re-layouts  15 us (7%)
  between operations  14.3 us (6%)
  blocking collectives  12.5 us (6%)
  other arithmetic  2.33 us (1%)
    all_gather x1, waiting for transfers between devices, per_device(): everyone = lax.all_gather(queries, 'index', tiled=True)  30.2 us
    ppermute x15, waiting for transfers between devices, travel(): return lax.ppermute(x, 'rep', rep_pairs(step))  29.8 us
    all_to_all x1, waiting for transfers between devices, per_device(): lax.all_to_all(outgoing.reshape(groups, span, feature), 'index', split_ax...  25.3 us
    ppermute x15, starting transfers between devices, travel(): return lax.ppermute(x, 'rep', rep_pairs(step))  24.2 us
    pallas_call x2, Pallas kernels, per_device(): pl.pallas_call(functools.partial(pair_kernel, chunk, blocks, scale), out_...  14.9 us
    all_gather x1, blocking collectives, per_device(): lax.all_gather(quarter.reshape(query_count, share, feature), 'rep')  12.5 us
    pallas_call x1, Pallas kernels, per_device(): pl.pallas_call(functools.partial(sort_kernel, capacity, page_bits, query_...  12.1 us
    all_to_all x1, starting transfers between devices, per_device(): lax.all_to_all(table.reshape(groups, capacity), 'index', split_axis=0, co...  8.42 us
  transfers between devices with their start and end apart: 18, of which 11 were waited for; matrix products, arithmetic and copies ran while one was open for 2% of the time, Pallas kernels for 14%

profile of v4, /device:TPU:0, one launch (start us, length us, event | category | flops | bytes accessed | tf_op | source)
XLA Modules:
  0.0 218.2 jit_solution(4294051175813852929)
XLA Ops:
  7.2 0.7 all-gather.2.cloned.1.call-update
  7.9 0.8 copy.14
  8.7 0.7 reshape.51.listed
  9.3 5.1 %route.1 = (s32[768]{0:T(1024)}, s32[384]{0:T(512)}, s32[384]{0:T(512)}) custom-call(s32[384]{0:T(512)} %reshape.51.listed, s32[2048]{0:T(1024)} %page_slot.1), custom_call_target="tpu_custom_call" | custom-call | tf_op jit(solution)/shard_map/route/pallas_call | solution.py:311
  14.5 1.4 all_to_all.9
  15.8 8.4 %all-to-all-start = ((s32[32,1,24]{2,1,0:T(1,128)}), s32[32,1,24]{2,1,0:T(1,128)S(1)}, u32[]{:S(2)}, u32[]{:S(2)}) async-start(s32[32,1,24]{2,1,0:T(1,128)} %bitcast), calls=%async_computation | async-start | bytes 32768 | tf_op jit(solution)/shard_map/all_to_all | solution.py:319
  24.3 0.7 broadcast_subtract_fusion.limits
  24.9 6.6 %all-to-all-done = s32[32,1,24]{2,1,0:T(1,128)S(1)} async-done(((s32[32,1,24]{2,1,0:T(1,128)}), s32[32,1,24]{2,1,0:T(1,128)S(1)}, u32[]{:S(2)}, u32[]{:S(2)}) %all-to-all-start) | async-done | bytes 3104 | tf_op jit(solution)/shard_map/all_to_all | solution.py:319
  31.6 0.5 broadcast.22
  32.1 0.7 reduce.5
  32.8 0.7 reshape.52.arrived
  33.5 12.1 %sort_pairs.1.order = s32[2216]{0:T(1024)} custom-call(s32[768]{0:T(1024)} %reshape.52.arrived), custom_call_target="tpu_custom_call" | custom-call | bytes 40000000 | tf_op jit(solution)/shard_map/sort_pairs/pallas_call | solution.py:323
  45.6 30.2 %all-gather.2.cloned.1.call-done.refs_1_ = bf16[1536,32,128]{2,1,0:T(8,128)(2,1)} async-done(((bf16[48,32,128]{2,1,0:T(8,128)(2,1)}), bf16[1536,32,128]{2,1,0:T(8,128)(2,1)}) %all-gather.2.cloned.1.call-update) | async-done | bytes 12582928 | tf_op jit(solution)/shard_map/all_gather | solution.py:321
  75.9 4.6 %copy-done = bf16[1536,32,128]{2,1,0:T(8,128)(2,1)S(1)} copy-done((bf16[1536,32,128]{2,1,0:T(8,128)(2,1)S(1)}, bf16[1536,32,128]{2,1,0:T(8,128)(2,1)}, u32[]{:S(2)}) %copy-start) | copy-done | bytes 12582936
  80.4 2.2 %copy-done.1 = bf16[64,256,128]{2,1,0:T(8,128)(2,1)S(1)} copy-done((bf16[64,256,128]{2,1,0:T(8,128)(2,1)S(1)}, bf16[64,256,128]{2,1,0:T(8,128)(2,1)}, u32[]{:S(2)}) %copy-start.1) | copy-done | bytes 4194328
  82.6 0.7 copy-done.2
  83.3 7.5 %pairs.2 = (bf16[1632,128]{1,0:T(8,128)(2,1)S(1)}, bf16[1632,128]{1,0:T(8,128)(2,1)S(1)}, bf16[1632,128]{1,0:T(8,128)(2,1)S(1)}, bf16[1632,128]{1,0:T(8,128)(2,1...) custom-call(s32[2216]{0:T(1024)S(1)} %copy-done.2, ...), custom_call_target="tpu_custom_call" | custom-call | bytes 60000000 | tf_op jit(solution)/shard_map/pairs/pallas_call | solution.py:347
  90.8 1.5 collective-permute-start
  92.3 1.8 collective-permute-start.1
  94.1 7.5 %pairs.3 = (bf16[1632,128]{1,0:T(8,128)(2,1)S(1)}, bf16[1632,128]{1,0:T(8,128)(2,1)S(1)}, bf16[1632,128]{1,0:T(8,128)(2,1)S(1)}, bf16[1632,128]{1,0:T(8,128)(2,1...) custom-call(s32[2216]{0:T(1024)S(1)} %copy-done.2, ...), custom_call_target="tpu_custom_call" | custom-call | bytes 60000000 | tf_op jit(solution)/shard_map/pairs/pallas_call | solution.py:347
  101.6 0.3 collective-permute-start.6
  101.9 3.0 %collective-permute-start.7 = (bf16[1632,128]{1,0:T(8,128)(2,1)S(1)}, bf16[1632,128]{1,0:T(8,128)(2,1)S(1)}, u32[]{:S(2)}, u32[]{:S(2)}) collective-permute-start(bf16[1632,128]{1,0:T(8,128)(2,1)S(1)} %get-tuple-element.44), channel_id=1, source_target_pairs={{0,3},{1,0},{2,1},{3,2},{4,7},{5,4},{6,5},{7,6},{8,11},{9,8},{10,9... | collective-permute-start | bytes 1253384 | tf_op jit(solution)/shard_map/ppermute | solution.py:343
  104.9 1.4 merge.4
  106.2 0.5 collective-permute-start.2
  106.8 2.8 %collective-permute-start.3 = (bf16[1632,128]{1,0:T(8,128)(2,1)S(1)}, bf16[1632,128]{1,0:T(8,128)(2,1)S(1)}, u32[]{:S(2)}, u32[]{:S(2)}) collective-permute-start(bf16[1632,128]{1,0:T(8,128)(2,1)S(1)} %get-tuple-element.36), channel_id=1, source_target_pairs={{0,3},{1,0},{2,1},{3,2},{4,7},{5,4},{6,5},{7,6},{8,11},{9,8},{10,9... | collective-permute-start | bytes 1253384 | tf_op jit(solution)/shard_map/ppermute | solution.py:343
  109.5 5.9 %collective-permute-done.6.refs_0_ = bf16[1632,128]{1,0:T(8,128)(2,1)S(1)} collective-permute-done((bf16[1632,128]{1,0:T(8,128)(2,1)S(1)}, bf16[1632,128]{1,0:T(8,128)(2,1)S(1)}, u32[]{:S(2)}, u32[]{:S(2)}) %collective-permute-start.6) | collective-permute-done | bytes 417824 | tf_op jit(solution)/shard_map/ppermute | solution.py:343
  115.4 1.4 merge.6
  116.8 0.6 collective-permute-start.8
  117.4 2.8 %collective-permute-start.9 = (bf16[1632,128]{1,0:T(8,128)(2,1)S(1)}, bf16[1632,128]{1,0:T(8,128)(2,1)S(1)}, u32[]{:S(2)}, u32[]{:S(2)}) collective-permute-start(bf16[1632,128]{1,0:T(8,128)(2,1)S(1)} %get-tuple-element.48), channel_id=1, source_target_pairs={{0,3},{1,0},{2,1},{3,2},{4,7},{5,4},{6,5},{7,6},{8,11},{9,8},{10,9... | collective-permute-start | bytes 1253384 | tf_op jit(solution)/shard_map/ppermute | solution.py:343
  120.2 4.2 %collective-permute-done.2.refs_0_ = bf16[1632,128]{1,0:T(8,128)(2,1)S(1)} collective-permute-done((bf16[1632,128]{1,0:T(8,128)(2,1)S(1)}, bf16[1632,128]{1,0:T(8,128)(2,1)S(1)}, u32[]{:S(2)}, u32[]{:S(2)}) %collective-permute-start.2) | collective-permute-done | bytes 417824 | tf_op jit(solution)/shard_map/ppermute | solution.py:343
  124.3 1.4 merge.5
  125.7 0.6 collective-permute-start.4
  126.3 3.0 %collective-permute-start.5 = (bf16[1632,128]{1,0:T(8,128)(2,1)S(1)}, bf16[1632,128]{1,0:T(8,128)(2,1)S(1)}, u32[]{:S(2)}, u32[]{:S(2)}) collective-permute-start(bf16[1632,128]{1,0:T(8,128)(2,1)S(1)} %get-tuple-element.40), channel_id=1, source_target_pairs={{0,3},{1,0},{2,1},{3,2},{4,7},{5,4},{6,5},{7,6},{8,11},{9,8},{10,9... | collective-permute-start | bytes 1253384 | tf_op jit(solution)/shard_map/ppermute | solution.py:343
  129.3 4.0 %collective-permute-done.8.refs_0_ = bf16[1632,128]{1,0:T(8,128)(2,1)S(1)} collective-permute-done((bf16[1632,128]{1,0:T(8,128)(2,1)S(1)}, bf16[1632,128]{1,0:T(8,128)(2,1)S(1)}, u32[]{:S(2)}, u32[]{:S(2)}) %collective-permute-start.8) | collective-permute-done | bytes 417824 | tf_op jit(solution)/shard_map/ppermute | solution.py:343
  133.3 1.4 merge.7
  134.7 0.6 collective-permute-start.10
  135.3 2.8 %collective-permute-start.11 = (bf16[1632,128]{1,0:T(8,128)(2,1)S(1)}, bf16[1632,128]{1,0:T(8,128)(2,1)S(1)}, u32[]{:S(2)}, u32[]{:S(2)}) collective-permute-start(bf16[1632,128]{1,0:T(8,128)(2,1)S(1)} %get-tuple-element.52), channel_id=1, source_target_pairs={{0,3},{1,0},{2,1},{3,2},{4,7},{5,4},{6,5},{7,6},{8,11},{9,8},{10,9... | collective-permute-start | bytes 1253384 | tf_op jit(solution)/shard_map/ppermute | solution.py:343
  138.1 4.2 %collective-permute-done.4.refs_0_ = bf16[1632,128]{1,0:T(8,128)(2,1)S(1)} collective-permute-done((bf16[1632,128]{1,0:T(8,128)(2,1)S(1)}, bf16[1632,128]{1,0:T(8,128)(2,1)S(1)}, u32[]{:S(2)}, u32[]{:S(2)}) %collective-permute-start.4) | collective-permute-done | bytes 417824 | tf_op jit(solution)/shard_map/ppermute | solution.py:343
  142.3 7.6 %collective-permute-done.10.refs_4_ = bf16[1632,128]{1,0:T(8,128)(2,1)S(1)} collective-permute-done((bf16[1632,128]{1,0:T(8,128)(2,1)S(1)}, bf16[1632,128]{1,0:T(8,128)(2,1)S(1)}, u32[]{:S(2)}, u32[]{:S(2)}) %collective-permute-start.10) | collective-permute-done | bytes 417824 | tf_op jit(solution)/shard_map/ppermute | solution.py:343
  149.9 3.9 %merge_last.1 = bf16[6656,128]{1,0:T(8,128)(2,1)} custom-call(bf16[1632,128]{1,0:T(8,128)(2,1)S(1)} %collective-permute-done.4.refs_0_, bf16[1632,128]{1,0:T(8,128)(2,1)S(1)} %get-tuple-element.39.refs_1_, bf16[1632,128]{1,0:T(8,128)(2,1)S(1)} %collective-permute-done.5.refs_2_, bf16[1632,128]{1,0:T(8,128)(2,1)S(1)} %get-tuple-element.41.refs_3_, ...), custom_call_target="tpu_custom_call" | custom-call | tf_op jit(solution)/shard_map/merge_last/pallas_call | solution.py:378
  153.8 5.6 %all-to-all-start.1 = ((bf16[32,208,128]{2,1,0:T(8,128)(2,1)}), bf16[32,208,128]{2,1,0:T(8,128)(2,1)S(1)}, u32[]{:S(2)}, u32[]{:S(2)}) async-start(bf16[32,208,128]{2,1,0:T(8,128)(2,1)} %bitcast.2), calls=%async_computation.1 | async-start | bytes 3407872 | tf_op jit(solution)/shard_map/all_to_all | solution.py:386
  159.4 25.3 %all-to-all-done.1 = bf16[32,208,128]{2,1,0:T(8,128)(2,1)S(1)} async-done(((bf16[32,208,128]{2,1,0:T(8,128)(2,1)}), bf16[32,208,128]{2,1,0:T(8,128)(2,1)S(1)}, u32[]{:S(2)}, u32[]{:S(2)}) %all-to-all-start.1) | async-done | bytes 1703968 | tf_op jit(solution)/shard_map/all_to_all | solution.py:386
  184.8 0.1 reshape.61
  184.9 0.1 reduce_sum.18
  185.0 0.1 constant_dynamic-slice_fusion
  185.1 0.1 reshape.56
  185.3 1.5 collective-permute-start.14
  186.8 1.6 collective-permute-start.13
  188.4 0.8 collective-permute-start.12
  189.2 0.1 sub.48
  189.2 1.2 collective-permute-done.14
  190.4 0.3 collective-permute-done.13
  190.8 2.4 %collective-permute-done.12 = f32[768]{0:T(1024)S(1)} collective-permute-done((f32[768]{0:T(1024)S(1)}, f32[768]{0:T(1024)S(1)}, u32[]{:S(2)}, u32[]{:S(2)}) %collective-permute-start.12) | collective-permute-done | bytes 3104 | tf_op jit(solution)/shard_map/ppermute | solution.py:343
  193.2 1.9 gather_fusion
  195.1 0.1 reshape.57
  195.2 0.1 slice_reduce_fusion
  195.3 0.1 reduce_max.9
  195.4 0.2 exponential_reduce_fusion
  195.6 0.5 fusion
  196.1 0.1 sub.44
  196.2 0.1 sub.45
  196.3 1.7 gradients.1
  198.0 12.5 %all_gather.7 = bf16[4,48,8,128]{3,2,1,0:T(8,128)(2,1)S(1)} all-gather(bf16[1,48,8,128]{3,2,1,0:T(8,128)(2,1)S(1)} %bitcast.11), channel_id=1, replica_groups=mesh['index'=32,'rep'=4] {'rep'}, dimensions={0}, use_global_device_ids=true | all-gather | bytes 491520 | tf_op jit(solution)/shard_map/all_gather | solution.py:409
  210.5 0.8 copy.18
  (22 shorter events, 0.1 us)
Async XLA Ops:
  7.2 68.7 %all-gather.2.cloned.1.call-start = ((), (), s32[]{:S(2)}) async-start(), calls=%async_computation.2 | async-start | bytes 12976128 | tf_op jit(solution)/shard_map/all_gather | solution.py:321
  15.8 15.7 %all-to-all-start = ((s32[32,1,24]{2,1,0:T(1,128)}), s32[32,1,24]{2,1,0:T(1,128)S(1)}, u32[]{:S(2)}, u32[]{:S(2)}) async-start(s32[32,1,24]{2,1,0:T(1,128)} %bitcast), calls=%async_computation | async-start | bytes 32768 | tf_op jit(solution)/shard_map/all_to_all | solution.py:319
  75.9 4.6 %copy-start = (bf16[1536,32,128]{2,1,0:T(8,128)(2,1)S(1)}, bf16[1536,32,128]{2,1,0:T(8,128)(2,1)}, u32[]{:S(2)}) copy-start(bf16[1536,32,128]{2,1,0:T(8,128)(2,1)} %all-gather.2.cloned.1.call-done.refs_1_) | copy-start | bytes 37748740
  80.4 2.2 %copy-start.1 = (bf16[64,256,128]{2,1,0:T(8,128)(2,1)S(1)}, bf16[64,256,128]{2,1,0:T(8,128)(2,1)}, u32[]{:S(2)}) copy-start(bf16[64,256,128]{2,1,0:T(8,128)(2,1)} %refs_0_.3) | copy-start | bytes 12582916
  82.6 0.7 copy-start.2
  90.8 14.1 %collective-permute-start = (bf16[1632,128]{1,0:T(8,128)(2,1)S(1)}, bf16[1632,128]{1,0:T(8,128)(2,1)S(1)}, u32[]{:S(2)}, u32[]{:S(2)}) collective-permute-start(bf16[1632,128]{1,0:T(8,128)(2,1)S(1)} %get-tuple-element.30), channel_id=1, source_target_pairs={{0,1},{1,2},{2,3},{3,0},{4,5},{5,6},{6,7},{7,4},{8,9},{9,10},{10,1... | collective-permute-start | bytes 1253384 | tf_op jit(solution)/shard_map/ppermute | solution.py:343
  92.3 12.5 %collective-permute-start.1 = (bf16[1632,128]{1,0:T(8,128)(2,1)S(1)}, bf16[1632,128]{1,0:T(8,128)(2,1)S(1)}, u32[]{:S(2)}, u32[]{:S(2)}) collective-permute-start(bf16[1632,128]{1,0:T(8,128)(2,1)S(1)} %get-tuple-element.32), channel_id=1, source_target_pairs={{0,3},{1,0},{2,1},{3,2},{4,7},{5,4},{6,5},{7,6},{8,11},{9,8},{10,9... | collective-permute-start | bytes 1253384 | tf_op jit(solution)/shard_map/ppermute | solution.py:343
  101.6 13.8 %collective-permute-start.6 = (bf16[1632,128]{1,0:T(8,128)(2,1)S(1)}, bf16[1632,128]{1,0:T(8,128)(2,1)S(1)}, u32[]{:S(2)}, u32[]{:S(2)}) collective-permute-start(bf16[1632,128]{1,0:T(8,128)(2,1)S(1)} %get-tuple-element.42), channel_id=1, source_target_pairs={{0,1},{1,2},{2,3},{3,0},{4,5},{5,6},{6,7},{7,4},{8,9},{9,10},{10,1... | collective-permute-start | bytes 1253384 | tf_op jit(solution)/shard_map/ppermute | solution.py:343
  101.9 13.5 %collective-permute-start.7 = (bf16[1632,128]{1,0:T(8,128)(2,1)S(1)}, bf16[1632,128]{1,0:T(8,128)(2,1)S(1)}, u32[]{:S(2)}, u32[]{:S(2)}) collective-permute-start(bf16[1632,128]{1,0:T(8,128)(2,1)S(1)} %get-tuple-element.44), channel_id=1, source_target_pairs={{0,3},{1,0},{2,1},{3,2},{4,7},{5,4},{6,5},{7,6},{8,11},{9,8},{10,9... | collective-permute-start | bytes 1253384 | tf_op jit(solution)/shard_map/ppermute | solution.py:343
  106.2 18.1 %collective-permute-start.2 = (bf16[1632,128]{1,0:T(8,128)(2,1)S(1)}, bf16[1632,128]{1,0:T(8,128)(2,1)S(1)}, u32[]{:S(2)}, u32[]{:S(2)}) collective-permute-start(bf16[1632,128]{1,0:T(8,128)(2,1)S(1)} %get-tuple-element.34), channel_id=1, source_target_pairs={{0,1},{1,2},{2,3},{3,0},{4,5},{5,6},{6,7},{7,4},{8,9},{9,10},{10,1... | collective-permute-start | bytes 1253384 | tf_op jit(solution)/shard_map/ppermute | solution.py:343
  106.8 17.6 %collective-permute-start.3 = (bf16[1632,128]{1,0:T(8,128)(2,1)S(1)}, bf16[1632,128]{1,0:T(8,128)(2,1)S(1)}, u32[]{:S(2)}, u32[]{:S(2)}) collective-permute-start(bf16[1632,128]{1,0:T(8,128)(2,1)S(1)} %get-tuple-element.36), channel_id=1, source_target_pairs={{0,3},{1,0},{2,1},{3,2},{4,7},{5,4},{6,5},{7,6},{8,11},{9,8},{10,9... | collective-permute-start | bytes 1253384 | tf_op jit(solution)/shard_map/ppermute | solution.py:343
  116.8 16.5 %collective-permute-start.8 = (bf16[1632,128]{1,0:T(8,128)(2,1)S(1)}, bf16[1632,128]{1,0:T(8,128)(2,1)S(1)}, u32[]{:S(2)}, u32[]{:S(2)}) collective-permute-start(bf16[1632,128]{1,0:T(8,128)(2,1)S(1)} %get-tuple-element.46), channel_id=1, source_target_pairs={{0,1},{1,2},{2,3},{3,0},{4,5},{5,6},{6,7},{7,4},{8,9},{9,10},{10,1... | collective-permute-start | bytes 1253384 | tf_op jit(solution)/shard_map/ppermute | solution.py:343
  117.4 15.9 %collective-permute-start.9 = (bf16[1632,128]{1,0:T(8,128)(2,1)S(1)}, bf16[1632,128]{1,0:T(8,128)(2,1)S(1)}, u32[]{:S(2)}, u32[]{:S(2)}) collective-permute-start(bf16[1632,128]{1,0:T(8,128)(2,1)S(1)} %get-tuple-element.48), channel_id=1, source_target_pairs={{0,3},{1,0},{2,1},{3,2},{4,7},{5,4},{6,5},{7,6},{8,11},{9,8},{10,9... | collective-permute-start | bytes 1253384 | tf_op jit(solution)/shard_map/ppermute | solution.py:343
  125.7 16.5 %collective-permute-start.4 = (bf16[1632,128]{1,0:T(8,128)(2,1)S(1)}, bf16[1632,128]{1,0:T(8,128)(2,1)S(1)}, u32[]{:S(2)}, u32[]{:S(2)}) collective-permute-start(bf16[1632,128]{1,0:T(8,128)(2,1)S(1)} %get-tuple-element.38), channel_id=1, source_target_pairs={{0,1},{1,2},{2,3},{3,0},{4,5},{5,6},{6,7},{7,4},{8,9},{9,10},{10,1... | collective-permute-start | bytes 1253384 | tf_op jit(solution)/shard_map/ppermute | solution.py:343
  126.3 15.9 %collective-permute-start.5 = (bf16[1632,128]{1,0:T(8,128)(2,1)S(1)}, bf16[1632,128]{1,0:T(8,128)(2,1)S(1)}, u32[]{:S(2)}, u32[]{:S(2)}) collective-permute-start(bf16[1632,128]{1,0:T(8,128)(2,1)S(1)} %get-tuple-element.40), channel_id=1, source_target_pairs={{0,3},{1,0},{2,1},{3,2},{4,7},{5,4},{6,5},{7,6},{8,11},{9,8},{10,9... | collective-permute-start | bytes 1253384 | tf_op jit(solution)/shard_map/ppermute | solution.py:343
  134.7 15.2 %collective-permute-start.10 = (bf16[1632,128]{1,0:T(8,128)(2,1)S(1)}, bf16[1632,128]{1,0:T(8,128)(2,1)S(1)}, u32[]{:S(2)}, u32[]{:S(2)}) collective-permute-start(bf16[1632,128]{1,0:T(8,128)(2,1)S(1)} %get-tuple-element.50), channel_id=1, source_target_pairs={{0,1},{1,2},{2,3},{3,0},{4,5},{5,6},{6,7},{7,4},{8,9},{9,10},{10,1... | collective-permute-start | bytes 1253384 | tf_op jit(solution)/shard_map/ppermute | solution.py:343
  135.3 14.6 %collective-permute-start.11 = (bf16[1632,128]{1,0:T(8,128)(2,1)S(1)}, bf16[1632,128]{1,0:T(8,128)(2,1)S(1)}, u32[]{:S(2)}, u32[]{:S(2)}) collective-permute-start(bf16[1632,128]{1,0:T(8,128)(2,1)S(1)} %get-tuple-element.52), channel_id=1, source_target_pairs={{0,3},{1,0},{2,1},{3,2},{4,7},{5,4},{6,5},{7,6},{8,11},{9,8},{10,9... | collective-permute-start | bytes 1253384 | tf_op jit(solution)/shard_map/ppermute | solution.py:343
  153.8 5.6 %copy-start.4 = (s32[384]{0:T(512)S(1)}, s32[384]{0:T(512)}, u32[]{:S(2)}) copy-start(s32[384]{0:T(512)} %get-tuple-element.54) | copy-start | bytes 4612
  153.8 31.0 %all-to-all-start.1 = ((bf16[32,208,128]{2,1,0:T(8,128)(2,1)}), bf16[32,208,128]{2,1,0:T(8,128)(2,1)S(1)}, u32[]{:S(2)}, u32[]{:S(2)}) async-start(bf16[32,208,128]{2,1,0:T(8,128)(2,1)} %bitcast.2), calls=%async_computation.1 | async-start | bytes 3407872 | tf_op jit(solution)/shard_map/all_to_all | solution.py:386
  159.4 36.9 %copy-start.3 = (s32[384]{0:T(512)S(1)}, s32[384]{0:T(512)}, u32[]{:S(2)}) copy-start(s32[384]{0:T(512)} %get-tuple-element.55.place) | copy-start | bytes 4612
  185.3 5.2 %collective-permute-start.14 = (f32[768]{0:T(1024)S(1)}, f32[768]{0:T(1024)S(1)}, u32[]{:S(2)}, u32[]{:S(2)}) collective-permute-start(f32[768]{0:T(1024)S(1)} %reshape.56), channel_id=1, source_target_pairs={{0,2},{1,3},{2,0},{3,1},{4,6},{5,7},{6,4},{7,5},{8,10},{9,11},{10,... | collective-permute-start | bytes 9224 | tf_op jit(solution)/shard_map/ppermute | solution.py:343
  186.8 4.0 %collective-permute-start.13 = (f32[768]{0:T(1024)S(1)}, f32[768]{0:T(1024)S(1)}, u32[]{:S(2)}, u32[]{:S(2)}) collective-permute-start(f32[768]{0:T(1024)S(1)} %reshape.56), channel_id=1, source_target_pairs={{0,3},{1,0},{2,1},{3,2},{4,7},{5,4},{6,5},{7,6},{8,11},{9,8},{10,9... | collective-permute-start | bytes 9224 | tf_op jit(solution)/shard_map/ppermute | solution.py:343
  188.4 4.8 %collective-permute-start.12 = (f32[768]{0:T(1024)S(1)}, f32[768]{0:T(1024)S(1)}, u32[]{:S(2)}, u32[]{:S(2)}) collective-permute-start(f32[768]{0:T(1024)S(1)} %reshape.56), channel_id=1, source_target_pairs={{0,1},{1,2},{2,3},{3,0},{4,5},{5,6},{6,7},{7,4},{8,9},{9,10},{10,1... | collective-permute-start | bytes 9224 | tf_op jit(solution)/shard_map/ppermute | solution.py:343
Sparse Core Ops, SparseCore 0:
  10.2 65.5 all-gather.1

commit v5 on v4

--- a/solution.py
+++ b/solution.py
@@ -12,7 +12,7 @@
 LOSS_SCALE = 32.0
 NEG = -1e30
 BLOCK = 4
-UNROLL = 16
+UNROLL = 32
 CHUNKS = 2
 LANES = 128
 STRIDE = 256
@@ -147,7 +147,14 @@
     total_base = page_base + CHUNKS * blocks
     pages, held = refs[:2]
     outs = refs[2:10]
-    wide, stats = refs[10:]
+    wide, stats = refs[10:12]
+    if chunk == 0:
+        copies = [pltpu.make_async_copy(x, y, refs[14].at[k]) for k, (x, y) in enumerate(zip(refs[:2], refs[12:14], strict=True))]
+        for c in copies:
+            c.start()
+        for c in copies:
+            c.wait()
+        pages, held = refs[12:14]
     part = pages.shape[1]
     tokens = held.shape[1]
     share = tokens // 4
@@ -347,13 +354,14 @@
         parts = pl.pallas_call(
             functools.partial(pair_kernel, chunk, blocks, scale),
             out_shape=(jax.ShapeDtypeStruct((packed, feature), BF16),) * 8,
-            in_specs=[SMEM] * 3 + [VMEM] * 2,
+            in_specs=[SMEM] * 3 + [VMEM if chunk else ANY] * 2,
             out_specs=(VMEM,) * 8,
             scratch_shapes=[
                 pltpu.VMEM((4, 2 * STRIDE * share, feature), F32),
                 pltpu.VMEM((2, 2 * STRIDE // LANES, query_len, LANES), F32),
-            ],
-            compiler_params=params(28),
+            ]
+            + ([] if chunk else [pltpu.VMEM(x.shape, BF16) for x in (page_store, everyone)] + [pltpu.SemaphoreType.DMA((2,))]),
+            compiler_params=params(28 if chunk else 36),
             cost_estimate=pl.CostEstimate(flops=0, bytes_accessed=60_000_000, transcendentals=0),
             name="pairs",
         )(order, limits, me, page_store, everyone)

time: 220 us -> 219 us (level)
  Pallas kernels: 43.2 us -> 48.6 us
  local copies, waits for them, and re-layouts: 15 us -> 10.4 us
    pallas_call x2, Pallas kernels: 14.9 us -> 20.2 us  [per_device(): pl.pallas_call(functools.partial(pair_kernel, chunk, blocks, scale), out_...]
    unnamed x11, local copies, waits for them, and re-layouts: 8.24 us -> 3.67 us
where the time goes in v5:
time: 219 us
  waiting for transfers between devices  92.5 us (42%)
  Pallas kernels  48.6 us (22%)
  starting transfers between devices  38.2 us (17%)
  between operations  14.3 us (7%)
  blocking collectives  12.5 us (6%)
  local copies, waits for them, and re-layouts  10.4 us (5%)
  other arithmetic  2.33 us (1%)
    all_gather x1, waiting for transfers between devices, per_device(): everyone = lax.all_gather(queries, 'index', tiled=True)  30.1 us
    ppermute x15, waiting for transfers between devices, travel(): return lax.ppermute(x, 'rep', rep_pairs(step))  29.8 us
    all_to_all x1, waiting for transfers between devices, per_device(): lax.all_to_all(outgoing.reshape(groups, span, feature), 'index', split_ax...  25.3 us
    ppermute x15, starting transfers between devices, travel(): return lax.ppermute(x, 'rep', rep_pairs(step))  24.2 us
    pallas_call x2, Pallas kernels, per_device(): pl.pallas_call(functools.partial(pair_kernel, chunk, blocks, scale), out_...  20.2 us
    all_gather x1, blocking collectives, per_device(): lax.all_gather(quarter.reshape(query_count, share, feature), 'rep')  12.5 us
    pallas_call x1, Pallas kernels, per_device(): pl.pallas_call(functools.partial(sort_kernel, capacity, page_bits, query_...  12.3 us
    all_to_all x1, starting transfers between devices, per_device(): lax.all_to_all(table.reshape(groups, capacity), 'index', split_axis=0, co...  8.42 us
  transfers between devices with their start and end apart: 18, of which 11 were waited for; matrix products, arithmetic and copies ran while one was open for 2% of the time, Pallas kernels for 14%

profile of v5, /device:TPU:0, one launch (start us, length us, event | category | flops | bytes accessed | tf_op | source)
XLA Modules:
  0.0 218.9 jit_solution(10046628664814790200)
XLA Ops:
  7.2 0.0 all-gather.2.cloned.1.call-start
  7.2 0.7 all-gather.2.cloned.1.call-update
  7.9 0.8 copy.14
  8.7 0.7 reshape.51.listed
  9.3 5.1 %route.1 = (s32[768]{0:T(1024)}, s32[384]{0:T(512)}, s32[384]{0:T(512)}) custom-call(s32[384]{0:T(512)} %reshape.51.listed, s32[2048]{0:T(1024)} %page_slot.1), custom_call_target="tpu_custom_call" | custom-call | tf_op jit(solution)/shard_map/route/pallas_call | solution.py:318
  14.5 1.4 all_to_all.9
  15.8 8.4 %all-to-all-start = ((s32[32,1,24]{2,1,0:T(1,128)}), s32[32,1,24]{2,1,0:T(1,128)S(1)}, u32[]{:S(2)}, u32[]{:S(2)}) async-start(s32[32,1,24]{2,1,0:T(1,128)} %bitcast), calls=%async_computation | async-start | bytes 32768 | tf_op jit(solution)/shard_map/all_to_all | solution.py:326
  24.3 0.7 broadcast_subtract_fusion.limits
  24.9 6.6 %all-to-all-done = s32[32,1,24]{2,1,0:T(1,128)S(1)} async-done(((s32[32,1,24]{2,1,0:T(1,128)}), s32[32,1,24]{2,1,0:T(1,128)S(1)}, u32[]{:S(2)}, u32[]{:S(2)}) %all-to-all-start) | async-done | bytes 3104 | tf_op jit(solution)/shard_map/all_to_all | solution.py:326
  31.6 0.5 broadcast.22
  32.1 0.7 reduce.5
  32.8 0.7 reshape.52.arrived
  33.5 12.3 %sort_pairs.1.order = s32[2376]{0:T(1024)} custom-call(s32[768]{0:T(1024)} %reshape.52.arrived), custom_call_target="tpu_custom_call" | custom-call | bytes 40000000 | tf_op jit(solution)/shard_map/sort_pairs/pallas_call | solution.py:330
  45.8 30.1 %all-gather.2.cloned.1.call-done.refs_1_ = bf16[1536,32,128]{2,1,0:T(8,128)(2,1)} async-done(((bf16[48,32,128]{2,1,0:T(8,128)(2,1)}), bf16[1536,32,128]{2,1,0:T(8,128)(2,1)}) %all-gather.2.cloned.1.call-update) | async-done | bytes 12582928 | tf_op jit(solution)/shard_map/all_gather | solution.py:328
  75.9 2.2 copy-done.1
  78.1 0.7 copy-done.2
  78.8 12.6 %pairs.2 = (bf16[1632,128]{1,0:T(8,128)(2,1)S(1)}, bf16[1632,128]{1,0:T(8,128)(2,1)S(1)}, bf16[1632,128]{1,0:T(8,128)(2,1)S(1)}, bf16[1632,128]{1,0:T(8,128)(2,1...) custom-call(s32[2376]{0:T(1024)S(1)} %copy-done.2, ...), custom_call_target="tpu_custom_call" | custom-call | bytes 60000000 | tf_op jit(solution)/shard_map/pairs/pallas_call | solution.py:354
  91.4 1.5 collective-permute-start
  92.9 1.8 collective-permute-start.1
  94.7 7.6 %pairs.3 = (bf16[1632,128]{1,0:T(8,128)(2,1)S(1)}, bf16[1632,128]{1,0:T(8,128)(2,1)S(1)}, bf16[1632,128]{1,0:T(8,128)(2,1)S(1)}, bf16[1632,128]{1,0:T(8,128)(2,1...) custom-call(s32[2376]{0:T(1024)S(1)} %copy-done.2, ...), custom_call_target="tpu_custom_call" | custom-call | bytes 60000000 | tf_op jit(solution)/shard_map/pairs/pallas_call | solution.py:354
  102.2 0.3 collective-permute-start.6
  102.6 3.0 %collective-permute-start.7 = (bf16[1632,128]{1,0:T(8,128)(2,1)S(1)}, bf16[1632,128]{1,0:T(8,128)(2,1)S(1)}, u32[]{:S(2)}, u32[]{:S(2)}) collective-permute-start(bf16[1632,128]{1,0:T(8,128)(2,1)S(1)} %get-tuple-element.44), channel_id=1, source_target_pairs={{0,3},{1,0},{2,1},{3,2},{4,7},{5,4},{6,5},{7,6},{8,11},{9,8},{10,9... | collective-permute-start | bytes 1253384 | tf_op jit(solution)/shard_map/ppermute | solution.py:350
  105.6 1.4 merge.4
  106.9 0.4 collective-permute-start.2
  107.3 2.9 %collective-permute-start.3 = (bf16[1632,128]{1,0:T(8,128)(2,1)S(1)}, bf16[1632,128]{1,0:T(8,128)(2,1)S(1)}, u32[]{:S(2)}, u32[]{:S(2)}) collective-permute-start(bf16[1632,128]{1,0:T(8,128)(2,1)S(1)} %get-tuple-element.36), channel_id=1, source_target_pairs={{0,3},{1,0},{2,1},{3,2},{4,7},{5,4},{6,5},{7,6},{8,11},{9,8},{10,9... | collective-permute-start | bytes 1253384 | tf_op jit(solution)/shard_map/ppermute | solution.py:350
  110.2 5.8 %collective-permute-done.6.refs_0_ = bf16[1632,128]{1,0:T(8,128)(2,1)S(1)} collective-permute-done((bf16[1632,128]{1,0:T(8,128)(2,1)S(1)}, bf16[1632,128]{1,0:T(8,128)(2,1)S(1)}, u32[]{:S(2)}, u32[]{:S(2)}) %collective-permute-start.6) | collective-permute-done | bytes 417824 | tf_op jit(solution)/shard_map/ppermute | solution.py:350
  116.1 1.4 merge.6
  117.4 0.6 collective-permute-start.8
  118.1 3.0 %collective-permute-start.9 = (bf16[1632,128]{1,0:T(8,128)(2,1)S(1)}, bf16[1632,128]{1,0:T(8,128)(2,1)S(1)}, u32[]{:S(2)}, u32[]{:S(2)}) collective-permute-start(bf16[1632,128]{1,0:T(8,128)(2,1)S(1)} %get-tuple-element.48), channel_id=1, source_target_pairs={{0,3},{1,0},{2,1},{3,2},{4,7},{5,4},{6,5},{7,6},{8,11},{9,8},{10,9... | collective-permute-start | bytes 1253384 | tf_op jit(solution)/shard_map/ppermute | solution.py:350
  121.0 4.0 %collective-permute-done.2.refs_0_ = bf16[1632,128]{1,0:T(8,128)(2,1)S(1)} collective-permute-done((bf16[1632,128]{1,0:T(8,128)(2,1)S(1)}, bf16[1632,128]{1,0:T(8,128)(2,1)S(1)}, u32[]{:S(2)}, u32[]{:S(2)}) %collective-permute-start.2) | collective-permute-done | bytes 417824 | tf_op jit(solution)/shard_map/ppermute | solution.py:350
  125.0 1.4 merge.5
  126.4 0.6 collective-permute-start.4
  127.0 2.8 %collective-permute-start.5 = (bf16[1632,128]{1,0:T(8,128)(2,1)S(1)}, bf16[1632,128]{1,0:T(8,128)(2,1)S(1)}, u32[]{:S(2)}, u32[]{:S(2)}) collective-permute-start(bf16[1632,128]{1,0:T(8,128)(2,1)S(1)} %get-tuple-element.40), channel_id=1, source_target_pairs={{0,3},{1,0},{2,1},{3,2},{4,7},{5,4},{6,5},{7,6},{8,11},{9,8},{10,9... | collective-permute-start | bytes 1253384 | tf_op jit(solution)/shard_map/ppermute | solution.py:350
  129.8 4.2 %collective-permute-done.8.refs_0_ = bf16[1632,128]{1,0:T(8,128)(2,1)S(1)} collective-permute-done((bf16[1632,128]{1,0:T(8,128)(2,1)S(1)}, bf16[1632,128]{1,0:T(8,128)(2,1)S(1)}, u32[]{:S(2)}, u32[]{:S(2)}) %collective-permute-start.8) | collective-permute-done | bytes 417824 | tf_op jit(solution)/shard_map/ppermute | solution.py:350
  134.0 1.4 merge.7
  135.4 0.6 collective-permute-start.10
  136.0 2.8 %collective-permute-start.11 = (bf16[1632,128]{1,0:T(8,128)(2,1)S(1)}, bf16[1632,128]{1,0:T(8,128)(2,1)S(1)}, u32[]{:S(2)}, u32[]{:S(2)}) collective-permute-start(bf16[1632,128]{1,0:T(8,128)(2,1)S(1)} %get-tuple-element.52), channel_id=1, source_target_pairs={{0,3},{1,0},{2,1},{3,2},{4,7},{5,4},{6,5},{7,6},{8,11},{9,8},{10,9... | collective-permute-start | bytes 1253384 | tf_op jit(solution)/shard_map/ppermute | solution.py:350
  138.8 4.2 %collective-permute-done.4.refs_0_ = bf16[1632,128]{1,0:T(8,128)(2,1)S(1)} collective-permute-done((bf16[1632,128]{1,0:T(8,128)(2,1)S(1)}, bf16[1632,128]{1,0:T(8,128)(2,1)S(1)}, u32[]{:S(2)}, u32[]{:S(2)}) %collective-permute-start.4) | collective-permute-done | bytes 417824 | tf_op jit(solution)/shard_map/ppermute | solution.py:350
  142.9 7.6 %collective-permute-done.10.refs_4_ = bf16[1632,128]{1,0:T(8,128)(2,1)S(1)} collective-permute-done((bf16[1632,128]{1,0:T(8,128)(2,1)S(1)}, bf16[1632,128]{1,0:T(8,128)(2,1)S(1)}, u32[]{:S(2)}, u32[]{:S(2)}) %collective-permute-start.10) | collective-permute-done | bytes 417824 | tf_op jit(solution)/shard_map/ppermute | solution.py:350
  150.6 3.9 %merge_last.1 = bf16[6656,128]{1,0:T(8,128)(2,1)} custom-call(bf16[1632,128]{1,0:T(8,128)(2,1)S(1)} %collective-permute-done.4.refs_0_, bf16[1632,128]{1,0:T(8,128)(2,1)S(1)} %get-tuple-element.39.refs_1_, bf16[1632,128]{1,0:T(8,128)(2,1)S(1)} %collective-permute-done.5.refs_2_, bf16[1632,128]{1,0:T(8,128)(2,1)S(1)} %get-tuple-element.41.refs_3_, ...), custom_call_target="tpu_custom_call" | custom-call | tf_op jit(solution)/shard_map/merge_last/pallas_call | solution.py:386
  154.5 5.6 %all-to-all-start.1 = ((bf16[32,208,128]{2,1,0:T(8,128)(2,1)}), bf16[32,208,128]{2,1,0:T(8,128)(2,1)S(1)}, u32[]{:S(2)}, u32[]{:S(2)}) async-start(bf16[32,208,128]{2,1,0:T(8,128)(2,1)} %bitcast.2), calls=%async_computation.1 | async-start | bytes 3407872 | tf_op jit(solution)/shard_map/all_to_all | solution.py:394
  160.1 25.3 %all-to-all-done.1 = bf16[32,208,128]{2,1,0:T(8,128)(2,1)S(1)} async-done(((bf16[32,208,128]{2,1,0:T(8,128)(2,1)}), bf16[32,208,128]{2,1,0:T(8,128)(2,1)S(1)}, u32[]{:S(2)}, u32[]{:S(2)}) %all-to-all-start.1) | async-done | bytes 1703968 | tf_op jit(solution)/shard_map/all_to_all | solution.py:394
  185.5 0.1 reshape.61
  185.6 0.1 reduce_sum.18
  185.7 0.1 constant_dynamic-slice_fusion
  185.8 0.1 reshape.56
  185.9 1.5 collective-permute-start.14
  187.5 1.6 collective-permute-start.13
  189.0 0.8 collective-permute-start.12
  189.8 0.1 sub.48
  189.9 1.2 collective-permute-done.14
  191.1 0.3 collective-permute-done.13
  191.4 2.4 %collective-permute-done.12 = f32[768]{0:T(1024)S(1)} collective-permute-done((f32[768]{0:T(1024)S(1)}, f32[768]{0:T(1024)S(1)}, u32[]{:S(2)}, u32[]{:S(2)}) %collective-permute-start.12) | collective-permute-done | bytes 3104 | tf_op jit(solution)/shard_map/ppermute | solution.py:350
  193.9 1.9 gather_fusion
  195.8 0.1 reshape.57
  195.8 0.1 slice_reduce_fusion
  196.0 0.1 reduce_max.9
  196.1 0.2 exponential_reduce_fusion
  196.3 0.5 fusion
  196.8 0.1 sub.44
  196.9 0.1 sub.45
  197.0 1.7 gradients.1
  198.7 12.5 %all_gather.7 = bf16[4,48,8,128]{3,2,1,0:T(8,128)(2,1)S(1)} all-gather(bf16[1,48,8,128]{3,2,1,0:T(8,128)(2,1)S(1)} %bitcast.11), channel_id=1, replica_groups=mesh['index'=32,'rep'=4] {'rep'}, dimensions={0}, use_global_device_ids=true | all-gather | bytes 491520 | tf_op jit(solution)/shard_map/all_gather | solution.py:417
  211.2 0.8 copy.18
  (22 shorter events, 0.1 us)
Async XLA Ops:
  7.2 68.7 %all-gather.2.cloned.1.call-start = ((), (), s32[]{:S(2)}) async-start(), calls=%async_computation.2 | async-start | bytes 12976128 | tf_op jit(solution)/shard_map/all_gather | solution.py:328
  15.8 15.7 %all-to-all-start = ((s32[32,1,24]{2,1,0:T(1,128)}), s32[32,1,24]{2,1,0:T(1,128)S(1)}, u32[]{:S(2)}, u32[]{:S(2)}) async-start(s32[32,1,24]{2,1,0:T(1,128)} %bitcast), calls=%async_computation | async-start | bytes 32768 | tf_op jit(solution)/shard_map/all_to_all | solution.py:326
  75.9 2.2 copy-start.1
  78.1 0.7 copy-start.2
  78.8 15.9 %copy-start = (bf16[1536,32,128]{2,1,0:T(8,128)(2,1)S(1)}, bf16[1536,32,128]{2,1,0:T(8,128)(2,1)}, u32[]{:S(2)}) copy-start(bf16[1536,32,128]{2,1,0:T(8,128)(2,1)} %all-gather.2.cloned.1.call-done.refs_1_) | copy-start | bytes 37748740
  91.4 14.2 %collective-permute-start = (bf16[1632,128]{1,0:T(8,128)(2,1)S(1)}, bf16[1632,128]{1,0:T(8,128)(2,1)S(1)}, u32[]{:S(2)}, u32[]{:S(2)}) collective-permute-start(bf16[1632,128]{1,0:T(8,128)(2,1)S(1)} %get-tuple-element.30), channel_id=1, source_target_pairs={{0,1},{1,2},{2,3},{3,0},{4,5},{5,6},{6,7},{7,4},{8,9},{9,10},{10,1... | collective-permute-start | bytes 1253384 | tf_op jit(solution)/shard_map/ppermute | solution.py:350
  92.9 12.7 %collective-permute-start.1 = (bf16[1632,128]{1,0:T(8,128)(2,1)S(1)}, bf16[1632,128]{1,0:T(8,128)(2,1)S(1)}, u32[]{:S(2)}, u32[]{:S(2)}) collective-permute-start(bf16[1632,128]{1,0:T(8,128)(2,1)S(1)} %get-tuple-element.32), channel_id=1, source_target_pairs={{0,3},{1,0},{2,1},{3,2},{4,7},{5,4},{6,5},{7,6},{8,11},{9,8},{10,9... | collective-permute-start | bytes 1253384 | tf_op jit(solution)/shard_map/ppermute | solution.py:350
  102.2 13.8 %collective-permute-start.6 = (bf16[1632,128]{1,0:T(8,128)(2,1)S(1)}, bf16[1632,128]{1,0:T(8,128)(2,1)S(1)}, u32[]{:S(2)}, u32[]{:S(2)}) collective-permute-start(bf16[1632,128]{1,0:T(8,128)(2,1)S(1)} %get-tuple-element.42), channel_id=1, source_target_pairs={{0,1},{1,2},{2,3},{3,0},{4,5},{5,6},{6,7},{7,4},{8,9},{9,10},{10,1... | collective-permute-start | bytes 1253384 | tf_op jit(solution)/shard_map/ppermute | solution.py:350
  102.6 13.5 %collective-permute-start.7 = (bf16[1632,128]{1,0:T(8,128)(2,1)S(1)}, bf16[1632,128]{1,0:T(8,128)(2,1)S(1)}, u32[]{:S(2)}, u32[]{:S(2)}) collective-permute-start(bf16[1632,128]{1,0:T(8,128)(2,1)S(1)} %get-tuple-element.44), channel_id=1, source_target_pairs={{0,3},{1,0},{2,1},{3,2},{4,7},{5,4},{6,5},{7,6},{8,11},{9,8},{10,9... | collective-permute-start | bytes 1253384 | tf_op jit(solution)/shard_map/ppermute | solution.py:350
  106.9 18.1 %collective-permute-start.2 = (bf16[1632,128]{1,0:T(8,128)(2,1)S(1)}, bf16[1632,128]{1,0:T(8,128)(2,1)S(1)}, u32[]{:S(2)}, u32[]{:S(2)}) collective-permute-start(bf16[1632,128]{1,0:T(8,128)(2,1)S(1)} %get-tuple-element.34), channel_id=1, source_target_pairs={{0,1},{1,2},{2,3},{3,0},{4,5},{5,6},{6,7},{7,4},{8,9},{9,10},{10,1... | collective-permute-start | bytes 1253384 | tf_op jit(solution)/shard_map/ppermute | solution.py:350
  107.3 17.7 %collective-permute-start.3 = (bf16[1632,128]{1,0:T(8,128)(2,1)S(1)}, bf16[1632,128]{1,0:T(8,128)(2,1)S(1)}, u32[]{:S(2)}, u32[]{:S(2)}) collective-permute-start(bf16[1632,128]{1,0:T(8,128)(2,1)S(1)} %get-tuple-element.36), channel_id=1, source_target_pairs={{0,3},{1,0},{2,1},{3,2},{4,7},{5,4},{6,5},{7,6},{8,11},{9,8},{10,9... | collective-permute-start | bytes 1253384 | tf_op jit(solution)/shard_map/ppermute | solution.py:350
  117.4 16.5 %collective-permute-start.8 = (bf16[1632,128]{1,0:T(8,128)(2,1)S(1)}, bf16[1632,128]{1,0:T(8,128)(2,1)S(1)}, u32[]{:S(2)}, u32[]{:S(2)}) collective-permute-start(bf16[1632,128]{1,0:T(8,128)(2,1)S(1)} %get-tuple-element.46), channel_id=1, source_target_pairs={{0,1},{1,2},{2,3},{3,0},{4,5},{5,6},{6,7},{7,4},{8,9},{9,10},{10,1... | collective-permute-start | bytes 1253384 | tf_op jit(solution)/shard_map/ppermute | solution.py:350
  118.1 15.9 %collective-permute-start.9 = (bf16[1632,128]{1,0:T(8,128)(2,1)S(1)}, bf16[1632,128]{1,0:T(8,128)(2,1)S(1)}, u32[]{:S(2)}, u32[]{:S(2)}) collective-permute-start(bf16[1632,128]{1,0:T(8,128)(2,1)S(1)} %get-tuple-element.48), channel_id=1, source_target_pairs={{0,3},{1,0},{2,1},{3,2},{4,7},{5,4},{6,5},{7,6},{8,11},{9,8},{10,9... | collective-permute-start | bytes 1253384 | tf_op jit(solution)/shard_map/ppermute | solution.py:350
  126.4 16.5 %collective-permute-start.4 = (bf16[1632,128]{1,0:T(8,128)(2,1)S(1)}, bf16[1632,128]{1,0:T(8,128)(2,1)S(1)}, u32[]{:S(2)}, u32[]{:S(2)}) collective-permute-start(bf16[1632,128]{1,0:T(8,128)(2,1)S(1)} %get-tuple-element.38), channel_id=1, source_target_pairs={{0,1},{1,2},{2,3},{3,0},{4,5},{5,6},{6,7},{7,4},{8,9},{9,10},{10,1... | collective-permute-start | bytes 1253384 | tf_op jit(solution)/shard_map/ppermute | solution.py:350
  127.0 15.9 %collective-permute-start.5 = (bf16[1632,128]{1,0:T(8,128)(2,1)S(1)}, bf16[1632,128]{1,0:T(8,128)(2,1)S(1)}, u32[]{:S(2)}, u32[]{:S(2)}) collective-permute-start(bf16[1632,128]{1,0:T(8,128)(2,1)S(1)} %get-tuple-element.40), channel_id=1, source_target_pairs={{0,3},{1,0},{2,1},{3,2},{4,7},{5,4},{6,5},{7,6},{8,11},{9,8},{10,9... | collective-permute-start | bytes 1253384 | tf_op jit(solution)/shard_map/ppermute | solution.py:350
  135.4 15.2 %collective-permute-start.10 = (bf16[1632,128]{1,0:T(8,128)(2,1)S(1)}, bf16[1632,128]{1,0:T(8,128)(2,1)S(1)}, u32[]{:S(2)}, u32[]{:S(2)}) collective-permute-start(bf16[1632,128]{1,0:T(8,128)(2,1)S(1)} %get-tuple-element.50), channel_id=1, source_target_pairs={{0,1},{1,2},{2,3},{3,0},{4,5},{5,6},{6,7},{7,4},{8,9},{9,10},{10,1... | collective-permute-start | bytes 1253384 | tf_op jit(solution)/shard_map/ppermute | solution.py:350
  136.0 14.6 %collective-permute-start.11 = (bf16[1632,128]{1,0:T(8,128)(2,1)S(1)}, bf16[1632,128]{1,0:T(8,128)(2,1)S(1)}, u32[]{:S(2)}, u32[]{:S(2)}) collective-permute-start(bf16[1632,128]{1,0:T(8,128)(2,1)S(1)} %get-tuple-element.52), channel_id=1, source_target_pairs={{0,3},{1,0},{2,1},{3,2},{4,7},{5,4},{6,5},{7,6},{8,11},{9,8},{10,9... | collective-permute-start | bytes 1253384 | tf_op jit(solution)/shard_map/ppermute | solution.py:350
  154.5 5.6 %copy-start.4 = (s32[384]{0:T(512)S(1)}, s32[384]{0:T(512)}, u32[]{:S(2)}) copy-start(s32[384]{0:T(512)} %get-tuple-element.54) | copy-start | bytes 4612
  154.5 31.0 %all-to-all-start.1 = ((bf16[32,208,128]{2,1,0:T(8,128)(2,1)}), bf16[32,208,128]{2,1,0:T(8,128)(2,1)S(1)}, u32[]{:S(2)}, u32[]{:S(2)}) async-start(bf16[32,208,128]{2,1,0:T(8,128)(2,1)} %bitcast.2), calls=%async_computation.1 | async-start | bytes 3407872 | tf_op jit(solution)/shard_map/all_to_all | solution.py:394
  160.1 36.9 %copy-start.3 = (s32[384]{0:T(512)S(1)}, s32[384]{0:T(512)}, u32[]{:S(2)}) copy-start(s32[384]{0:T(512)} %get-tuple-element.55.place) | copy-start | bytes 4612
  185.9 5.2 %collective-permute-start.14 = (f32[768]{0:T(1024)S(1)}, f32[768]{0:T(1024)S(1)}, u32[]{:S(2)}, u32[]{:S(2)}) collective-permute-start(f32[768]{0:T(1024)S(1)} %reshape.56), channel_id=1, source_target_pairs={{0,2},{1,3},{2,0},{3,1},{4,6},{5,7},{6,4},{7,5},{8,10},{9,11},{10,... | collective-permute-start | bytes 9224 | tf_op jit(solution)/shard_map/ppermute | solution.py:350
  187.5 4.0 %collective-permute-start.13 = (f32[768]{0:T(1024)S(1)}, f32[768]{0:T(1024)S(1)}, u32[]{:S(2)}, u32[]{:S(2)}) collective-permute-start(f32[768]{0:T(1024)S(1)} %reshape.56), channel_id=1, source_target_pairs={{0,3},{1,0},{2,1},{3,2},{4,7},{5,4},{6,5},{7,6},{8,11},{9,8},{10,9... | collective-permute-start | bytes 9224 | tf_op jit(solution)/shard_map/ppermute | solution.py:350
  189.0 4.8 %collective-permute-start.12 = (f32[768]{0:T(1024)S(1)}, f32[768]{0:T(1024)S(1)}, u32[]{:S(2)}, u32[]{:S(2)}) collective-permute-start(f32[768]{0:T(1024)S(1)} %reshape.56), channel_id=1, source_target_pairs={{0,1},{1,2},{2,3},{3,0},{4,5},{5,6},{6,7},{7,4},{8,9},{9,10},{10,1... | collective-permute-start | bytes 9224 | tf_op jit(solution)/shard_map/ppermute | solution.py:350
Sparse Core Ops, SparseCore 0:
  10.2 65.5 all-gather.1

commit v6 on v4

--- a/solution.py
+++ b/solution.py
@@ -206,13 +206,13 @@
 
 
 def merge_kernel(last, root, share, sub, *refs):
-    n_in = 4 * CHUNKS if last else 4
+    n_in = 4
     ins = refs[:n_in]
-    outs = refs[n_in:]
+    outs = refs[-1:] if last == 2 else refs[n_in:]
     length = ins[0].shape[0] - 2 * PIECES * 2 * share
     span = 2 * sub * share + 2 * share
     for n in range(n_in // 2):
-        chunk, h = n // 2, n % 2
+        chunk, h = max(last - 1, 0), n % 2
         came, own = ins[2 * n], ins[2 * n + 1]
 
         def joined(ref, s):
@@ -229,9 +229,9 @@
             logs = TAU * (peak + jnp.log(total))
             rows = [jnp.sum(logs[k * share : (k + 1) * share], axis=0, keepdims=True) for k in range(2)]
             if chunk == 0:
-                kept = {**(kept if h else {}), h: rows}
+                outs[1][2 * h : 2 * h + 2, :] = jnp.concatenate(rows, axis=0)
             else:
-                both = jnp.concatenate(kept[h] + rows, axis=0)
+                both = jnp.concatenate([refs[n_in + 1][2 * h : 2 * h + 2, :]] + rows, axis=0)
                 tile = jnp.concatenate([x.astype(F32) for x in split(both)] + [both * 0.0], axis=0).astype(BF16)
                 sources = length // (sub * share)
                 for source in range(sources):
@@ -254,10 +254,15 @@
 
             rows = slice(at, at + 2 * share)
             value = came[rows, :].astype(F32) * factor(part_a) + own[rows, :].astype(F32) * factor(part_b)
-            if last:
+            if last == 1:
+                outs[0][h * length + pair * 2 * share : h * length + (pair + 1) * 2 * share, :] = value.astype(BF16)
+            elif last:
                 source, j = 2 * pair // sub, 2 * pair % sub
                 to = (h * (length // (sub * share)) + source) * span + (chunk * sub + j) * share
                 outs[0][to : to + 2 * share, :] = value.astype(BF16)
+                earlier = h * length + pair * 2 * share
+                to = to - sub * share
+                outs[0][to : to + 2 * share, :] = refs[n_in][earlier : earlier + 2 * share, :]
             else:
                 outs[h][rows, :] = value.astype(BF16)
 
@@ -363,10 +368,20 @@
             came = [travel(held[0], 1), travel(held[1], -1)]
             own = [parts[(2, 1, 0)[hop] * 2], parts[(2, 3, 0)[hop] * 2 + 1]]
             if hop == 2:
-                finals += [came[0], own[0], came[1], own[1]]
+                finals = [came[0], own[0], came[1], own[1], *finals]
+                if chunk == 0:
+                    finals = pl.pallas_call(
+                        functools.partial(merge_kernel, 1, root, share, sub),
+                        out_shape=(jax.ShapeDtypeStruct((2 * length, feature), BF16), jax.ShapeDtypeStruct((4, LANES), F32)),
+                        in_specs=[VMEM] * 4,
+                        out_specs=(VMEM,) * 2,
+                        compiler_params=params(24),
+                        cost_estimate=pl.CostEstimate(flops=0, bytes_accessed=8_000_000, transcendentals=0),
+                        name="merge_first",
+                    )(*finals)
                 break
             held = pl.pallas_call(
-                functools.partial(merge_kernel, False, root, share, sub),
+                functools.partial(merge_kernel, 0, root, share, sub),
                 out_shape=(jax.ShapeDtypeStruct((packed, feature), BF16),) * 2,
                 in_specs=[VMEM] * 4,
                 out_specs=(VMEM,) * 2,
@@ -376,9 +391,9 @@
             )(came[0], own[0], came[1], own[1])
     span = 2 * sub * share + 2 * share
     outgoing = pl.pallas_call(
-        functools.partial(merge_kernel, True, root, share, sub),
+        functools.partial(merge_kernel, 2, root, share, sub),
         out_shape=jax.ShapeDtypeStruct((groups * span, feature), BF16),
-        in_specs=[VMEM] * (4 * CHUNKS),
+        in_specs=[VMEM] * 6,
         out_specs=VMEM,
         compiler_params=params(24),
         name="merge_last",

time: 220 us -> 218 us (level)
    pallas_call x5 -> x6, Pallas kernels: 9.32 us -> 9.42 us  [the longest x4 5.44 us: per_device(): pl.pallas_call(functools.partial(merge_kernel, 0, root, share, sub), out_...]
  transfers between devices with their start and end apart: 18 -> 18, of which waited for: 11 -> 9; matrix products, arithmetic and copies ran while one was open for 2% -> 2% of each run, Pallas kernels for 14% -> 14%
where the time goes in v6:
time: 218 us
  waiting for transfers between devices  91 us (42%)
  Pallas kernels  43.3 us (20%)
  starting transfers between devices  40 us (18%)
  local copies, waits for them, and re-layouts  14.9 us (7%)
  between operations  14.3 us (7%)
  blocking collectives  12.5 us (6%)
  other arithmetic  2.33 us (1%)
    all_gather x1, waiting for transfers between devices, per_device(): everyone = lax.all_gather(queries, 'index', tiled=True)  30.2 us
    ppermute x15, waiting for transfers between devices, travel(): return lax.ppermute(x, 'rep', rep_pairs(step))  28.1 us
    all_to_all x1, waiting for transfers between devices, per_device(): lax.all_to_all(outgoing.reshape(groups, span, feature), 'index', split_ax...  25.3 us
    ppermute x15, starting transfers between devices, travel(): return lax.ppermute(x, 'rep', rep_pairs(step))  25.1 us
    pallas_call x2, Pallas kernels, per_device(): pl.pallas_call(functools.partial(pair_kernel, chunk, blocks, scale), out_...  14.9 us
    all_gather x1, blocking collectives, per_device(): lax.all_gather(quarter.reshape(query_count, share, feature), 'rep')  12.5 us
    pallas_call x1, Pallas kernels, per_device(): pl.pallas_call(functools.partial(sort_kernel, capacity, page_bits, query_...  12.2 us
    all_to_all x1, starting transfers between devices, per_device(): lax.all_to_all(table.reshape(groups, capacity), 'index', split_axis=0, co...  8.42 us
  transfers between devices with their start and end apart: 18, of which 9 were waited for; matrix products, arithmetic and copies ran while one was open for 2% of the time, Pallas kernels for 14%

profile of v6, /device:TPU:0, one launch (start us, length us, event | category | flops | bytes accessed | tf_op | source)
XLA Modules:
  0.0 218.4 jit_solution(3502432106282187280)
XLA Ops:
  7.2 0.0 all-gather.2.cloned.1.call-start
  7.2 0.7 all-gather.2.cloned.1.call-update
  7.9 0.8 copy.14
  8.7 0.7 reshape.51.listed
  9.3 5.1 %route.1 = (s32[768]{0:T(1024)}, s32[384]{0:T(512)}, s32[384]{0:T(512)}) custom-call(s32[384]{0:T(512)} %reshape.51.listed, s32[2048]{0:T(1024)} %page_slot.1), custom_call_target="tpu_custom_call" | custom-call | tf_op jit(solution)/shard_map/route/pallas_call | solution.py:316
  14.5 1.4 all_to_all.9
  15.8 8.4 %all-to-all-start = ((s32[32,1,24]{2,1,0:T(1,128)}), s32[32,1,24]{2,1,0:T(1,128)S(1)}, u32[]{:S(2)}, u32[]{:S(2)}) async-start(s32[32,1,24]{2,1,0:T(1,128)} %bitcast), calls=%async_computation | async-start | bytes 32768 | tf_op jit(solution)/shard_map/all_to_all | solution.py:324
  24.3 0.7 broadcast_subtract_fusion.limits
  24.9 6.6 %all-to-all-done = s32[32,1,24]{2,1,0:T(1,128)S(1)} async-done(((s32[32,1,24]{2,1,0:T(1,128)}), s32[32,1,24]{2,1,0:T(1,128)S(1)}, u32[]{:S(2)}, u32[]{:S(2)}) %all-to-all-start) | async-done | bytes 3104 | tf_op jit(solution)/shard_map/all_to_all | solution.py:324
  31.6 0.5 broadcast.22
  32.1 0.7 reduce.5
  32.8 0.7 reshape.52.arrived
  33.5 12.2 %sort_pairs.1.order = s32[2216]{0:T(1024)} custom-call(s32[768]{0:T(1024)} %reshape.52.arrived), custom_call_target="tpu_custom_call" | custom-call | bytes 40000000 | tf_op jit(solution)/shard_map/sort_pairs/pallas_call | solution.py:328
  45.6 30.2 %all-gather.2.cloned.1.call-done.refs_1_ = bf16[1536,32,128]{2,1,0:T(8,128)(2,1)} async-done(((bf16[48,32,128]{2,1,0:T(8,128)(2,1)}), bf16[1536,32,128]{2,1,0:T(8,128)(2,1)}) %all-gather.2.cloned.1.call-update) | async-done | bytes 12582928 | tf_op jit(solution)/shard_map/all_gather | solution.py:326
  75.9 4.6 %copy-done = bf16[1536,32,128]{2,1,0:T(8,128)(2,1)S(1)} copy-done((bf16[1536,32,128]{2,1,0:T(8,128)(2,1)S(1)}, bf16[1536,32,128]{2,1,0:T(8,128)(2,1)}, u32[]{:S(2)}) %copy-start) | copy-done | bytes 12582936
  80.4 2.2 %copy-done.1 = bf16[64,256,128]{2,1,0:T(8,128)(2,1)S(1)} copy-done((bf16[64,256,128]{2,1,0:T(8,128)(2,1)S(1)}, bf16[64,256,128]{2,1,0:T(8,128)(2,1)}, u32[]{:S(2)}) %copy-start.1) | copy-done | bytes 4194328
  82.6 0.7 copy-done.2
  83.3 7.4 %pairs.3 = (bf16[1632,128]{1,0:T(8,128)(2,1)S(1)}, bf16[1632,128]{1,0:T(8,128)(2,1)S(1)}, bf16[1632,128]{1,0:T(8,128)(2,1)S(1)}, bf16[1632,128]{1,0:T(8,128)(2,1...) custom-call(s32[2216]{0:T(1024)S(1)} %copy-done.2, ...), custom_call_target="tpu_custom_call" | custom-call | bytes 60000000 | tf_op jit(solution)/shard_map/pairs/pallas_call | solution.py:352
  90.8 1.5 collective-permute-start.6
  92.3 1.8 collective-permute-start.7
  94.1 7.5 %pairs.2 = (bf16[1632,128]{1,0:T(8,128)(2,1)S(1)}, bf16[1632,128]{1,0:T(8,128)(2,1)S(1)}, bf16[1632,128]{1,0:T(8,128)(2,1)S(1)}, bf16[1632,128]{1,0:T(8,128)(2,1...) custom-call(s32[2216]{0:T(1024)S(1)} %copy-done.2, ...), custom_call_target="tpu_custom_call" | custom-call | bytes 60000000 | tf_op jit(solution)/shard_map/pairs/pallas_call | solution.py:352
  101.5 0.3 collective-permute-start
  101.9 3.0 %collective-permute-start.1 = (bf16[1632,128]{1,0:T(8,128)(2,1)S(1)}, bf16[1632,128]{1,0:T(8,128)(2,1)S(1)}, u32[]{:S(2)}, u32[]{:S(2)}) collective-permute-start(bf16[1632,128]{1,0:T(8,128)(2,1)S(1)} %get-tuple-element.34), channel_id=1, source_target_pairs={{0,3},{1,0},{2,1},{3,2},{4,7},{5,4},{6,5},{7,6},{8,11},{9,8},{10,9... | collective-permute-start | bytes 1253384 | tf_op jit(solution)/shard_map/ppermute | solution.py:348
  104.9 1.4 merge.6
  106.2 0.5 collective-permute-start.8
  106.8 2.8 %collective-permute-start.9 = (bf16[1632,128]{1,0:T(8,128)(2,1)S(1)}, bf16[1632,128]{1,0:T(8,128)(2,1)S(1)}, u32[]{:S(2)}, u32[]{:S(2)}) collective-permute-start(bf16[1632,128]{1,0:T(8,128)(2,1)S(1)} %get-tuple-element.50), channel_id=1, source_target_pairs={{0,3},{1,0},{2,1},{3,2},{4,7},{5,4},{6,5},{7,6},{8,11},{9,8},{10,9... | collective-permute-start | bytes 1253384 | tf_op jit(solution)/shard_map/ppermute | solution.py:348
  109.5 5.8 %collective-permute-done.refs_0_ = bf16[1632,128]{1,0:T(8,128)(2,1)S(1)} collective-permute-done((bf16[1632,128]{1,0:T(8,128)(2,1)S(1)}, bf16[1632,128]{1,0:T(8,128)(2,1)S(1)}, u32[]{:S(2)}, u32[]{:S(2)}) %collective-permute-start) | collective-permute-done | bytes 417824 | tf_op jit(solution)/shard_map/ppermute | solution.py:348
  115.4 1.4 merge.4
  116.7 0.6 collective-permute-start.2
  117.4 2.8 %collective-permute-start.3 = (bf16[1632,128]{1,0:T(8,128)(2,1)S(1)}, bf16[1632,128]{1,0:T(8,128)(2,1)S(1)}, u32[]{:S(2)}, u32[]{:S(2)}) collective-permute-start(bf16[1632,128]{1,0:T(8,128)(2,1)S(1)} %get-tuple-element.38), channel_id=1, source_target_pairs={{0,3},{1,0},{2,1},{3,2},{4,7},{5,4},{6,5},{7,6},{8,11},{9,8},{10,9... | collective-permute-start | bytes 1253384 | tf_op jit(solution)/shard_map/ppermute | solution.py:348
  120.2 4.2 %collective-permute-done.8.refs_0_ = bf16[1632,128]{1,0:T(8,128)(2,1)S(1)} collective-permute-done((bf16[1632,128]{1,0:T(8,128)(2,1)S(1)}, bf16[1632,128]{1,0:T(8,128)(2,1)S(1)}, u32[]{:S(2)}, u32[]{:S(2)}) %collective-permute-start.8) | collective-permute-done | bytes 417824 | tf_op jit(solution)/shard_map/ppermute | solution.py:348
  124.3 1.4 merge.7
  125.7 0.6 collective-permute-start.10
  126.3 3.0 %collective-permute-start.11 = (bf16[1632,128]{1,0:T(8,128)(2,1)S(1)}, bf16[1632,128]{1,0:T(8,128)(2,1)S(1)}, u32[]{:S(2)}, u32[]{:S(2)}) collective-permute-start(bf16[1632,128]{1,0:T(8,128)(2,1)S(1)} %get-tuple-element.54), channel_id=1, source_target_pairs={{0,3},{1,0},{2,1},{3,2},{4,7},{5,4},{6,5},{7,6},{8,11},{9,8},{10,9... | collective-permute-start | bytes 1253384 | tf_op jit(solution)/shard_map/ppermute | solution.py:348
  129.3 4.0 %collective-permute-done.2.refs_0_ = bf16[1632,128]{1,0:T(8,128)(2,1)S(1)} collective-permute-done((bf16[1632,128]{1,0:T(8,128)(2,1)S(1)}, bf16[1632,128]{1,0:T(8,128)(2,1)S(1)}, u32[]{:S(2)}, u32[]{:S(2)}) %collective-permute-start.2) | collective-permute-done | bytes 417824 | tf_op jit(solution)/shard_map/ppermute | solution.py:348
  133.3 1.4 merge.5
  134.6 0.6 collective-permute-start.4
  135.3 2.8 %collective-permute-start.5 = (bf16[1632,128]{1,0:T(8,128)(2,1)S(1)}, bf16[1632,128]{1,0:T(8,128)(2,1)S(1)}, u32[]{:S(2)}, u32[]{:S(2)}) collective-permute-start(bf16[1632,128]{1,0:T(8,128)(2,1)S(1)} %get-tuple-element.42), channel_id=1, source_target_pairs={{0,3},{1,0},{2,1},{3,2},{4,7},{5,4},{6,5},{7,6},{8,11},{9,8},{10,9... | collective-permute-start | bytes 1253384 | tf_op jit(solution)/shard_map/ppermute | solution.py:348
  138.1 4.2 %collective-permute-done.10.refs_0_ = bf16[1632,128]{1,0:T(8,128)(2,1)S(1)} collective-permute-done((bf16[1632,128]{1,0:T(8,128)(2,1)S(1)}, bf16[1632,128]{1,0:T(8,128)(2,1)S(1)}, u32[]{:S(2)}, u32[]{:S(2)}) %collective-permute-start.10) | collective-permute-done | bytes 417824 | tf_op jit(solution)/shard_map/ppermute | solution.py:348
  142.2 1.4 merge_first.1
  143.6 6.3 %collective-permute-done.4.refs_0_ = bf16[1632,128]{1,0:T(8,128)(2,1)S(1)} collective-permute-done((bf16[1632,128]{1,0:T(8,128)(2,1)S(1)}, bf16[1632,128]{1,0:T(8,128)(2,1)S(1)}, u32[]{:S(2)}, u32[]{:S(2)}) %collective-permute-start.4) | collective-permute-done | bytes 417824 | tf_op jit(solution)/shard_map/ppermute | solution.py:348
  149.9 2.6 %merge_last.1 = bf16[6656,128]{1,0:T(8,128)(2,1)} custom-call(bf16[1632,128]{1,0:T(8,128)(2,1)S(1)} %collective-permute-done.4.refs_0_, bf16[1632,128]{1,0:T(8,128)(2,1)S(1)} %get-tuple-element.41.refs_1_, bf16[1632,128]{1,0:T(8,128)(2,1)S(1)} %collective-permute-done.5.refs_2_, bf16[1632,128]{1,0:T(8,128)(2,1)S(1)} %get-tuple-element.43.refs_3_, ...), custom_call_target="tpu_custom_call" | custom-call | tf_op jit(solution)/shard_map/merge_last/pallas_call | solution.py:393
  152.5 6.5 %all-to-all-start.1 = ((bf16[32,208,128]{2,1,0:T(8,128)(2,1)}), bf16[32,208,128]{2,1,0:T(8,128)(2,1)S(1)}, u32[]{:S(2)}, u32[]{:S(2)}) async-start(bf16[32,208,128]{2,1,0:T(8,128)(2,1)} %bitcast.2), calls=%async_computation.1 | async-start | bytes 3407872 | tf_op jit(solution)/shard_map/all_to_all | solution.py:401
  159.0 25.3 %all-to-all-done.1 = bf16[32,208,128]{2,1,0:T(8,128)(2,1)S(1)} async-done(((bf16[32,208,128]{2,1,0:T(8,128)(2,1)}), bf16[32,208,128]{2,1,0:T(8,128)(2,1)S(1)}, u32[]{:S(2)}, u32[]{:S(2)}) %all-to-all-start.1) | async-done | bytes 1703968 | tf_op jit(solution)/shard_map/all_to_all | solution.py:401
  184.4 0.1 reshape.61
  184.5 0.1 reduce_sum.18
  184.6 0.1 constant_dynamic-slice_fusion
  184.7 0.1 reshape.56
  184.9 0.4 collective-permute-start.12
  185.2 3.0 %collective-permute-start.13 = (f32[768]{0:T(1024)S(1)}, f32[768]{0:T(1024)S(1)}, u32[]{:S(2)}, u32[]{:S(2)}) collective-permute-start(f32[768]{0:T(1024)S(1)} %reshape.56), channel_id=1, source_target_pairs={{0,3},{1,0},{2,1},{3,2},{4,7},{5,4},{6,5},{7,6},{8,11},{9,8},{10,9... | collective-permute-start | bytes 9224 | tf_op jit(solution)/shard_map/ppermute | solution.py:348
  188.2 1.4 collective-permute-start.14
  189.6 0.1 sub.48
  189.8 3.6 %collective-permute-done.14 = f32[768]{0:T(1024)S(1)} collective-permute-done((f32[768]{0:T(1024)S(1)}, f32[768]{0:T(1024)S(1)}, u32[]{:S(2)}, u32[]{:S(2)}) %collective-permute-start.14) | collective-permute-done | bytes 3104 | tf_op jit(solution)/shard_map/ppermute | solution.py:348
  193.4 1.9 gather_fusion
  195.3 0.1 reshape.57
  195.3 0.1 slice_reduce_fusion
  195.5 0.1 reduce_max.9
  195.6 0.2 exponential_reduce_fusion
  195.8 0.5 fusion
  196.3 0.1 sub.44
  196.4 0.1 sub.45
  196.5 1.7 gradients.1
  198.2 12.5 %all_gather.7 = bf16[4,48,8,128]{3,2,1,0:T(8,128)(2,1)S(1)} all-gather(bf16[1,48,8,128]{3,2,1,0:T(8,128)(2,1)S(1)} %bitcast.11), channel_id=1, replica_groups=mesh['index'=32,'rep'=4] {'rep'}, dimensions={0}, use_global_device_ids=true | all-gather | bytes 491520 | tf_op jit(solution)/shard_map/all_gather | solution.py:424
  210.7 0.8 copy.18
  (23 shorter events, 0.1 us)
Async XLA Ops:
  7.2 68.7 %all-gather.2.cloned.1.call-start = ((), (), s32[]{:S(2)}) async-start(), calls=%async_computation.2 | async-start | bytes 12976128 | tf_op jit(solution)/shard_map/all_gather | solution.py:326
  15.8 15.7 %all-to-all-start = ((s32[32,1,24]{2,1,0:T(1,128)}), s32[32,1,24]{2,1,0:T(1,128)S(1)}, u32[]{:S(2)}, u32[]{:S(2)}) async-start(s32[32,1,24]{2,1,0:T(1,128)} %bitcast), calls=%async_computation | async-start | bytes 32768 | tf_op jit(solution)/shard_map/all_to_all | solution.py:324
  75.9 4.6 %copy-start = (bf16[1536,32,128]{2,1,0:T(8,128)(2,1)S(1)}, bf16[1536,32,128]{2,1,0:T(8,128)(2,1)}, u32[]{:S(2)}) copy-start(bf16[1536,32,128]{2,1,0:T(8,128)(2,1)} %all-gather.2.cloned.1.call-done.refs_1_) | copy-start | bytes 37748740
  80.4 2.2 %copy-start.1 = (bf16[64,256,128]{2,1,0:T(8,128)(2,1)S(1)}, bf16[64,256,128]{2,1,0:T(8,128)(2,1)}, u32[]{:S(2)}) copy-start(bf16[64,256,128]{2,1,0:T(8,128)(2,1)} %refs_0_.3) | copy-start | bytes 12582916
  82.6 0.7 copy-start.2
  90.8 14.1 %collective-permute-start.6 = (bf16[1632,128]{1,0:T(8,128)(2,1)S(1)}, bf16[1632,128]{1,0:T(8,128)(2,1)S(1)}, u32[]{:S(2)}, u32[]{:S(2)}) collective-permute-start(bf16[1632,128]{1,0:T(8,128)(2,1)S(1)} %get-tuple-element.44), channel_id=1, source_target_pairs={{0,1},{1,2},{2,3},{3,0},{4,5},{5,6},{6,7},{7,4},{8,9},{9,10},{10,1... | collective-permute-start | bytes 1253384 | tf_op jit(solution)/shard_map/ppermute | solution.py:348
  92.3 12.5 %collective-permute-start.7 = (bf16[1632,128]{1,0:T(8,128)(2,1)S(1)}, bf16[1632,128]{1,0:T(8,128)(2,1)S(1)}, u32[]{:S(2)}, u32[]{:S(2)}) collective-permute-start(bf16[1632,128]{1,0:T(8,128)(2,1)S(1)} %get-tuple-element.46), channel_id=1, source_target_pairs={{0,3},{1,0},{2,1},{3,2},{4,7},{5,4},{6,5},{7,6},{8,11},{9,8},{10,9... | collective-permute-start | bytes 1253384 | tf_op jit(solution)/shard_map/ppermute | solution.py:348
  101.5 13.8 %collective-permute-start = (bf16[1632,128]{1,0:T(8,128)(2,1)S(1)}, bf16[1632,128]{1,0:T(8,128)(2,1)S(1)}, u32[]{:S(2)}, u32[]{:S(2)}) collective-permute-start(bf16[1632,128]{1,0:T(8,128)(2,1)S(1)} %get-tuple-element.32), channel_id=1, source_target_pairs={{0,1},{1,2},{2,3},{3,0},{4,5},{5,6},{6,7},{7,4},{8,9},{9,10},{10,1... | collective-permute-start | bytes 1253384 | tf_op jit(solution)/shard_map/ppermute | solution.py:348
  101.9 13.5 %collective-permute-start.1 = (bf16[1632,128]{1,0:T(8,128)(2,1)S(1)}, bf16[1632,128]{1,0:T(8,128)(2,1)S(1)}, u32[]{:S(2)}, u32[]{:S(2)}) collective-permute-start(bf16[1632,128]{1,0:T(8,128)(2,1)S(1)} %get-tuple-element.34), channel_id=1, source_target_pairs={{0,3},{1,0},{2,1},{3,2},{4,7},{5,4},{6,5},{7,6},{8,11},{9,8},{10,9... | collective-permute-start | bytes 1253384 | tf_op jit(solution)/shard_map/ppermute | solution.py:348
  106.2 18.1 %collective-permute-start.8 = (bf16[1632,128]{1,0:T(8,128)(2,1)S(1)}, bf16[1632,128]{1,0:T(8,128)(2,1)S(1)}, u32[]{:S(2)}, u32[]{:S(2)}) collective-permute-start(bf16[1632,128]{1,0:T(8,128)(2,1)S(1)} %get-tuple-element.48), channel_id=1, source_target_pairs={{0,1},{1,2},{2,3},{3,0},{4,5},{5,6},{6,7},{7,4},{8,9},{9,10},{10,1... | collective-permute-start | bytes 1253384 | tf_op jit(solution)/shard_map/ppermute | solution.py:348
  106.8 17.6 %collective-permute-start.9 = (bf16[1632,128]{1,0:T(8,128)(2,1)S(1)}, bf16[1632,128]{1,0:T(8,128)(2,1)S(1)}, u32[]{:S(2)}, u32[]{:S(2)}) collective-permute-start(bf16[1632,128]{1,0:T(8,128)(2,1)S(1)} %get-tuple-element.50), channel_id=1, source_target_pairs={{0,3},{1,0},{2,1},{3,2},{4,7},{5,4},{6,5},{7,6},{8,11},{9,8},{10,9... | collective-permute-start | bytes 1253384 | tf_op jit(solution)/shard_map/ppermute | solution.py:348
  116.7 16.5 %collective-permute-start.2 = (bf16[1632,128]{1,0:T(8,128)(2,1)S(1)}, bf16[1632,128]{1,0:T(8,128)(2,1)S(1)}, u32[]{:S(2)}, u32[]{:S(2)}) collective-permute-start(bf16[1632,128]{1,0:T(8,128)(2,1)S(1)} %get-tuple-element.36), channel_id=1, source_target_pairs={{0,1},{1,2},{2,3},{3,0},{4,5},{5,6},{6,7},{7,4},{8,9},{9,10},{10,1... | collective-permute-start | bytes 1253384 | tf_op jit(solution)/shard_map/ppermute | solution.py:348
  117.4 15.9 %collective-permute-start.3 = (bf16[1632,128]{1,0:T(8,128)(2,1)S(1)}, bf16[1632,128]{1,0:T(8,128)(2,1)S(1)}, u32[]{:S(2)}, u32[]{:S(2)}) collective-permute-start(bf16[1632,128]{1,0:T(8,128)(2,1)S(1)} %get-tuple-element.38), channel_id=1, source_target_pairs={{0,3},{1,0},{2,1},{3,2},{4,7},{5,4},{6,5},{7,6},{8,11},{9,8},{10,9... | collective-permute-start | bytes 1253384 | tf_op jit(solution)/shard_map/ppermute | solution.py:348
  125.7 16.5 %collective-permute-start.10 = (bf16[1632,128]{1,0:T(8,128)(2,1)S(1)}, bf16[1632,128]{1,0:T(8,128)(2,1)S(1)}, u32[]{:S(2)}, u32[]{:S(2)}) collective-permute-start(bf16[1632,128]{1,0:T(8,128)(2,1)S(1)} %get-tuple-element.52), channel_id=1, source_target_pairs={{0,1},{1,2},{2,3},{3,0},{4,5},{5,6},{6,7},{7,4},{8,9},{9,10},{10,1... | collective-permute-start | bytes 1253384 | tf_op jit(solution)/shard_map/ppermute | solution.py:348
  126.3 15.9 %collective-permute-start.11 = (bf16[1632,128]{1,0:T(8,128)(2,1)S(1)}, bf16[1632,128]{1,0:T(8,128)(2,1)S(1)}, u32[]{:S(2)}, u32[]{:S(2)}) collective-permute-start(bf16[1632,128]{1,0:T(8,128)(2,1)S(1)} %get-tuple-element.54), channel_id=1, source_target_pairs={{0,3},{1,0},{2,1},{3,2},{4,7},{5,4},{6,5},{7,6},{8,11},{9,8},{10,9... | collective-permute-start | bytes 1253384 | tf_op jit(solution)/shard_map/ppermute | solution.py:348
  134.6 15.2 %collective-permute-start.4 = (bf16[1632,128]{1,0:T(8,128)(2,1)S(1)}, bf16[1632,128]{1,0:T(8,128)(2,1)S(1)}, u32[]{:S(2)}, u32[]{:S(2)}) collective-permute-start(bf16[1632,128]{1,0:T(8,128)(2,1)S(1)} %get-tuple-element.40), channel_id=1, source_target_pairs={{0,1},{1,2},{2,3},{3,0},{4,5},{5,6},{6,7},{7,4},{8,9},{9,10},{10,1... | collective-permute-start | bytes 1253384 | tf_op jit(solution)/shard_map/ppermute | solution.py:348
  135.3 14.6 %collective-permute-start.5 = (bf16[1632,128]{1,0:T(8,128)(2,1)S(1)}, bf16[1632,128]{1,0:T(8,128)(2,1)S(1)}, u32[]{:S(2)}, u32[]{:S(2)}) collective-permute-start(bf16[1632,128]{1,0:T(8,128)(2,1)S(1)} %get-tuple-element.42), channel_id=1, source_target_pairs={{0,3},{1,0},{2,1},{3,2},{4,7},{5,4},{6,5},{7,6},{8,11},{9,8},{10,9... | collective-permute-start | bytes 1253384 | tf_op jit(solution)/shard_map/ppermute | solution.py:348
  152.5 6.5 %copy-start.4 = (s32[384]{0:T(512)S(1)}, s32[384]{0:T(512)}, u32[]{:S(2)}) copy-start(s32[384]{0:T(512)} %get-tuple-element.58) | copy-start | bytes 4612
  152.5 31.9 %all-to-all-start.1 = ((bf16[32,208,128]{2,1,0:T(8,128)(2,1)}), bf16[32,208,128]{2,1,0:T(8,128)(2,1)S(1)}, u32[]{:S(2)}, u32[]{:S(2)}) async-start(bf16[32,208,128]{2,1,0:T(8,128)(2,1)} %bitcast.2), calls=%async_computation.1 | async-start | bytes 3407872 | tf_op jit(solution)/shard_map/all_to_all | solution.py:401
  159.0 37.5 %copy-start.3 = (s32[384]{0:T(512)S(1)}, s32[384]{0:T(512)}, u32[]{:S(2)}) copy-start(s32[384]{0:T(512)} %get-tuple-element.59.place) | copy-start | bytes 4612
  184.9 4.9 %collective-permute-start.12 = (f32[768]{0:T(1024)S(1)}, f32[768]{0:T(1024)S(1)}, u32[]{:S(2)}, u32[]{:S(2)}) collective-permute-start(f32[768]{0:T(1024)S(1)} %reshape.56), channel_id=1, source_target_pairs={{0,1},{1,2},{2,3},{3,0},{4,5},{5,6},{6,7},{7,4},{8,9},{9,10},{10,1... | collective-permute-start | bytes 9224 | tf_op jit(solution)/shard_map/ppermute | solution.py:348
  185.2 4.5 %collective-permute-start.13 = (f32[768]{0:T(1024)S(1)}, f32[768]{0:T(1024)S(1)}, u32[]{:S(2)}, u32[]{:S(2)}) collective-permute-start(f32[768]{0:T(1024)S(1)} %reshape.56), channel_id=1, source_target_pairs={{0,3},{1,0},{2,1},{3,2},{4,7},{5,4},{6,5},{7,6},{8,11},{9,8},{10,9... | collective-permute-start | bytes 9224 | tf_op jit(solution)/shard_map/ppermute | solution.py:348
  188.2 5.1 %collective-permute-start.14 = (f32[768]{0:T(1024)S(1)}, f32[768]{0:T(1024)S(1)}, u32[]{:S(2)}, u32[]{:S(2)}) collective-permute-start(f32[768]{0:T(1024)S(1)} %reshape.56), channel_id=1, source_target_pairs={{0,2},{1,3},{2,0},{3,1},{4,6},{5,7},{6,4},{7,5},{8,10},{9,11},{10,... | collective-permute-start | bytes 9224 | tf_op jit(solution)/shard_map/ppermute | solution.py:348
Sparse Core Ops, SparseCore 0:
  10.2 65.5 all-gather.1

commit v7 on v6

--- a/solution.py
+++ b/solution.py
@@ -12,7 +12,7 @@
 LOSS_SCALE = 32.0
 NEG = -1e30
 BLOCK = 4
-UNROLL = 16
+UNROLL = 32
 CHUNKS = 2
 LANES = 128
 STRIDE = 256

time: 218 us -> 218 us (level)
  transfers between devices with their start and end apart: 18 -> 18, of which waited for: 9 -> 10; matrix products, arithmetic and copies ran while one was open for 2% -> 2% of each run, Pallas kernels for 14% -> 15%
where the time goes in v7:
time: 218 us
  waiting for transfers between devices  89.8 us (41%)
  Pallas kernels  43.6 us (20%)
  starting transfers between devices  40.1 us (18%)
  local copies, waits for them, and re-layouts  14.9 us (7%)
  between operations  14.3 us (7%)
  blocking collectives  12.5 us (6%)
  other arithmetic  2.33 us (1%)
    all_gather x1, waiting for transfers between devices, per_device(): everyone = lax.all_gather(queries, 'index', tiled=True)  30.1 us
    ppermute x15, waiting for transfers between devices, travel(): return lax.ppermute(x, 'rep', rep_pairs(step))  27 us
    all_to_all x1, waiting for transfers between devices, per_device(): lax.all_to_all(outgoing.reshape(groups, span, feature), 'index', split_ax...  25.3 us
    ppermute x15, starting transfers between devices, travel(): return lax.ppermute(x, 'rep', rep_pairs(step))  24.7 us
    pallas_call x2, Pallas kernels, per_device(): pl.pallas_call(functools.partial(pair_kernel, chunk, blocks, scale), out_...  15.1 us
    all_gather x1, blocking collectives, per_device(): lax.all_gather(quarter.reshape(query_count, share, feature), 'rep')  12.5 us
    pallas_call x1, Pallas kernels, per_device(): pl.pallas_call(functools.partial(sort_kernel, capacity, page_bits, query_...  12.3 us
    all_to_all x1, starting transfers between devices, per_device(): lax.all_to_all(table.reshape(groups, capacity), 'index', split_axis=0, co...  8.42 us
  transfers between devices with their start and end apart: 18, of which 10 were waited for; matrix products, arithmetic and copies ran while one was open for 2% of the time, Pallas kernels for 15%

profile of v7, /device:TPU:0, one launch (start us, length us, event | category | flops | bytes accessed | tf_op | source)
XLA Modules:
  0.0 217.6 jit_solution(3796059122770148224)
XLA Ops:
  7.2 0.7 all-gather.2.cloned.1.call-update
  7.9 0.8 copy.14
  8.7 0.7 reshape.51.listed
  9.3 5.1 %route.1 = (s32[768]{0:T(1024)}, s32[384]{0:T(512)}, s32[384]{0:T(512)}) custom-call(s32[384]{0:T(512)} %reshape.51.listed, s32[2048]{0:T(1024)} %page_slot.1), custom_call_target="tpu_custom_call" | custom-call | tf_op jit(solution)/shard_map/route/pallas_call | solution.py:316
  14.5 1.4 all_to_all.9
  15.8 8.4 %all-to-all-start = ((s32[32,1,24]{2,1,0:T(1,128)}), s32[32,1,24]{2,1,0:T(1,128)S(1)}, u32[]{:S(2)}, u32[]{:S(2)}) async-start(s32[32,1,24]{2,1,0:T(1,128)} %bitcast), calls=%async_computation | async-start | bytes 32768 | tf_op jit(solution)/shard_map/all_to_all | solution.py:324
  24.3 0.7 broadcast_subtract_fusion.limits
  24.9 6.6 %all-to-all-done = s32[32,1,24]{2,1,0:T(1,128)S(1)} async-done(((s32[32,1,24]{2,1,0:T(1,128)}), s32[32,1,24]{2,1,0:T(1,128)S(1)}, u32[]{:S(2)}, u32[]{:S(2)}) %all-to-all-start) | async-done | bytes 3104 | tf_op jit(solution)/shard_map/all_to_all | solution.py:324
  31.6 0.5 broadcast.22
  32.1 0.7 reduce.5
  32.8 0.7 reshape.52.arrived
  33.5 12.3 %sort_pairs.1.order = s32[2376]{0:T(1024)} custom-call(s32[768]{0:T(1024)} %reshape.52.arrived), custom_call_target="tpu_custom_call" | custom-call | bytes 40000000 | tf_op jit(solution)/shard_map/sort_pairs/pallas_call | solution.py:328
  45.8 30.1 %all-gather.2.cloned.1.call-done.refs_1_ = bf16[1536,32,128]{2,1,0:T(8,128)(2,1)} async-done(((bf16[48,32,128]{2,1,0:T(8,128)(2,1)}), bf16[1536,32,128]{2,1,0:T(8,128)(2,1)}) %all-gather.2.cloned.1.call-update) | async-done | bytes 12582928 | tf_op jit(solution)/shard_map/all_gather | solution.py:326
  75.9 4.6 %copy-done = bf16[1536,32,128]{2,1,0:T(8,128)(2,1)S(1)} copy-done((bf16[1536,32,128]{2,1,0:T(8,128)(2,1)S(1)}, bf16[1536,32,128]{2,1,0:T(8,128)(2,1)}, u32[]{:S(2)}) %copy-start) | copy-done | bytes 12582936
  80.4 2.2 %copy-done.1 = bf16[64,256,128]{2,1,0:T(8,128)(2,1)S(1)} copy-done((bf16[64,256,128]{2,1,0:T(8,128)(2,1)S(1)}, bf16[64,256,128]{2,1,0:T(8,128)(2,1)}, u32[]{:S(2)}) %copy-start.1) | copy-done | bytes 4194328
  82.6 0.7 copy-done.2
  83.3 7.6 %pairs.3 = (bf16[1632,128]{1,0:T(8,128)(2,1)S(1)}, bf16[1632,128]{1,0:T(8,128)(2,1)S(1)}, bf16[1632,128]{1,0:T(8,128)(2,1)S(1)}, bf16[1632,128]{1,0:T(8,128)(2,1...) custom-call(s32[2376]{0:T(1024)S(1)} %copy-done.2, ...), custom_call_target="tpu_custom_call" | custom-call | bytes 60000000 | tf_op jit(solution)/shard_map/pairs/pallas_call | solution.py:352
  90.9 1.5 collective-permute-start.6
  92.4 1.8 collective-permute-start.7
  94.2 7.6 %pairs.2 = (bf16[1632,128]{1,0:T(8,128)(2,1)S(1)}, bf16[1632,128]{1,0:T(8,128)(2,1)S(1)}, bf16[1632,128]{1,0:T(8,128)(2,1)S(1)}, bf16[1632,128]{1,0:T(8,128)(2,1...) custom-call(s32[2376]{0:T(1024)S(1)} %copy-done.2, ...), custom_call_target="tpu_custom_call" | custom-call | bytes 60000000 | tf_op jit(solution)/shard_map/pairs/pallas_call | solution.py:352
  101.8 0.3 collective-permute-start
  102.1 3.0 %collective-permute-start.1 = (bf16[1632,128]{1,0:T(8,128)(2,1)S(1)}, bf16[1632,128]{1,0:T(8,128)(2,1)S(1)}, u32[]{:S(2)}, u32[]{:S(2)}) collective-permute-start(bf16[1632,128]{1,0:T(8,128)(2,1)S(1)} %get-tuple-element.34), channel_id=1, source_target_pairs={{0,3},{1,0},{2,1},{3,2},{4,7},{5,4},{6,5},{7,6},{8,11},{9,8},{10,9... | collective-permute-start | bytes 1253384 | tf_op jit(solution)/shard_map/ppermute | solution.py:348
  105.1 1.4 merge.6
  106.5 1.4 collective-permute-start.8
  107.9 1.9 collective-permute-start.9
  109.8 5.9 %collective-permute-done.refs_0_ = bf16[1632,128]{1,0:T(8,128)(2,1)S(1)} collective-permute-done((bf16[1632,128]{1,0:T(8,128)(2,1)S(1)}, bf16[1632,128]{1,0:T(8,128)(2,1)S(1)}, u32[]{:S(2)}, u32[]{:S(2)}) %collective-permute-start) | collective-permute-done | bytes 417824 | tf_op jit(solution)/shard_map/ppermute | solution.py:348
  115.6 1.4 merge.4
  117.0 0.6 collective-permute-start.2
  117.6 3.0 %collective-permute-start.3 = (bf16[1632,128]{1,0:T(8,128)(2,1)S(1)}, bf16[1632,128]{1,0:T(8,128)(2,1)S(1)}, u32[]{:S(2)}, u32[]{:S(2)}) collective-permute-start(bf16[1632,128]{1,0:T(8,128)(2,1)S(1)} %get-tuple-element.38), channel_id=1, source_target_pairs={{0,3},{1,0},{2,1},{3,2},{4,7},{5,4},{6,5},{7,6},{8,11},{9,8},{10,9... | collective-permute-start | bytes 1253384 | tf_op jit(solution)/shard_map/ppermute | solution.py:348
  120.6 4.0 %collective-permute-done.8.refs_0_ = bf16[1632,128]{1,0:T(8,128)(2,1)S(1)} collective-permute-done((bf16[1632,128]{1,0:T(8,128)(2,1)S(1)}, bf16[1632,128]{1,0:T(8,128)(2,1)S(1)}, u32[]{:S(2)}, u32[]{:S(2)}) %collective-permute-start.8) | collective-permute-done | bytes 417824 | tf_op jit(solution)/shard_map/ppermute | solution.py:348
  124.6 1.4 merge.7
  126.0 0.6 collective-permute-start.10
  126.5 2.8 %collective-permute-start.11 = (bf16[1632,128]{1,0:T(8,128)(2,1)S(1)}, bf16[1632,128]{1,0:T(8,128)(2,1)S(1)}, u32[]{:S(2)}, u32[]{:S(2)}) collective-permute-start(bf16[1632,128]{1,0:T(8,128)(2,1)S(1)} %get-tuple-element.54), channel_id=1, source_target_pairs={{0,3},{1,0},{2,1},{3,2},{4,7},{5,4},{6,5},{7,6},{8,11},{9,8},{10,9... | collective-permute-start | bytes 1253384 | tf_op jit(solution)/shard_map/ppermute | solution.py:348
  129.3 4.2 %collective-permute-done.2.refs_0_ = bf16[1632,128]{1,0:T(8,128)(2,1)S(1)} collective-permute-done((bf16[1632,128]{1,0:T(8,128)(2,1)S(1)}, bf16[1632,128]{1,0:T(8,128)(2,1)S(1)}, u32[]{:S(2)}, u32[]{:S(2)}) %collective-permute-start.2) | collective-permute-done | bytes 417824 | tf_op jit(solution)/shard_map/ppermute | solution.py:348
  133.5 1.4 merge.5
  134.9 0.6 collective-permute-start.4
  135.5 2.8 %collective-permute-start.5 = (bf16[1632,128]{1,0:T(8,128)(2,1)S(1)}, bf16[1632,128]{1,0:T(8,128)(2,1)S(1)}, u32[]{:S(2)}, u32[]{:S(2)}) collective-permute-start(bf16[1632,128]{1,0:T(8,128)(2,1)S(1)} %get-tuple-element.42), channel_id=1, source_target_pairs={{0,3},{1,0},{2,1},{3,2},{4,7},{5,4},{6,5},{7,6},{8,11},{9,8},{10,9... | collective-permute-start | bytes 1253384 | tf_op jit(solution)/shard_map/ppermute | solution.py:348
  138.3 4.2 %collective-permute-done.10.refs_0_ = bf16[1632,128]{1,0:T(8,128)(2,1)S(1)} collective-permute-done((bf16[1632,128]{1,0:T(8,128)(2,1)S(1)}, bf16[1632,128]{1,0:T(8,128)(2,1)S(1)}, u32[]{:S(2)}, u32[]{:S(2)}) %collective-permute-start.10) | collective-permute-done | bytes 417824 | tf_op jit(solution)/shard_map/ppermute | solution.py:348
  142.5 1.4 merge_first.1
  143.9 4.9 %collective-permute-done.4.refs_0_ = bf16[1632,128]{1,0:T(8,128)(2,1)S(1)} collective-permute-done((bf16[1632,128]{1,0:T(8,128)(2,1)S(1)}, bf16[1632,128]{1,0:T(8,128)(2,1)S(1)}, u32[]{:S(2)}, u32[]{:S(2)}) %collective-permute-start.4) | collective-permute-done | bytes 417824 | tf_op jit(solution)/shard_map/ppermute | solution.py:348
  148.8 2.6 %merge_last.1 = bf16[6656,128]{1,0:T(8,128)(2,1)} custom-call(bf16[1632,128]{1,0:T(8,128)(2,1)S(1)} %collective-permute-done.4.refs_0_, bf16[1632,128]{1,0:T(8,128)(2,1)S(1)} %get-tuple-element.41.refs_1_, bf16[1632,128]{1,0:T(8,128)(2,1)S(1)} %collective-permute-done.5.refs_2_, bf16[1632,128]{1,0:T(8,128)(2,1)S(1)} %get-tuple-element.43.refs_3_, ...), custom_call_target="tpu_custom_call" | custom-call | tf_op jit(solution)/shard_map/merge_last/pallas_call | solution.py:393
  151.4 7.0 %all-to-all-start.1 = ((bf16[32,208,128]{2,1,0:T(8,128)(2,1)}), bf16[32,208,128]{2,1,0:T(8,128)(2,1)S(1)}, u32[]{:S(2)}, u32[]{:S(2)}) async-start(bf16[32,208,128]{2,1,0:T(8,128)(2,1)} %bitcast.2), calls=%async_computation.1 | async-start | bytes 3407872 | tf_op jit(solution)/shard_map/all_to_all | solution.py:401
  158.4 25.3 %all-to-all-done.1 = bf16[32,208,128]{2,1,0:T(8,128)(2,1)S(1)} async-done(((bf16[32,208,128]{2,1,0:T(8,128)(2,1)}), bf16[32,208,128]{2,1,0:T(8,128)(2,1)S(1)}, u32[]{:S(2)}, u32[]{:S(2)}) %all-to-all-start.1) | async-done | bytes 1703968 | tf_op jit(solution)/shard_map/all_to_all | solution.py:401
  183.8 0.1 reshape.61
  183.9 0.1 reduce_sum.18
  184.0 0.1 constant_dynamic-slice_fusion
  184.1 0.1 reshape.56
  184.2 0.3 collective-permute-start.12
  184.5 3.0 %collective-permute-start.13 = (f32[768]{0:T(1024)S(1)}, f32[768]{0:T(1024)S(1)}, u32[]{:S(2)}, u32[]{:S(2)}) collective-permute-start(f32[768]{0:T(1024)S(1)} %reshape.56), channel_id=1, source_target_pairs={{0,3},{1,0},{2,1},{3,2},{4,7},{5,4},{6,5},{7,6},{8,11},{9,8},{10,9... | collective-permute-start | bytes 9224 | tf_op jit(solution)/shard_map/ppermute | solution.py:348
  187.5 1.2 collective-permute-start.14
  188.7 0.1 sub.48
  188.8 0.3 collective-permute-done.12
  189.1 3.5 %collective-permute-done.14 = f32[768]{0:T(1024)S(1)} collective-permute-done((f32[768]{0:T(1024)S(1)}, f32[768]{0:T(1024)S(1)}, u32[]{:S(2)}, u32[]{:S(2)}) %collective-permute-start.14) | collective-permute-done | bytes 3104 | tf_op jit(solution)/shard_map/ppermute | solution.py:348
  192.7 1.9 gather_fusion
  194.5 0.1 reshape.57
  194.6 0.1 slice_reduce_fusion
  194.7 0.1 reduce_max.9
  194.9 0.2 exponential_reduce_fusion
  195.1 0.5 fusion
  195.6 0.1 sub.44
  195.7 0.1 sub.45
  195.8 1.7 gradients.1
  197.5 12.5 %all_gather.7 = bf16[4,48,8,128]{3,2,1,0:T(8,128)(2,1)S(1)} all-gather(bf16[1,48,8,128]{3,2,1,0:T(8,128)(2,1)S(1)} %bitcast.11), channel_id=1, replica_groups=mesh['index'=32,'rep'=4] {'rep'}, dimensions={0}, use_global_device_ids=true | all-gather | bytes 491520 | tf_op jit(solution)/shard_map/all_gather | solution.py:424
  210.0 0.8 copy.18
  (23 shorter events, 0.1 us)
Async XLA Ops:
  7.2 68.7 %all-gather.2.cloned.1.call-start = ((), (), s32[]{:S(2)}) async-start(), calls=%async_computation.2 | async-start | bytes 12976128 | tf_op jit(solution)/shard_map/all_gather | solution.py:326
  15.8 15.7 %all-to-all-start = ((s32[32,1,24]{2,1,0:T(1,128)}), s32[32,1,24]{2,1,0:T(1,128)S(1)}, u32[]{:S(2)}, u32[]{:S(2)}) async-start(s32[32,1,24]{2,1,0:T(1,128)} %bitcast), calls=%async_computation | async-start | bytes 32768 | tf_op jit(solution)/shard_map/all_to_all | solution.py:324
  75.9 4.6 %copy-start = (bf16[1536,32,128]{2,1,0:T(8,128)(2,1)S(1)}, bf16[1536,32,128]{2,1,0:T(8,128)(2,1)}, u32[]{:S(2)}) copy-start(bf16[1536,32,128]{2,1,0:T(8,128)(2,1)} %all-gather.2.cloned.1.call-done.refs_1_) | copy-start | bytes 37748740
  80.4 2.2 %copy-start.1 = (bf16[64,256,128]{2,1,0:T(8,128)(2,1)S(1)}, bf16[64,256,128]{2,1,0:T(8,128)(2,1)}, u32[]{:S(2)}) copy-start(bf16[64,256,128]{2,1,0:T(8,128)(2,1)} %refs_0_.3) | copy-start | bytes 12582916
  82.6 0.7 copy-start.2
  90.9 14.2 %collective-permute-start.6 = (bf16[1632,128]{1,0:T(8,128)(2,1)S(1)}, bf16[1632,128]{1,0:T(8,128)(2,1)S(1)}, u32[]{:S(2)}, u32[]{:S(2)}) collective-permute-start(bf16[1632,128]{1,0:T(8,128)(2,1)S(1)} %get-tuple-element.44), channel_id=1, source_target_pairs={{0,1},{1,2},{2,3},{3,0},{4,5},{5,6},{6,7},{7,4},{8,9},{9,10},{10,1... | collective-permute-start | bytes 1253384 | tf_op jit(solution)/shard_map/ppermute | solution.py:348
  92.4 12.6 %collective-permute-start.7 = (bf16[1632,128]{1,0:T(8,128)(2,1)S(1)}, bf16[1632,128]{1,0:T(8,128)(2,1)S(1)}, u32[]{:S(2)}, u32[]{:S(2)}) collective-permute-start(bf16[1632,128]{1,0:T(8,128)(2,1)S(1)} %get-tuple-element.46), channel_id=1, source_target_pairs={{0,3},{1,0},{2,1},{3,2},{4,7},{5,4},{6,5},{7,6},{8,11},{9,8},{10,9... | collective-permute-start | bytes 1253384 | tf_op jit(solution)/shard_map/ppermute | solution.py:348
  101.8 13.9 %collective-permute-start = (bf16[1632,128]{1,0:T(8,128)(2,1)S(1)}, bf16[1632,128]{1,0:T(8,128)(2,1)S(1)}, u32[]{:S(2)}, u32[]{:S(2)}) collective-permute-start(bf16[1632,128]{1,0:T(8,128)(2,1)S(1)} %get-tuple-element.32), channel_id=1, source_target_pairs={{0,1},{1,2},{2,3},{3,0},{4,5},{5,6},{6,7},{7,4},{8,9},{9,10},{10,1... | collective-permute-start | bytes 1253384 | tf_op jit(solution)/shard_map/ppermute | solution.py:348
  102.1 13.5 %collective-permute-start.1 = (bf16[1632,128]{1,0:T(8,128)(2,1)S(1)}, bf16[1632,128]{1,0:T(8,128)(2,1)S(1)}, u32[]{:S(2)}, u32[]{:S(2)}) collective-permute-start(bf16[1632,128]{1,0:T(8,128)(2,1)S(1)} %get-tuple-element.34), channel_id=1, source_target_pairs={{0,3},{1,0},{2,1},{3,2},{4,7},{5,4},{6,5},{7,6},{8,11},{9,8},{10,9... | collective-permute-start | bytes 1253384 | tf_op jit(solution)/shard_map/ppermute | solution.py:348
  106.5 18.1 %collective-permute-start.8 = (bf16[1632,128]{1,0:T(8,128)(2,1)S(1)}, bf16[1632,128]{1,0:T(8,128)(2,1)S(1)}, u32[]{:S(2)}, u32[]{:S(2)}) collective-permute-start(bf16[1632,128]{1,0:T(8,128)(2,1)S(1)} %get-tuple-element.48), channel_id=1, source_target_pairs={{0,1},{1,2},{2,3},{3,0},{4,5},{5,6},{6,7},{7,4},{8,9},{9,10},{10,1... | collective-permute-start | bytes 1253384 | tf_op jit(solution)/shard_map/ppermute | solution.py:348
  107.9 16.7 %collective-permute-start.9 = (bf16[1632,128]{1,0:T(8,128)(2,1)S(1)}, bf16[1632,128]{1,0:T(8,128)(2,1)S(1)}, u32[]{:S(2)}, u32[]{:S(2)}) collective-permute-start(bf16[1632,128]{1,0:T(8,128)(2,1)S(1)} %get-tuple-element.50), channel_id=1, source_target_pairs={{0,3},{1,0},{2,1},{3,2},{4,7},{5,4},{6,5},{7,6},{8,11},{9,8},{10,9... | collective-permute-start | bytes 1253384 | tf_op jit(solution)/shard_map/ppermute | solution.py:348
  117.0 16.5 %collective-permute-start.2 = (bf16[1632,128]{1,0:T(8,128)(2,1)S(1)}, bf16[1632,128]{1,0:T(8,128)(2,1)S(1)}, u32[]{:S(2)}, u32[]{:S(2)}) collective-permute-start(bf16[1632,128]{1,0:T(8,128)(2,1)S(1)} %get-tuple-element.36), channel_id=1, source_target_pairs={{0,1},{1,2},{2,3},{3,0},{4,5},{5,6},{6,7},{7,4},{8,9},{9,10},{10,1... | collective-permute-start | bytes 1253384 | tf_op jit(solution)/shard_map/ppermute | solution.py:348
  117.6 16.0 %collective-permute-start.3 = (bf16[1632,128]{1,0:T(8,128)(2,1)S(1)}, bf16[1632,128]{1,0:T(8,128)(2,1)S(1)}, u32[]{:S(2)}, u32[]{:S(2)}) collective-permute-start(bf16[1632,128]{1,0:T(8,128)(2,1)S(1)} %get-tuple-element.38), channel_id=1, source_target_pairs={{0,3},{1,0},{2,1},{3,2},{4,7},{5,4},{6,5},{7,6},{8,11},{9,8},{10,9... | collective-permute-start | bytes 1253384 | tf_op jit(solution)/shard_map/ppermute | solution.py:348
  126.0 16.5 %collective-permute-start.10 = (bf16[1632,128]{1,0:T(8,128)(2,1)S(1)}, bf16[1632,128]{1,0:T(8,128)(2,1)S(1)}, u32[]{:S(2)}, u32[]{:S(2)}) collective-permute-start(bf16[1632,128]{1,0:T(8,128)(2,1)S(1)} %get-tuple-element.52), channel_id=1, source_target_pairs={{0,1},{1,2},{2,3},{3,0},{4,5},{5,6},{6,7},{7,4},{8,9},{9,10},{10,1... | collective-permute-start | bytes 1253384 | tf_op jit(solution)/shard_map/ppermute | solution.py:348
  126.5 16.0 %collective-permute-start.11 = (bf16[1632,128]{1,0:T(8,128)(2,1)S(1)}, bf16[1632,128]{1,0:T(8,128)(2,1)S(1)}, u32[]{:S(2)}, u32[]{:S(2)}) collective-permute-start(bf16[1632,128]{1,0:T(8,128)(2,1)S(1)} %get-tuple-element.54), channel_id=1, source_target_pairs={{0,3},{1,0},{2,1},{3,2},{4,7},{5,4},{6,5},{7,6},{8,11},{9,8},{10,9... | collective-permute-start | bytes 1253384 | tf_op jit(solution)/shard_map/ppermute | solution.py:348
  134.9 13.9 %collective-permute-start.4 = (bf16[1632,128]{1,0:T(8,128)(2,1)S(1)}, bf16[1632,128]{1,0:T(8,128)(2,1)S(1)}, u32[]{:S(2)}, u32[]{:S(2)}) collective-permute-start(bf16[1632,128]{1,0:T(8,128)(2,1)S(1)} %get-tuple-element.40), channel_id=1, source_target_pairs={{0,1},{1,2},{2,3},{3,0},{4,5},{5,6},{6,7},{7,4},{8,9},{9,10},{10,1... | collective-permute-start | bytes 1253384 | tf_op jit(solution)/shard_map/ppermute | solution.py:348
  135.5 13.3 %collective-permute-start.5 = (bf16[1632,128]{1,0:T(8,128)(2,1)S(1)}, bf16[1632,128]{1,0:T(8,128)(2,1)S(1)}, u32[]{:S(2)}, u32[]{:S(2)}) collective-permute-start(bf16[1632,128]{1,0:T(8,128)(2,1)S(1)} %get-tuple-element.42), channel_id=1, source_target_pairs={{0,3},{1,0},{2,1},{3,2},{4,7},{5,4},{6,5},{7,6},{8,11},{9,8},{10,9... | collective-permute-start | bytes 1253384 | tf_op jit(solution)/shard_map/ppermute | solution.py:348
  151.4 7.0 %copy-start.4 = (s32[384]{0:T(512)S(1)}, s32[384]{0:T(512)}, u32[]{:S(2)}) copy-start(s32[384]{0:T(512)} %get-tuple-element.58) | copy-start | bytes 4612
  151.4 32.4 %all-to-all-start.1 = ((bf16[32,208,128]{2,1,0:T(8,128)(2,1)}), bf16[32,208,128]{2,1,0:T(8,128)(2,1)S(1)}, u32[]{:S(2)}, u32[]{:S(2)}) async-start(bf16[32,208,128]{2,1,0:T(8,128)(2,1)} %bitcast.2), calls=%async_computation.1 | async-start | bytes 3407872 | tf_op jit(solution)/shard_map/all_to_all | solution.py:401
  158.4 37.4 %copy-start.3 = (s32[384]{0:T(512)S(1)}, s32[384]{0:T(512)}, u32[]{:S(2)}) copy-start(s32[384]{0:T(512)} %get-tuple-element.59.place) | copy-start | bytes 4612
  184.2 4.9 %collective-permute-start.12 = (f32[768]{0:T(1024)S(1)}, f32[768]{0:T(1024)S(1)}, u32[]{:S(2)}, u32[]{:S(2)}) collective-permute-start(f32[768]{0:T(1024)S(1)} %reshape.56), channel_id=1, source_target_pairs={{0,1},{1,2},{2,3},{3,0},{4,5},{5,6},{6,7},{7,4},{8,9},{9,10},{10,1... | collective-permute-start | bytes 9224 | tf_op jit(solution)/shard_map/ppermute | solution.py:348
  184.5 4.6 %collective-permute-start.13 = (f32[768]{0:T(1024)S(1)}, f32[768]{0:T(1024)S(1)}, u32[]{:S(2)}, u32[]{:S(2)}) collective-permute-start(f32[768]{0:T(1024)S(1)} %reshape.56), channel_id=1, source_target_pairs={{0,3},{1,0},{2,1},{3,2},{4,7},{5,4},{6,5},{7,6},{8,11},{9,8},{10,9... | collective-permute-start | bytes 9224 | tf_op jit(solution)/shard_map/ppermute | solution.py:348
  187.5 5.1 %collective-permute-start.14 = (f32[768]{0:T(1024)S(1)}, f32[768]{0:T(1024)S(1)}, u32[]{:S(2)}, u32[]{:S(2)}) collective-permute-start(f32[768]{0:T(1024)S(1)} %reshape.56), channel_id=1, source_target_pairs={{0,2},{1,3},{2,0},{3,1},{4,6},{5,7},{6,4},{7,5},{8,10},{9,11},{10,... | collective-permute-start | bytes 9224 | tf_op jit(solution)/shard_map/ppermute | solution.py:348
Sparse Core Ops, SparseCore 0:
  10.2 65.5 all-gather.1
